TPU v7x, 32 devices: a whole 2x2x4 slice. The times are simulated.
32 devices in a mesh: sec: 4 (over z), row: 2 (over y), col: 4 (over x, core).
Axes of the slice: x: 2, y: 2, z: 4, core: 2. Of those that a mesh axis runs over, the one named last changes fastest.
Arguments:
- labels: int32 [8, 128, 512], P('col', 'row', 'sec'), may hold values 0 or 1
- jitter: float32 [2, 8, 128, 512], P(None, 'col', 'row', 'sec'), may hold values from 0.5 to 1.5
- shells: int32 [128, 512], P('row', 'sec'), may hold values from 0 to 255, as said below
Outputs:
- populations: float32 [38, 8, 128, 512], P(None, 'col', 'row', 'sec')
- spectrum: float32 [8, 256], P('col')
Inputs may be any that keep to these rules, and one draw needn't show every extreme that they name: shells are radial bins of |k|: with kx' = kx for kx < 64, else kx - 128 (ky' likewise with 512), shells[kx, ky] = min(floor(sqrt(kx'^2 + ky'^2 + j)), 255), where j is 0 or 1 per wavevector (0 at k = 0); every label from 0 to 255 belongs to at least one wavevector.
All inputs are finite; a program needn't handle non-finite values. No bound on the sum of `labels` on one device may be relied on, other than what follows from the above.
Results may differ from a plain program's by a relative error of at most 0.002.
Values may be sent and summed in bfloat16 or wider, within the bound.
No kernel may reach another device: no remote copies, remote signals or barrier semaphores. Data moves between devices by JAX's collectives and lax.ppermute only.
A program may use at most 64 MiB of HBM per device.

v0:
```python
import math

import jax
import jax.numpy as jnp
from jax import lax
from jax.sharding import PartitionSpec as P

NSHELL = 256


LATTICE = (
    (0, 0, 0),
    (1, 0, 0),
    (-1, 0, 0),
    (0, 1, 0),
    (0, -1, 0),
    (0, 0, 1),
    (0, 0, -1),
    (1, 1, 0),
    (-1, -1, 0),
    (1, -1, 0),
    (-1, 1, 0),
    (1, 0, 1),
    (-1, 0, -1),
    (1, 0, -1),
    (-1, 0, 1),
    (0, 1, 1),
    (0, -1, -1),
    (0, 1, -1),
    (0, -1, 1),
)
WEIGHTS = (1.0 / 3.0,) + (1.0 / 18.0,) * 6 + (1.0 / 36.0,) * 12


def with_halo(block, sides, width):
    for axis, dim in sides:
        count = lax.axis_size(axis)
        forward = [(i, i + 1) for i in range(count - 1)]
        forward.append((count - 1, 0))
        backward = [(target, source) for source, target in forward]
        low = lax.ppermute(
            lax.slice_in_dim(block, block.shape[dim] - width, None, axis=dim), axis, forward
        )
        high = lax.ppermute(lax.slice_in_dim(block, 0, width, axis=dim), axis, backward)
        block = jnp.concatenate([low, block, high], axis=dim)
    return block


def density_pair(labels, jitter):
    heavy_a = jnp.where(labels == 1, jnp.float32(1.0), jnp.float32(0.2))
    heavy_b = jnp.where(labels == 1, jnp.float32(0.2), jnp.float32(1.0))
    return jnp.stack([heavy_a * jitter[0], heavy_b * jitter[1]])


def pull_sums(padded):
    inner_z = padded.shape[1] - 2
    inner_x = padded.shape[2] - 2
    inner_y = padded.shape[3] - 2
    zeros_field = jnp.zeros((2, inner_z, inner_x, inner_y), jnp.float32)
    totals_axis = [zeros_field, zeros_field, zeros_field]
    for offsets, weight in zip(LATTICE[1:], WEIGHTS[1:]):
        shifted = padded[
            :,
            1 + offsets[2] : 1 + offsets[2] + inner_z,
            1 + offsets[0] : 1 + offsets[0] + inner_x,
            1 + offsets[1] : 1 + offsets[1] + inner_y,
        ]
        for axis_id in range(3):
            if offsets[axis_id] != 0:
                totals_axis[axis_id] = totals_axis[axis_id] + weight * offsets[axis_id] * shifted
    return jnp.stack(totals_axis, axis=1)


def relax_stack(densities, pull_terms):
    velocities = (-1.6 * pull_terms[1], -1.6 * pull_terms[0])
    term_list = []
    for component in range(2):
        velocity = velocities[component]
        density = densities[component]
        squared = velocity[0] * velocity[0] + velocity[1] * velocity[1] + velocity[2] * velocity[2]
        for offsets, weight in zip(LATTICE, WEIGHTS):
            projected = (
                offsets[0] * velocity[0] + offsets[1] * velocity[1] + offsets[2] * velocity[2]
            )
            term_list.append(
                weight
                * density
                * (1.0 + 1.25 * (3.0 * projected + 4.5 * projected * projected - 1.5 * squared))
            )
    return jnp.stack(term_list)


def stream_pull(relaxed, depth_z, width_x, width_y):
    moved_list = []
    for number in range(38):
        offsets = LATTICE[number % 19]
        moved_list.append(
            relaxed[
                number,
                1 - offsets[2] : 1 - offsets[2] + depth_z,
                1 - offsets[0] : 1 - offsets[0] + width_x,
                1 - offsets[1] : 1 - offsets[1] + width_y,
            ]
        )
    return jnp.stack(moved_list)


def x_part(portion, first_kx, width_x, full_x):
    count_x = portion.shape[1]
    freq_x = first_kx + jnp.arange(width_x, dtype=jnp.int32)[:, None]
    pos_x = jnp.arange(count_x, dtype=jnp.int32)[None, :]
    angles = (freq_x * pos_x % full_x).astype(jnp.float32) * (2.0 * math.pi / full_x)
    table = jnp.concatenate(
        [jnp.cos(angles).astype(jnp.bfloat16), (-jnp.sin(angles)).astype(jnp.bfloat16)], 0
    )
    return jnp.einsum("kx,zxy->zky", table, portion, preferred_element_type=jnp.float32)


def y_part(portion, first_ky, width_x, width_y, full_y):
    count_y = portion.shape[2]
    pos_y = jnp.arange(count_y, dtype=jnp.int32)[:, None]
    freq_y = first_ky + jnp.arange(width_y, dtype=jnp.int32)[None, :]
    angles = (pos_y * freq_y % full_y).astype(jnp.float32) * (2.0 * math.pi / full_y)
    cos_y = jnp.cos(angles).astype(jnp.bfloat16)
    sin_y = jnp.sin(angles).astype(jnp.bfloat16)
    right_side = jnp.concatenate(
        [jnp.concatenate([cos_y, -sin_y], 1), jnp.concatenate([sin_y, cos_y], 1)], 0
    )
    left_side = jnp.concatenate([portion[:, :width_x], portion[:, width_x:]], axis=2)
    return jnp.einsum("zkv,vw->zkw", left_side, right_side, preferred_element_type=jnp.float32)


def on_device(labels, jitter, shells):
    depth_z, width_x, width_y = labels.shape
    densities = density_pair(labels, jitter)
    padded = with_halo(densities, (("sec", 3), ("row", 2), ("col", 1)), 2)
    pull_terms = pull_sums(padded)
    relaxed = relax_stack(padded[:, 1:-1, 1:-1, 1:-1], pull_terms)
    populations = stream_pull(relaxed, depth_z, width_x, width_y)
    order_b = (densities[0] - densities[1]).astype(jnp.bfloat16)
    full_x = width_x * lax.axis_size("row")
    full_y = width_y * lax.axis_size("sec")
    first_kx = lax.axis_index("row") * width_x
    first_ky = lax.axis_index("sec") * width_y
    rows_all = lax.all_gather(order_b, "row", axis=1, tiled=True)
    whole_plane = lax.all_gather(rows_all, "sec", axis=2, tiled=True)
    half_step = x_part(whole_plane, first_kx, width_x, full_x).astype(jnp.bfloat16)
    transform = y_part(half_step, first_ky, width_x, width_y, full_y)
    real_part = transform[..., :width_y]
    imag_part = transform[..., width_y:]
    power_map = real_part * real_part + imag_part * imag_part
    cell_count = width_x * width_y
    flat_shells = shells.reshape(cell_count)
    totals = jax.ops.segment_sum(
        power_map.reshape(depth_z, cell_count).T, flat_shells, num_segments=NSHELL
    )
    counts = jax.ops.segment_sum(
        jnp.ones((cell_count,), jnp.float32), flat_shells, num_segments=NSHELL
    )
    totals, counts = lax.psum((totals, counts), ("sec", "row"))
    spectrum = (totals / (counts[:, None] * float(full_x * full_y))).T
    return (populations, spectrum)


def solution(mesh):
    in_specs = (P("col", "row", "sec"), P(None, "col", "row", "sec"), P("row", "sec"))
    out_specs = (P(None, "col", "row", "sec"), P("col", None))
    return jax.shard_map(
        on_device, mesh=mesh, in_specs=in_specs, out_specs=out_specs, check_vma=False
    )
```

profile of v0, /device:TPU:0, one launch (start us, length us, event | category | flops | bytes accessed | tf_op | source)
XLA Modules:
  0.0 194.9 jit_solution(5162693363096428347)
XLA Ops:
  0.6 0.9 subtract_convert_fusion
  1.6 0.9 fusion.129
  2.6 3.1 %collective-permute-start = (f32[2,2,64,2]{3,2,1,0:T(8,128)S(1)}, f32[2,2,64,2]{3,2,1,0:T(8,128)S(1)}, u32[]{:S(2)}, u32[]{:S(2)}) collective-permute-start(f32[2,2,64,2]{3,2,1,0:T(8,128)S(1)} %get-tuple-element.162), channel_id=1, source_target_pairs={{0,8},{8,16},{16,24},{24,0},{1,9},{9,17},{17,25},{25,1},{2,10},{10... | collective-permute-start | bytes 6152 | tf_op jit(solution)/shard_map/ppermute | solution.py:41
  5.6 2.1 %collective-permute-start.1 = (f32[2,2,64,2]{3,2,1,0:T(8,128)S(1)}, f32[2,2,64,2]{3,2,1,0:T(8,128)S(1)}, u32[]{:S(2)}, u32[]{:S(2)}) collective-permute-start(f32[2,2,64,2]{3,2,1,0:T(8,128)S(1)} %get-tuple-element.163), channel_id=1, source_target_pairs={{8,0},{16,8},{24,16},{0,24},{9,1},{17,9},{25,17},{1,25},{10,2},{18... | collective-permute-start | bytes 6152 | tf_op jit(solution)/shard_map/ppermute | solution.py:44
  7.7 1.1 sine_convert_fusion
  8.8 1.0 fusion.131
  9.8 0.2 cosine_convert_fusion.1
  10.1 4.6 %all_gather.6 = bf16[2,128,128]{2,1,0:T(8,128)(2,1)S(1)} all-gather(bf16[2,64,128]{2,1,0:T(8,128)(2,1)S(1)} %get-tuple-element.6), channel_id=1, replica_groups=mesh['sec'=4,'row'=2,'col'=4] {'row'}, dimensions={1}, use_global_device_ids=true | all-gather | bytes 98304 | tf_op jit(solution)/shard_map/all_gather | solution.py:145
  14.7 12.8 %all_gather.7 = bf16[2,128,512]{2,1,0:T(8,128)(2,1)S(1)} all-gather(bf16[2,128,128]{2,1,0:T(8,128)(2,1)S(1)} %all_gather.6), channel_id=1, replica_groups=mesh['sec'=4,'row'=2,'col'=4] {'sec'}, dimensions={2}, use_global_device_ids=true | all-gather | bytes 327680 | tf_op jit(solution)/shard_map/all_gather | solution.py:146
  27.7 0.2 fusion.32
  28.0 2.6 %copy.11 = f32[2,64,128]{0,2,1:T(8,128)} copy(f32[2,64,128]{2,1,0:T(8,128)S(1)} %fusion.48) | data formatting | bytes 131072 | tf_op jit(solution)/shard_map/reshape | solution.py:155
  30.6 44.3 %scatter_custom_fusion = f32[256,2]{1,0:T(8,128)S(1)} fusion(s32[8192]{0:T(1024)} %bitcast.455, f32[8192,2]{1,0:T(8,128)} %bitcast.454, f32[]{:T(128)} %constant.36.clone.1), kind=kCustom, calls=%fused_computation.441 | custom fusion | flops 16384 | bytes 2560 | tf_op jit(solution)/shard_map/scatter-add | solution.py:154
  75.0 57.2 %scatter_custom_fusion.1 = f32[256]{0:T(256)S(1)} fusion(s32[8192]{0:T(1024)} %bitcast.456, f32[8192]{0:T(1024)S(1)} %broadcast.405, f32[]{:T(128)} %constant.36.clone.1), kind=kCustom, calls=%fused_computation.466 | custom fusion | flops 8192 | bytes 1536 | tf_op jit(solution)/shard_map/scatter-add | solution.py:157
  132.2 37.3 %all-reduce = (f32[256,2]{1,0:T(8,128)S(1)}, f32[256]{0:T(256)S(1)}) all-reduce(f32[256,2]{1,0:T(8,128)S(1)} %scatter_custom_fusion, f32[256]{0:T(256)S(1)} %scatter_custom_fusion.1), channel_id=1, replica_groups=mesh['sec'=4,'row'=2,'col'=4] {'sec','row'}, use_global_device_ids=true, to_apply=%region_1.2 | all-reduce | flops 768 | bytes 6144 | tf_op jit(solution)/shard_map/psum | solution.py:160
  169.7 2.0 %collective-permute-start.3 = (f32[2,2,2,132]{3,2,1,0:T(2,128)S(1)}, f32[2,2,2,132]{3,2,1,0:T(2,128)S(1)}, u32[]{:S(2)}, u32[]{:S(2)}) collective-permute-start(f32[2,2,2,132]{3,2,1,0:T(2,128)S(1)} %get-tuple-element.157), channel_id=1, source_target_pairs={{4,0},{0,4},{5,1},{1,5},{6,2},{2,6},{7,3},{3,7},{12,8},{8,12},{13,... | collective-permute-start | bytes 12680 | tf_op jit(solution)/shard_map/ppermute | solution.py:44
  171.7 1.6 collective-permute-done.2
  173.6 1.7 collective-permute-start.5
  175.5 0.7 copy.10
  176.1 4.9 %collective-permute-done.4 = f32[2,2,68,132]{3,2,1,0:T(8,128)S(1)} collective-permute-done((f32[2,2,68,132]{3,2,1,0:T(8,128)S(1)}, f32[2,2,68,132]{3,2,1,0:T(8,128)S(1)}, u32[]{:S(2)}, u32[]{:S(2)}) %collective-permute-start.4) | collective-permute-done | bytes 143648 | tf_op jit(solution)/shard_map/ppermute | solution.py:41
  181.1 0.9 collective-permute-done.5
  181.9 0.3 pad_maximum_fusion.2
  182.4 1.3 fusion.31
  183.7 0.9 fusion.21
  184.7 1.3 fusion.11
  186.2 0.3 broadcast_multiply_fusion
  186.5 0.3 broadcast_multiply_fusion.26
  186.9 0.4 broadcast_multiply_fusion.23
  187.2 0.4 broadcast_multiply_fusion.30
  187.9 0.3 broadcast_multiply_fusion.14
  188.2 0.3 broadcast_multiply_fusion.4
  188.5 0.3 broadcast_multiply_fusion.5
  193.4 1.4 copy-done
  (60 shorter events, 5.9 us)
Async XLA Ops:
  2.6 166.9 %collective-permute-start = (f32[2,2,64,2]{3,2,1,0:T(8,128)S(1)}, f32[2,2,64,2]{3,2,1,0:T(8,128)S(1)}, u32[]{:S(2)}, u32[]{:S(2)}) collective-permute-start(f32[2,2,64,2]{3,2,1,0:T(8,128)S(1)} %get-tuple-element.162), channel_id=1, source_target_pairs={{0,8},{8,16},{16,24},{24,0},{1,9},{9,17},{17,25},{25,1},{2,10},{10... | collective-permute-start | bytes 6152 | tf_op jit(solution)/shard_map/ppermute | solution.py:41
  5.6 163.8 %collective-permute-start.1 = (f32[2,2,64,2]{3,2,1,0:T(8,128)S(1)}, f32[2,2,64,2]{3,2,1,0:T(8,128)S(1)}, u32[]{:S(2)}, u32[]{:S(2)}) collective-permute-start(f32[2,2,64,2]{3,2,1,0:T(8,128)S(1)} %get-tuple-element.163), channel_id=1, source_target_pairs={{8,0},{16,8},{24,16},{0,24},{9,1},{17,9},{25,17},{1,25},{10,2},{18... | collective-permute-start | bytes 6152 | tf_op jit(solution)/shard_map/ppermute | solution.py:44
  169.6 3.7 %collective-permute-start.2 = (f32[2,2,2,132]{3,2,1,0:T(2,128)S(1)}, f32[2,2,2,132]{3,2,1,0:T(2,128)S(1)}, u32[]{:S(2)}, u32[]{:S(2)}) collective-permute-start(f32[2,2,2,132]{3,2,1,0:T(2,128)S(1)} %get-tuple-element.156), channel_id=1, source_target_pairs={{0,4},{4,0},{1,5},{5,1},{2,6},{6,2},{3,7},{7,3},{8,12},{12,8},{9,1... | collective-permute-start | bytes 12680 | tf_op jit(solution)/shard_map/ppermute | solution.py:41
  169.7 3.7 %collective-permute-start.3 = (f32[2,2,2,132]{3,2,1,0:T(2,128)S(1)}, f32[2,2,2,132]{3,2,1,0:T(2,128)S(1)}, u32[]{:S(2)}, u32[]{:S(2)}) collective-permute-start(f32[2,2,2,132]{3,2,1,0:T(2,128)S(1)} %get-tuple-element.157), channel_id=1, source_target_pairs={{4,0},{0,4},{5,1},{1,5},{6,2},{2,6},{7,3},{3,7},{12,8},{8,12},{13,... | collective-permute-start | bytes 12680 | tf_op jit(solution)/shard_map/ppermute | solution.py:44
  173.6 7.5 %collective-permute-start.4 = (f32[2,2,68,132]{3,2,1,0:T(8,128)S(1)}, f32[2,2,68,132]{3,2,1,0:T(8,128)S(1)}, u32[]{:S(2)}, u32[]{:S(2)}) collective-permute-start(f32[2,2,68,132]{3,2,1,0:T(8,128)S(1)} %pad_maximum_fusion.3), channel_id=1, source_target_pairs={{0,1},{1,2},{2,3},{3,0},{4,5},{5,6},{6,7},{7,4},{8,9},{9,10},{10,1... | collective-permute-start | bytes 430856 | tf_op jit(solution)/shard_map/ppermute | solution.py:41
  173.6 8.3 %collective-permute-start.5 = (f32[2,2,68,132]{3,2,1,0:T(8,128)S(1)}, f32[2,2,68,132]{3,2,1,0:T(8,128)S(1)}, u32[]{:S(2)}, u32[]{:S(2)}) collective-permute-start(f32[2,2,68,132]{3,2,1,0:T(8,128)S(1)} %pad_maximum_fusion.3), channel_id=1, source_target_pairs={{1,0},{2,1},{3,2},{0,3},{5,4},{6,5},{7,6},{4,7},{9,8},{10,9},{11,1... | collective-permute-start | bytes 430856 | tf_op jit(solution)/shard_map/ppermute | solution.py:44
  193.4 1.5 copy-start
where the time goes:
time: 196 us; the launch traced here: 195 us
  other arithmetic  117 us (60%)
  blocking collectives  54.7 us (28%)
  starting transfers between devices  9.04 us (5%)
  waiting for transfers between devices  7.51 us (4%)
  local copies, waits for them, and re-layouts  4.76 us (2%)
    scatter-add x1, other arithmetic, on_device(): jax.ops.segment_sum(jnp.ones((cell_count,), jnp.float32), flat_shells, nu...  57.2 us
    scatter-add x1, other arithmetic, on_device(): jax.ops.segment_sum(power_map.reshape(depth_z, cell_count).T, flat_shells...  44.3 us
    psum x1, blocking collectives, on_device(): totals, counts = lax.psum((totals, counts), ('sec', 'row'))  37.3 us
    all_gather x1, blocking collectives, on_device(): whole_plane = lax.all_gather(rows_all, 'sec', axis=2, tiled=True)  12.8 us
    ppermute x3, waiting for transfers between devices, with_halo(): lax.ppermute(lax.slice_in_dim(block, block.shape[dim] - width, None, axis...  6.56 us
    ppermute x3, starting transfers between devices, with_halo(): lax.ppermute(lax.slice_in_dim(block, 0, width, axis=dim), axis, backward)  5.84 us
    all_gather x1, blocking collectives, on_device(): rows_all = lax.all_gather(order_b, 'row', axis=1, tiled=True)  4.59 us
    unnamed x37, other arithmetic  4.13 us
  transfers between devices with their start and end apart: 6, of which 4 were waited for; matrix products, arithmetic and copies ran while one was open for 55% of the time, Pallas kernels for 0%

commit v1 on v0

v1 whole, which is shorter than its diff:
```python
import functools
import math

import jax
import jax.numpy as jnp
import ml_dtypes
import numpy as np
from jax import lax
from jax.experimental import pallas as pl
from jax.experimental.pallas import tpu as pltpu
from jax.sharding import PartitionSpec as P

NSHELL = 256
LO = 16
ROWS = 72
F32 = jnp.float32
BF16 = jnp.bfloat16

LATTICE = (
    (0, 0, 0),
    (1, 0, 0),
    (-1, 0, 0),
    (0, 1, 0),
    (0, -1, 0),
    (0, 0, 1),
    (0, 0, -1),
    (1, 1, 0),
    (-1, -1, 0),
    (1, -1, 0),
    (-1, 1, 0),
    (1, 0, 1),
    (-1, 0, -1),
    (1, 0, -1),
    (-1, 0, 1),
    (0, 1, 1),
    (0, -1, -1),
    (0, 1, -1),
    (0, -1, 1),
)
WEIGHTS = (1.0 / 3.0,) + (1.0 / 18.0,) * 6 + (1.0 / 36.0,) * 12


def xor_pairs(count, bits):
    return [(i, i ^ bits) for i in range(count)]


def shift_pairs(count, step):
    return [(i, (i + step) % count) for i in range(count)]


def ring_moves(count):
    if count == 2:
        return [xor_pairs(2, 1)]
    if count == 4:
        return [xor_pairs(4, 1), xor_pairs(4, 3)]
    return [shift_pairs(count, 1), shift_pairs(count, -1)]


def ring_pick(count, index):
    if count == 2:
        return 0, 0
    if count == 4:
        odd = lax.rem(index, 2)
        return 1 - odd, odd
    return 0, 1


def pair_product(first, second, count_second):
    return [
        (a * count_second + b, c * count_second + d) for a, c in first for b, d in second
    ]


def choose(items, which):
    if isinstance(which, int):
        return items[which]
    value = items[0]
    for number in range(1, len(items)):
        value = jnp.where(which == number, items[number], value)
    return value


def bf16_table(values):
    return np.asarray(values, np.float32).astype(ml_dtypes.bfloat16)


def angle_table(freq, pos, full):
    step = np.float32(2.0 * math.pi / full)
    return ((freq * pos) % full).astype(np.float32) * step


@functools.lru_cache(maxsize=None)
def make_tables(full_x, full_y, n_row, n_sec, wx, wy):
    half_x, half_y = full_x // 2, full_y // 2
    freq = np.arange(half_x)[:, None]
    pos = np.arange(full_x)[None, :]
    angles = angle_table(freq, pos, full_x)
    lower = -np.sin(angles)
    lower[0] = np.cos(angle_table(np.array([[half_x]]), pos, full_x))[0]
    table_x = np.concatenate([np.cos(angles), lower], 0)
    table_x = np.stack([table_x[:, r * wx : (r + 1) * wx] for r in range(n_row)])
    lanes = half_y + 128
    freq_y = np.arange(lanes)[None, :]
    angles = angle_table(np.arange(full_y)[:, None], freq_y, full_y)
    live = freq_y <= half_y
    table_y = np.concatenate([np.cos(angles) * live, np.sin(angles) * live], 1)
    hrows = half_x + 8
    radius = np.arange(hrows)[:, None] ** 2 + np.arange(lanes)[None, :] ** 2
    base = np.minimum(np.floor(np.sqrt(radius.astype(np.float64))).astype(np.int64), NSHELL - 1)
    valid = (np.arange(hrows)[:, None] <= half_x) & (np.arange(lanes)[None, :] <= half_y)
    hi = np.where(valid, base // LO, -1).astype(np.float32)
    lo = np.where(valid, base % LO, -1).astype(np.float32)
    mult_y = np.where(freq_y > half_y, 0, np.where((freq_y == 0) | (freq_y == half_y), 1, 2))
    signed_x = np.arange(full_x)
    signed_x = np.where(signed_x < half_x, signed_x, signed_x - full_x)
    signed_y = np.arange(full_y)
    signed_y = np.where(signed_y < half_y, signed_y, signed_y - full_y)
    square = signed_x[:, None] ** 2 + signed_y[None, :] ** 2
    root = np.floor(np.sqrt(square + 1.0) + 1e-9).astype(np.int64)
    special = (root * root == square + 1) & (root < NSHELL) & (square > 0)
    low_label = np.minimum(np.floor(np.sqrt(square.astype(np.float64))), NSHELL - 1)
    counts = np.bincount(low_label.astype(np.int64).ravel(), minlength=NSHELL)
    blocks = {}
    for r in range(n_row):
        for s in range(n_sec):
            where = np.argwhere(special[r * wx : (r + 1) * wx, s * wy : (s + 1) * wy])
            blocks[r, s] = [(int(a) + r * wx, int(b) + s * wy) for a, b in where]
    slots = max(len(v) for v in blocks.values())
    width = 128 * (-(-(n_row * slots) // 128))
    take_row = np.zeros((n_row * n_sec, wx, width))
    take_col = np.zeros((n_row * n_sec, wy, width))
    low = np.zeros((n_sec * width,))
    put_row = np.zeros((2 * hrows, n_sec * width))
    put_col = np.zeros((n_sec * width, lanes))
    for (r, s), points in blocks.items():
        for number, (kx, ky) in enumerate(points):
            lane = r * slots + number
            take_row[r * n_sec + s, kx - r * wx, lane] = 1
            take_col[r * n_sec + s, ky - s * wy, lane] = 1
            place = s * width + lane
            low[place] = root[kx, ky] - 1
            ax, ay = abs(int(signed_x[kx])), abs(int(signed_y[ky]))
            same = int(signed_x[kx]) * int(signed_y[ky]) >= 0 or ax == half_x or ay == half_y
            put_row[ax + (0 if same else hrows), place] = 1
            put_col[place, ay] = 1
    spread = (np.arange(NSHELL)[None, :] % LO == np.arange(LO)[:, None]).astype(np.float32)
    return dict(
        width=width,
        table_x=bf16_table(table_x),
        table_y=bf16_table(table_y),
        hi=hi,
        lo=lo,
        mult_y=mult_y.astype(np.float32),
        counts=counts.astype(np.float32)[None, :],
        take_row=np.asarray(take_row, np.float32),
        take_col=bf16_table(take_col),
        low=low.astype(np.float32)[None, :],
        put_row=np.asarray(put_row, np.float32),
        put_col=bf16_table(put_col),
        spread=spread,
    )


def own_densities(labels_ref, jitter_ref, z):
    heavy = labels_ref[z] == 1
    first = jnp.where(heavy, F32(1.0), F32(0.2)) * jitter_ref[0, z]
    second = jnp.where(heavy, F32(0.2), F32(1.0)) * jitter_ref[1, z]
    return first, second


def pack_kernel(n_sec, labels_ref, jitter_ref, shells_ref, take_row_ref, take_col_ref,
                col_ref, row_ref, edge_ref):
    depth, wx, wy = labels_ref.shape
    densities = [own_densities(labels_ref, jitter_ref, z) for z in range(depth)]
    edges = []
    for c in range(2):
        for z in range(depth):
            tile = densities[z][c]
            at = (c * depth + z) * wx
            col_ref[at : at + wx] = tile.astype(BF16)
            edges += [tile[0:2], tile[wx - 2 : wx]]
    for z in range(depth):
        row_ref[z * wx : (z + 1) * wx] = (densities[z][0] - densities[z][1]).astype(BF16)
    edge = jnp.concatenate(edges, axis=0).astype(BF16)
    edge_ref[...] = edge
    at = depth * wx
    count = edge.shape[0]
    row_ref[at : at + count] = edge
    block = lax.axis_index("row") * n_sec + lax.axis_index("sec")
    picked = jnp.dot(
        shells_ref[...].astype(F32).astype(BF16), take_col_ref[block], preferred_element_type=F32
    )
    marks = jnp.sum(picked * take_row_ref[block], axis=0, keepdims=True)
    width = marks.shape[1]
    lines = [marks[:, g * 128 : (g + 1) * 128] for g in range(width // 128)]
    lines.append(jnp.zeros((16 - len(lines), 128), F32))
    row_ref[at + count :] = jnp.concatenate(lines, axis=0).astype(BF16)


def middle_kernel(n_row, n_col, labels_ref, jitter_ref, *refs):
    depth, wx, wy = labels_ref.shape
    col_moves, row_moves = len(ring_moves(n_col)), len(ring_moves(n_row))
    col_refs, refs = refs[:col_moves], refs[col_moves:]
    row_refs, refs = refs[:n_row], refs[n_row:]
    diag_refs, refs = refs[: col_moves * row_moves], refs[col_moves * row_moves :]
    table_ref, msg_ref, dens_ref, lanes_ref = refs
    row, col = lax.axis_index("row"), lax.axis_index("col")
    full_x = table_ref.shape[1]

    for z in range(depth):
        half = None
        for k in range(n_row):
            part = jnp.dot(
                table_ref[row ^ k],
                row_refs[k][z * wx : (z + 1) * wx],
                preferred_element_type=F32,
            )
            half = part if half is None else half + part
        msg_ref[z * full_x : (z + 1) * full_x] = half.astype(BF16)

    at = depth * wx
    count = 8 * depth
    marks = sum(ref[at + count : at + count + 16].astype(F32) for ref in row_refs)

    own = [own_densities(labels_ref, jitter_ref, z) for z in range(depth)]
    col_prev, col_next = ring_pick(n_col, col)
    before = choose([r[...] for r in col_refs], col_prev).astype(F32)
    after = choose([r[...] for r in col_refs], col_next).astype(F32)
    edge_list = [r[at : at + count].astype(F32) for r in row_refs]
    edge_prev = choose(edge_list, row ^ lax.rem(row + n_row - 1, n_row)) if n_row > 2 else edge_list[1]
    edge_next = choose(edge_list, row ^ lax.rem(row + 1, n_row)) if n_row > 2 else edge_list[1]
    row_prev, row_next = ring_pick(n_row, row)
    diag = [r[...].astype(F32) for r in diag_refs]

    def diag_of(row_which, col_which):
        lines = [
            choose(diag[m * col_moves : (m + 1) * col_moves], col_which) for m in range(row_moves)
        ]
        return choose(lines, row_which)

    corner = {
        (0, -1): diag_of(row_prev, col_prev),
        (0, 1): diag_of(row_prev, col_next),
        (1, -1): diag_of(row_next, col_prev),
        (1, 1): diag_of(row_next, col_next),
    }
    lane = lax.broadcasted_iota(jnp.int32, (ROWS, wy), 1)
    gap = jnp.zeros((ROWS - wx - 4, wy), F32)
    strips = jnp.zeros((ROWS, wy), F32)
    layers = depth + 4
    for c in range(2):
        for layer in range(layers):
            z = layer - 2
            if z < 0:
                source, plane, low, high = before, depth + z, corner[0, -1], corner[1, -1]
            elif z >= depth:
                source, plane, low, high = after, z - depth, corner[0, 1], corner[1, 1]
            else:
                source, plane, low, high = None, z, edge_prev, edge_next
            where = c * depth + plane
            if source is None:
                body = own[plane][c]
            else:
                body = source[where * wx : (where + 1) * wx]
            tail = jnp.concatenate(
                [high[where * 4 : where * 4 + 2], gap, low[where * 4 + 2 : where * 4 + 4]], axis=0
            )
            tile = jnp.concatenate([body, tail], axis=0)
            group = c * layers + layer
            dens_ref[group] = tile
            at_lane = 8 * group
            moved = pltpu.roll(tile, (at_lane + 2) % wy, 1)
            strips = jnp.where((lane >= at_lane) & (lane < at_lane + 4), moved, strips)
    strips = strips + pltpu.roll(strips, 4, 1)
    lanes_ref[...] = strips
    at = depth * full_x
    pad = jnp.zeros((80 - ROWS, wy), F32)
    msg_ref[at : at + 80] = jnp.concatenate([strips, pad], axis=0).astype(BF16)
    msg_ref[at + 80 : at + 96] = marks.astype(BF16)


def turn(tile, shift, axis):
    shift = shift % tile.shape[axis]
    return tile if shift == 0 else pltpu.roll(tile, shift, axis)


def pull_of(below, here, above):
    around = below + above
    line_y = turn(here, -1, 1) + turn(here, 1, 1)
    line_x = turn(here, -1, 0) + turn(here, 1, 0)
    flat = 2.0 * here + around
    mix = flat + line_y
    pull_x = turn(mix, -1, 0) - turn(mix, 1, 0)
    mix = flat + line_x
    pull_y = turn(mix, -1, 1) - turn(mix, 1, 1)
    gap = above - below
    pull_z = 2.0 * gap + turn(gap, -1, 0) + turn(gap, 1, 0) + turn(gap, -1, 1) + turn(gap, 1, 1)
    return pull_x, pull_y, pull_z


def relax_terms(density, velocity):
    vx, vy, vz = velocity
    squared = vx * vx + vy * vy + vz * vz
    rest = density * (1.0 - 1.875 * squared)
    terms = [WEIGHTS[0] * rest]
    for number in range(1, 19, 2):
        offsets = LATTICE[number]
        projected = None
        for axis in range(3):
            if offsets[axis]:
                part = velocity[axis] if offsets[axis] > 0 else -velocity[axis]
                projected = part if projected is None else projected + part
        weighted = density * projected
        even = WEIGHTS[number] * (rest + 5.625 * (weighted * projected))
        odd = (WEIGHTS[number] * 3.75) * weighted
        terms += [even + odd, even - odd]
    return terms


def cells_kernel(dens_ref, out_ref):
    _, depth, wx, _ = out_ref.shape
    layers = depth + 4
    scale = -1.6 / 36.0
    for layer in range(1, layers - 1):
        for c in range(2):
            other = (1 - c) * layers + layer
            pulls = pull_of(dens_ref[other - 1], dens_ref[other], dens_ref[other + 1])
            velocity = [scale * p for p in pulls]
            terms = relax_terms(dens_ref[c * layers + layer], velocity)
            for number in range(19):
                cx, cy, cz = LATTICE[number]
                z = layer - 2 + cz
                if 0 <= z < depth:
                    tile = turn(turn(terms[number], cx, 0), cy, 1)
                    out_ref[c * 19 + number, z] = tile[:wx]


def final_kernel(n_sec, width, msg_own_ref, *refs):
    msg_refs = [msg_own_ref] + list(refs[: n_sec - 1])
    (lanes_ref, cells_ref, table_ref, hi_ref, lo_ref, mult_ref, counts_ref, low_ref, put_row_ref,
     put_col_ref, spread_ref, out_ref, spec_ref, lhs_ref, mark_ref, quant_ref) = refs[n_sec - 1 :]
    _, depth, wx, wy = out_ref.shape
    layers = depth + 4
    sec = lax.axis_index("sec")
    half_y = table_ref.shape[1] // 2 - 128
    lanes = half_y + 128
    full_y = table_ref.shape[0]
    full_x = lhs_ref.shape[0] // depth
    half_x = full_x // 2
    hrows = half_x + 8
    at = depth * full_x

    for k in range(n_sec):
        start = pl.multiple_of((sec ^ k) * wy, wy)
        lhs_ref[:, pl.ds(start, wy)] = msg_refs[k][:at]
        mark_ref[sec ^ k] = msg_refs[k][at + 80 : at + 96].astype(F32)
    transform = jnp.dot(lhs_ref[...], table_ref[...], preferred_element_type=F32)
    marks = jnp.concatenate(
        [mark_ref[s][g : g + 1] for s in range(n_sec) for g in range(width // 128)], axis=1
    )
    nudge = marks - low_ref[...]
    nudges = jnp.dot(
        (put_row_ref[...] * nudge).astype(BF16), put_col_ref[...], preferred_element_type=F32
    )
    plus, minus = nudges[:hrows], nudges[hrows:]
    mult = mult_ref[...]
    row_zero = lax.broadcasted_iota(jnp.int32, (half_x, lanes), 0) == 0
    rest = jnp.zeros((7, lanes), F32)
    slot = 0
    for z in range(depth):
        real = transform[z * full_x : z * full_x + half_x]
        imag = transform[z * full_x + half_x : (z + 1) * full_x]
        rc, rs = real[:, :lanes], real[:, lanes:]
        ic, is_ = imag[:, :lanes], imag[:, lanes:]
        top = rc * rc + rs * rs
        low = ic * ic + is_ * is_
        both = top + low
        cross = 2.0 * (rc * is_ - ic * rs)
        total = mult * jnp.where(row_zero, top, 2.0 * both)
        total = jnp.concatenate([total, mult * low[0:1], rest], axis=0)
        shifted = plus[:half_x] * jnp.where(row_zero, top, both + cross) + minus[:half_x] * (
            both - cross
        )
        shifted = jnp.concatenate([shifted, plus[half_x : half_x + 1] * low[0:1], rest], axis=0)
        for value in (total, shifted):
            head = value.astype(BF16).astype(F32)
            quant_ref[slot] = head
            quant_ref[slot + 1] = value - head
            slot += 2
    quant_ref[slot] = plus + minus
    slots = slot + 1

    digit = lax.broadcasted_iota(jnp.int32, (LO, lanes), 0).astype(F32)

    def add_rows(step, acc):
        start = pl.multiple_of(step * 8, 8)
        hi8 = hi_ref[pl.ds(start, 8)]
        lo8 = lo_ref[pl.ds(start, 8)]
        q8 = [quant_ref[q, pl.ds(start, 8)] for q in range(slots)]
        left, right = [], []
        for r in range(8):
            mask = hi8[r : r + 1] == digit
            right.append(jnp.where(lo8[r : r + 1] == digit, F32(1.0), F32(0.0)).astype(BF16))
            left.append(
                jnp.concatenate(
                    [jnp.where(mask, q[r : r + 1], F32(0.0)).astype(BF16) for q in q8], axis=0
                )
            )
        return acc + lax.dot_general(
            jnp.concatenate(left, axis=1),
            jnp.concatenate(right, axis=1),
            (((1,), (1,)), ((), ())),
            preferred_element_type=F32,
        )

    acc = lax.fori_loop(0, hrows // 8, add_rows, jnp.zeros((slots * LO, LO), F32))
    wide = lax.dot_general(
        acc, spread_ref[...], (((1,), (0,)), ((), ())),
        precision=lax.Precision.HIGHEST, preferred_element_type=F32,
    )
    at_hi = lax.broadcasted_iota(jnp.int32, (LO, NSHELL), 1) // LO
    keep = at_hi == lax.broadcasted_iota(jnp.int32, (LO, NSHELL), 0)

    def line(q):
        return jnp.sum(
            jnp.where(keep, wide[q * LO : (q + 1) * LO], 0.0), axis=0, keepdims=True
        )

    def moved(value):
        return pltpu.roll(jnp.broadcast_to(value, (8, NSHELL)), 1, 1)[0:1] - value

    counts = counts_ref[...] + moved(line(slots - 1))
    norm = counts * float(full_x * full_y)
    spectrum = [
        (line(4 * z) + line(4 * z + 1) + moved(line(4 * z + 2) + line(4 * z + 3))) / norm
        for z in range(depth)
    ]
    spec_ref[...] = jnp.concatenate(spectrum, axis=0)

    index = sec
    prev_k = index ^ lax.rem(index + n_sec - 1, n_sec)
    next_k = index ^ lax.rem(index + 1, n_sec)
    strips = [r[at : at + 80].astype(F32)[:ROWS] for r in msg_refs]
    place = lax.rem(lax.broadcasted_iota(jnp.int32, (ROWS, wy), 1), 8)
    tile = jnp.where(
        place < 2,
        choose(strips, prev_k),
        jnp.where(place >= 6, choose(strips, next_k), lanes_ref[...]),
    )
    pulls = pull_of(turn(tile, 8, 1), tile, turn(tile, -8, 1))
    span = 8 * layers
    first = lax.broadcasted_iota(jnp.int32, (ROWS, wy), 1) < span
    scale = -1.6 / 36.0
    velocity = [scale * jnp.where(first, turn(p, -span, 1), turn(p, span, 1)) for p in pulls]
    terms = relax_terms(tile, velocity)
    lane = lax.broadcasted_iota(jnp.int32, (wx, wy), 1)
    for number in range(19):
        cx, cy, cz = LATTICE[number]
        term = turn(terms[number], cx, 0)[:wx]
        if cy == 0:
            term = jnp.where(place[:wx] == 1, turn(term, -4, 1), term)
            mask = (lane == 0) | (lane == wy - 1)
        else:
            mask = lane < 2 if cy > 0 else lane >= wy - 2
        for c in range(2):
            for z in range(depth):
                group = 8 * (c * layers + 2 + z - cz)
                back = {1: group + 1, -1: group + 5 - (wy - 2), 0: group + 2}[cy]
                q = c * 19 + number
                out_ref[q, z] = jnp.where(mask, turn(term, -back, 1), cells_ref[q, z])


def call(kernel, outs, scratch=(), flops=0, moved=0):
    return pl.pallas_call(
        kernel,
        out_shape=outs,
        scratch_shapes=list(scratch),
        compiler_params=pltpu.CompilerParams(vmem_limit_bytes=48 * 1024 * 1024),
        cost_estimate=pl.CostEstimate(flops=flops, bytes_accessed=moved, transcendentals=0),
    )


def on_device(n_sec, n_row, n_col, labels, jitter, shells):
    depth, wx, wy = labels.shape
    full_x, full_y = wx * n_row, wy * n_sec
    tables = make_tables(full_x, full_y, n_row, n_sec, wx, wy)
    width = tables["width"]
    layers = depth + 4
    count = 8 * depth
    shape = jax.ShapeDtypeStruct

    col_msg, row_msg, edge_msg = call(
        functools.partial(pack_kernel, n_sec),
        [
            shape((2 * depth * wx, wy), BF16),
            shape((depth * wx + count + 16, wy), BF16),
            shape((count, wy), BF16),
        ],
    )(labels, jitter, shells, tables["take_row"], tables["take_col"])

    col_got = [lax.ppermute(col_msg, "col", m) for m in ring_moves(n_col)]
    row_got = [lax.ppermute(row_msg, "row", xor_pairs(n_row, k)) for k in range(1, n_row)]
    diag_got = [
        lax.ppermute(edge_msg, ("row", "col"), pair_product(a, b, n_col))
        for a in ring_moves(n_row)
        for b in ring_moves(n_col)
    ]

    msg_rows = depth * full_x + 96
    msg, dens, strips = call(
        functools.partial(middle_kernel, n_row, n_col),
        [
            shape((msg_rows, wy), BF16),
            shape((2 * layers, ROWS, wy), F32),
            shape((ROWS, wy), F32),
        ],
    )(labels, jitter, *col_got, row_msg, *row_got, *diag_got, tables["table_x"])

    sec_got = [lax.ppermute(msg, "sec", xor_pairs(n_sec, k)) for k in range(1, n_sec)]

    cells = call(
        cells_kernel,
        shape((38, depth, wx, wy), F32),
        flops=38 * depth * wx * wy * 40,
        moved=4 * 38 * depth * wx * wy,
    )(dens)

    hrows, lanes = full_x // 2 + 8, full_y // 2 + 128
    populations, spectrum = call(
        functools.partial(final_kernel, n_sec, width),
        [shape((38, depth, wx, wy), F32), shape((depth, NSHELL), F32)],
        [
            pltpu.VMEM((depth * full_x, full_y), BF16),
            pltpu.VMEM((n_sec, 16, 128), F32),
            pltpu.VMEM((4 * depth + 1, hrows, lanes), F32),
        ],
    )(
        msg, *sec_got, strips, cells, tables["table_y"], tables["hi"], tables["lo"],
        tables["mult_y"], tables["counts"], tables["low"], tables["put_row"], tables["put_col"],
        tables["spread"],
    )
    return populations, spectrum


def solution(mesh):
    in_specs = (P("col", "row", "sec"), P(None, "col", "row", "sec"), P("row", "sec"))
    out_specs = (P(None, "col", "row", "sec"), P("col", None))
    sizes = [mesh.shape[name] for name in ("sec", "row", "col")]
    return jax.shard_map(
        functools.partial(on_device, *sizes),
        mesh=mesh,
        in_specs=in_specs,
        out_specs=out_specs,
        check_vma=False,
    )
```

time: 196 us -> 33.7 us (0.17)
  other arithmetic: 117 us -> 0 us
  blocking collectives: 54.7 us -> 0 us
  Pallas kernels: 0 us -> 8.95 us
    scatter-add x2 -> x0, other arithmetic: 102 us -> none  [the longest x1 57.2 us: on_device(): jax.ops.segment_sum(jnp.ones((cell_count,), jnp.float32), flat_shells, nu...]
    psum x1 -> x0, blocking collectives: 37.3 us -> none  [on_device(): totals, counts = lax.psum((totals, counts), ('sec', 'row'))]
    all_gather x2 -> x0, blocking collectives: 17.4 us -> none  [the longest x1 12.8 us: on_device(): whole_plane = lax.all_gather(rows_all, 'sec', axis=2, tiled=True)]
    pallas_call x0 -> x4, Pallas kernels: none -> 8.95 us  [the longest x1 6.84 us: on_device(): call(functools.partial(final_kernel, n_sec, width), [shape((38, depth, wx...]
    another operation x7 -> x0, other arithmetic: 4.77 us -> none  [the longest x4 3.65 us: pull_sums(): return jnp.stack(totals_axis, axis=1)]
    unnamed x37 -> x0, other arithmetic: 4.13 us -> none
    unnamed x3 -> x30, local copies, waits for them, and re-layouts: 2.1 us -> 5.35 us
    mul x11 -> x0, other arithmetic: 2.7 us -> none  [the longest x7 2.15 us: relax_stack(): 4.5 * projected * projected]
  transfers between devices with their start and end apart: 6 -> 8, of which waited for: 4 -> 3; matrix products, arithmetic and copies ran while one was open for 55% -> 0% of each run, Pallas kernels for 0% -> 5%
where the time goes in v1:
time: 33.7 us; the launch traced here: 33.3 us
  starting transfers between devices  10.8 us (32%)
  Pallas kernels  8.95 us (27%)
  waiting for transfers between devices  7.46 us (22%)
  local copies, waits for them, and re-layouts  5.35 us (16%)
  between operations  0.77 us (2%)
    pallas_call x1, Pallas kernels, on_device(): call(functools.partial(final_kernel, n_sec, width), [shape((38, depth, wx...  6.84 us
    unnamed x30, local copies, waits for them, and re-layouts  5.35 us
    ppermute x3, waiting for transfers between devices, on_device(): lax.ppermute(msg, 'sec', xor_pairs(n_sec, k))  5.24 us
    ppermute x3, starting transfers between devices, on_device(): lax.ppermute(msg, 'sec', xor_pairs(n_sec, k))  4.43 us
    ppermute x2, starting transfers between devices, on_device(): col_got = [lax.ppermute(col_msg, 'col', m) for m in ring_moves(n_col)]  3.11 us
    ppermute x2, waiting for transfers between devices, on_device(): lax.ppermute(edge_msg, ('row', 'col'), pair_product(a, b, n_col))  2.22 us
    ppermute x2, starting transfers between devices, on_device(): lax.ppermute(edge_msg, ('row', 'col'), pair_product(a, b, n_col))  1.72 us
    pallas_call x1, Pallas kernels, on_device(): call(cells_kernel, shape((38, depth, wx, wy), F32), flops=38 * depth * wx...  1.7 us
  transfers between devices with their start and end apart: 8, of which 3 were waited for; matrix products, arithmetic and copies ran while one was open for 0% of the time, Pallas kernels for 5%

profile of v1, /device:TPU:0, one launch (start us, length us, event | category | flops | bytes accessed | tf_op | source)
XLA Modules:
  0.0 33.3 jit_solution(5087175373388170488)
XLA Ops:
  0.6 0.0 copy-start.12
  0.6 0.0 copy-start.14
  0.7 0.0 copy-start.13
  0.7 0.0 copy-start
  0.7 0.0 copy-start.1
  0.7 1.0 %copy-done.1 = f32[2,2,64,128]{3,2,1,0:T(8,128)S(1)} copy-done((f32[2,2,64,128]{3,2,1,0:T(8,128)S(1)}, f32[2,2,64,128]{3,2,1,0:T(8,128)}, u32[]{:S(2)}) %copy-start.1) | copy-done | bytes 131096
  1.7 0.9 %copy-done.4 = bf16[8,128,128]{2,1,0:T(8,128)(2,1)S(1)} copy-done((bf16[8,128,128]{2,1,0:T(8,128)(2,1)S(1)}, bf16[8,128,128]{2,1,0:T(8,128)(2,1)}, u32[]{:S(2)}) %copy-start.4) | copy-done | bytes 262168
  2.6 0.9 %copy-done.5 = f32[8,64,128]{2,1,0:T(8,128)S(1)} copy-done((f32[8,64,128]{2,1,0:T(8,128)S(1)}, f32[8,64,128]{2,1,0:T(8,128)}, u32[]{:S(2)}) %copy-start.5) | copy-done | bytes 262168
  3.6 0.8 %copy-done.6 = s32[2,64,128]{2,1,0:T(8,128)S(1)} copy-done((s32[2,64,128]{2,1,0:T(8,128)S(1)}, s32[2,64,128]{2,1,0:T(8,128)}, u32[]{:S(2)}) %copy-start.6) | copy-done | bytes 65560
  4.4 0.8 %copy-done.10 = s32[64,128]{1,0:T(8,128)S(1)} copy-done((s32[64,128]{1,0:T(8,128)S(1)}, s32[64,128]{1,0:T(8,128)}, u32[]{:S(2)}) %copy-start.10) | copy-done | bytes 32792
  5.2 0.2 shard_map.158
  5.3 2.4 %collective-permute-start.1 = (bf16[256,128]{1,0:T(8,128)(2,1)S(1)}, bf16[256,128]{1,0:T(8,128)(2,1)S(1)}, u32[]{:S(2)}, u32[]{:S(2)}) collective-permute-start(bf16[256,128]{1,0:T(8,128)(2,1)S(1)} %get-tuple-element.8), channel_id=1, source_target_pairs={{0,3},{1,2},{2,1},{3,0},{4,7},{5,6},{6,5},{7,4},{8,11},{9,10},{10,... | collective-permute-start | bytes 196616 | tf_op jit(solution)/shard_map/ppermute | solution.py:501
  7.8 0.7 %collective-permute-start = (bf16[256,128]{1,0:T(8,128)(2,1)S(1)}, bf16[256,128]{1,0:T(8,128)(2,1)S(1)}, u32[]{:S(2)}, u32[]{:S(2)}) collective-permute-start(bf16[256,128]{1,0:T(8,128)(2,1)S(1)} %get-tuple-element.8), channel_id=1, source_target_pairs={{0,1},{1,0},{2,3},{3,2},{4,5},{5,4},{6,7},{7,6},{8,9},{9,8},{10,11... | collective-permute-start | bytes 196616 | tf_op jit(solution)/shard_map/ppermute | solution.py:501
  8.4 1.5 %collective-permute-start.2 = (bf16[160,128]{1,0:T(8,128)(2,1)S(1)}, bf16[160,128]{1,0:T(8,128)(2,1)S(1)}, u32[]{:S(2)}, u32[]{:S(2)}) collective-permute-start(bf16[160,128]{1,0:T(8,128)(2,1)S(1)} %get-tuple-element.9.refs_2_), channel_id=1, source_target_pairs={{0,4},{4,0},{1,5},{5,1},{2,6},{6,2},{3,7},{7,3},{8,12},{12,8},{9,1... | collective-permute-start | bytes 122888 | tf_op jit(solution)/shard_map/ppermute | solution.py:502
  10.0 0.0 collective-permute-start.4
  10.0 1.7 %collective-permute-start.3 = (bf16[16,128]{1,0:T(8,128)(2,1)S(1)}, bf16[16,128]{1,0:T(8,128)(2,1)S(1)}, u32[]{:S(2)}, u32[]{:S(2)}) collective-permute-start(bf16[16,128]{1,0:T(8,128)(2,1)S(1)} %get-tuple-element.10), channel_id=1, source_target_pairs={{0,5},{1,4},{2,7},{3,6},{4,1},{5,0},{6,3},{7,2},{8,13},{9,12},{10,... | collective-permute-start | bytes 12296 | tf_op jit(solution)/shard_map/ppermute | solution.py:504
  11.7 2.2 %collective-permute-done.4.refs_5_ = bf16[16,128]{1,0:T(8,128)(2,1)S(1)} collective-permute-done((bf16[16,128]{1,0:T(8,128)(2,1)S(1)}, bf16[16,128]{1,0:T(8,128)(2,1)S(1)}, u32[]{:S(2)}, u32[]{:S(2)}) %collective-permute-start.4) | collective-permute-done | bytes 4128 | tf_op jit(solution)/shard_map/ppermute | solution.py:504
  13.9 0.0 collective-permute-done.3.refs_4_
  13.9 0.0 collective-permute-done.2.refs_3_
  13.9 0.0 collective-permute-done.1.refs_1_
  13.9 0.0 collective-permute-done.refs_0_
  13.9 0.0 copy-start.9
  13.9 0.8 %copy-done.9 = bf16[2,128,64]{2,1,0:T(8,128)(2,1)S(1)} copy-done((bf16[2,128,64]{2,1,0:T(8,128)(2,1)S(1)}, bf16[2,128,64]{2,1,0:T(8,128)(2,1)}, u32[]{:S(2)}) %copy-start.9) | copy-done | bytes 32792
  14.8 0.3 shard_map.159
  15.0 3.6 %collective-permute-start.7 = (bf16[352,128]{1,0:T(8,128)(2,1)S(1)}, bf16[352,128]{1,0:T(8,128)(2,1)S(1)}, u32[]{:S(2)}, u32[]{:S(2)}) collective-permute-start(bf16[352,128]{1,0:T(8,128)(2,1)S(1)} %get-tuple-element.11.msg_own_ref), channel_id=1, source_target_pairs={{0,24},{8,16},{16,8},{24,0},{1,25},{9,17},{17,9},{25,1},{2,26},{10... | collective-permute-start | bytes 270344 | tf_op jit(solution)/shard_map/ppermute | solution.py:519
  18.7 0.0 collective-permute-start.6
  18.7 0.8 %collective-permute-start.5 = (bf16[352,128]{1,0:T(8,128)(2,1)S(1)}, bf16[352,128]{1,0:T(8,128)(2,1)S(1)}, u32[]{:S(2)}, u32[]{:S(2)}) collective-permute-start(bf16[352,128]{1,0:T(8,128)(2,1)S(1)} %get-tuple-element.11.msg_own_ref), channel_id=1, source_target_pairs={{0,8},{8,0},{16,24},{24,16},{1,9},{9,1},{17,25},{25,17},{2,10},{10... | collective-permute-start | bytes 270344 | tf_op jit(solution)/shard_map/ppermute | solution.py:519
  19.5 1.7 %shard_map.160.refs_4_ = f32[38,2,64,128]{3,2,1,0:T(8,128)S(1)} custom-call(f32[12,72,128]{2,1,0:T(8,128)S(1)} %get-tuple-element.13.dens_ref), custom_call_target="tpu_custom_call" | custom-call | flops 24903680 | bytes 2490368 | tf_op jit(solution)/shard_map/pallas_call | solution.py:521
  21.2 1.0 %collective-permute-done.7.refs_2_ = bf16[352,128]{1,0:T(8,128)(2,1)S(1)} collective-permute-done((bf16[352,128]{1,0:T(8,128)(2,1)S(1)}, bf16[352,128]{1,0:T(8,128)(2,1)S(1)}, u32[]{:S(2)}, u32[]{:S(2)}) %collective-permute-start.7) | collective-permute-done | bytes 90144 | tf_op jit(solution)/shard_map/ppermute | solution.py:519
  22.2 4.2 %collective-permute-done.6.refs_1_ = bf16[352,128]{1,0:T(8,128)(2,1)S(1)} collective-permute-done((bf16[352,128]{1,0:T(8,128)(2,1)S(1)}, bf16[352,128]{1,0:T(8,128)(2,1)S(1)}, u32[]{:S(2)}, u32[]{:S(2)}) %collective-permute-start.6) | collective-permute-done | bytes 90144 | tf_op jit(solution)/shard_map/ppermute | solution.py:519
  26.4 0.0 collective-permute-done.5.refs_0_
  26.5 6.8 %shard_map.161 = (f32[38,2,64,128]{3,2,1,0:T(8,128)}, f32[2,256]{1,0:T(2,128)}) custom-call(bf16[352,128]{1,0:T(8,128)(2,1)S(1)} %get-tuple-element.11.msg_own_ref, bf16[352,128]{1,0:T(8,128)(2,1)S(1)} %collective-permute-done.5.refs_0_, bf16[352,128]{1,0:T(8,128)(2,1)S(1)} %collective-permute-done.6.refs_1_, ...), custom_call_target="tpu_custom_call" | custom-call | tf_op jit(solution)/shard_map/pallas_call | solution.py:529
  (18 shorter events, 0.0 us)
Async XLA Ops:
  0.6 25.8 %copy-start.12 = (f32[1,512]{1,0:T(1,128)S(1)}, f32[1,512]{1,0:T(1,128)}, u32[]{:S(2)}) copy-start(f32[1,512]{1,0:T(1,128)} %constant.32.clone.refs_10_) | copy-start | bytes 6148
  0.6 25.8 %copy-start.14 = (f32[1,256]{1,0:T(1,128)S(1)}, f32[1,256]{1,0:T(1,128)}, u32[]{:S(2)}) copy-start(f32[1,256]{1,0:T(1,128)} %constant.31.clone.refs_9_) | copy-start | bytes 3076
  0.7 25.7 %copy-start.13 = (f32[1,384]{1,0:T(1,128)S(1)}, f32[1,384]{1,0:T(1,128)}, u32[]{:S(2)}) copy-start(f32[1,384]{1,0:T(1,128)} %constant.30.clone.refs_8_) | copy-start | bytes 4612
  0.7 25.7 %copy-start = (bf16[512,768]{1,0:T(8,128)(2,1)S(1)}, bf16[512,768]{1,0:T(8,128)(2,1)}, u32[]{:S(2)}) copy-start(bf16[512,768]{1,0:T(8,128)(2,1)} %constant.27.clone.refs_5_) | copy-start | bytes 2359300
  0.7 1.0 %copy-start.1 = (f32[2,2,64,128]{3,2,1,0:T(8,128)S(1)}, f32[2,2,64,128]{3,2,1,0:T(8,128)}, u32[]{:S(2)}) copy-start(f32[2,2,64,128]{3,2,1,0:T(8,128)} %jitter_ref.3) | copy-start | bytes 393220
  1.7 0.9 %copy-start.4 = (bf16[8,128,128]{2,1,0:T(8,128)(2,1)S(1)}, bf16[8,128,128]{2,1,0:T(8,128)(2,1)}, u32[]{:S(2)}) copy-start(bf16[8,128,128]{2,1,0:T(8,128)(2,1)} %constant.25.clone.take_col_ref) | copy-start | bytes 786436
  2.6 0.9 %copy-start.5 = (f32[8,64,128]{2,1,0:T(8,128)S(1)}, f32[8,64,128]{2,1,0:T(8,128)}, u32[]{:S(2)}) copy-start(f32[8,64,128]{2,1,0:T(8,128)} %constant.24.clone.take_row_ref) | copy-start | bytes 786436
  3.6 0.8 %copy-start.6 = (s32[2,64,128]{2,1,0:T(8,128)S(1)}, s32[2,64,128]{2,1,0:T(8,128)}, u32[]{:S(2)}) copy-start(s32[2,64,128]{2,1,0:T(8,128)} %labels_ref.3) | copy-start | bytes 196612
  4.4 0.8 %copy-start.10 = (s32[64,128]{1,0:T(8,128)S(1)}, s32[64,128]{1,0:T(8,128)}, u32[]{:S(2)}) copy-start(s32[64,128]{1,0:T(8,128)} %shells_ref.1) | copy-start | bytes 98308
  5.2 21.3 %copy-start.2 = (bf16[512,384]{1,0:T(8,128)(2,1)S(1)}, bf16[512,384]{1,0:T(8,128)(2,1)}, u32[]{:S(2)}) copy-start(bf16[512,384]{1,0:T(8,128)(2,1)} %constant.34.clone.refs_12_) | copy-start | bytes 1179652
  5.2 21.3 %copy-start.3 = (f32[144,512]{1,0:T(8,128)S(1)}, f32[144,512]{1,0:T(8,128)}, u32[]{:S(2)}) copy-start(f32[144,512]{1,0:T(8,128)} %constant.33.clone.refs_11_) | copy-start | bytes 884740
  5.2 21.3 %copy-start.7 = (f32[72,384]{1,0:T(8,128)S(1)}, f32[72,384]{1,0:T(8,128)}, u32[]{:S(2)}) copy-start(f32[72,384]{1,0:T(8,128)} %constant.29.clone.refs_7_) | copy-start | bytes 331780
  5.2 21.3 %copy-start.8 = (f32[72,384]{1,0:T(8,128)S(1)}, f32[72,384]{1,0:T(8,128)}, u32[]{:S(2)}) copy-start(f32[72,384]{1,0:T(8,128)} %constant.28.clone.refs_6_) | copy-start | bytes 331780
  5.3 8.6 %collective-permute-start.1 = (bf16[256,128]{1,0:T(8,128)(2,1)S(1)}, bf16[256,128]{1,0:T(8,128)(2,1)S(1)}, u32[]{:S(2)}, u32[]{:S(2)}) collective-permute-start(bf16[256,128]{1,0:T(8,128)(2,1)S(1)} %get-tuple-element.8), channel_id=1, source_target_pairs={{0,3},{1,2},{2,1},{3,0},{4,7},{5,6},{6,5},{7,4},{8,11},{9,10},{10,... | collective-permute-start | bytes 196616 | tf_op jit(solution)/shard_map/ppermute | solution.py:501
  7.8 6.1 %collective-permute-start = (bf16[256,128]{1,0:T(8,128)(2,1)S(1)}, bf16[256,128]{1,0:T(8,128)(2,1)S(1)}, u32[]{:S(2)}, u32[]{:S(2)}) collective-permute-start(bf16[256,128]{1,0:T(8,128)(2,1)S(1)} %get-tuple-element.8), channel_id=1, source_target_pairs={{0,1},{1,0},{2,3},{3,2},{4,5},{5,4},{6,7},{7,6},{8,9},{9,8},{10,11... | collective-permute-start | bytes 196616 | tf_op jit(solution)/shard_map/ppermute | solution.py:501
  8.4 5.5 %collective-permute-start.2 = (bf16[160,128]{1,0:T(8,128)(2,1)S(1)}, bf16[160,128]{1,0:T(8,128)(2,1)S(1)}, u32[]{:S(2)}, u32[]{:S(2)}) collective-permute-start(bf16[160,128]{1,0:T(8,128)(2,1)S(1)} %get-tuple-element.9.refs_2_), channel_id=1, source_target_pairs={{0,4},{4,0},{1,5},{5,1},{2,6},{6,2},{3,7},{7,3},{8,12},{12,8},{9,1... | collective-permute-start | bytes 122888 | tf_op jit(solution)/shard_map/ppermute | solution.py:502
  10.0 3.9 %collective-permute-start.4 = (bf16[16,128]{1,0:T(8,128)(2,1)S(1)}, bf16[16,128]{1,0:T(8,128)(2,1)S(1)}, u32[]{:S(2)}, u32[]{:S(2)}) collective-permute-start(bf16[16,128]{1,0:T(8,128)(2,1)S(1)} %get-tuple-element.10), channel_id=1, source_target_pairs={{0,7},{1,6},{2,5},{3,4},{4,3},{5,2},{6,1},{7,0},{8,15},{9,14},{10,... | collective-permute-start | bytes 12296 | tf_op jit(solution)/shard_map/ppermute | solution.py:504
  10.0 3.9 %collective-permute-start.3 = (bf16[16,128]{1,0:T(8,128)(2,1)S(1)}, bf16[16,128]{1,0:T(8,128)(2,1)S(1)}, u32[]{:S(2)}, u32[]{:S(2)}) collective-permute-start(bf16[16,128]{1,0:T(8,128)(2,1)S(1)} %get-tuple-element.10), channel_id=1, source_target_pairs={{0,5},{1,4},{2,7},{3,6},{4,1},{5,0},{6,3},{7,2},{8,13},{9,12},{10,... | collective-permute-start | bytes 12296 | tf_op jit(solution)/shard_map/ppermute | solution.py:504
  13.9 0.8 %copy-start.9 = (bf16[2,128,64]{2,1,0:T(8,128)(2,1)S(1)}, bf16[2,128,64]{2,1,0:T(8,128)(2,1)}, u32[]{:S(2)}) copy-start(bf16[2,128,64]{2,1,0:T(8,128)(2,1)} %constant.26.clone.refs_6_) | copy-start | bytes 98308
  14.8 11.7 %copy-start.11 = (f32[16,256]{1,0:T(8,128)S(1)}, f32[16,256]{1,0:T(8,128)}, u32[]{:S(2)}) copy-start(f32[16,256]{1,0:T(8,128)} %constant.35.clone.refs_13_) | copy-start | bytes 49156
  15.0 7.2 %collective-permute-start.7 = (bf16[352,128]{1,0:T(8,128)(2,1)S(1)}, bf16[352,128]{1,0:T(8,128)(2,1)S(1)}, u32[]{:S(2)}, u32[]{:S(2)}) collective-permute-start(bf16[352,128]{1,0:T(8,128)(2,1)S(1)} %get-tuple-element.11.msg_own_ref), channel_id=1, source_target_pairs={{0,24},{8,16},{16,8},{24,0},{1,25},{9,17},{17,9},{25,1},{2,26},{10... | collective-permute-start | bytes 270344 | tf_op jit(solution)/shard_map/ppermute | solution.py:519
  18.7 7.7 %collective-permute-start.6 = (bf16[352,128]{1,0:T(8,128)(2,1)S(1)}, bf16[352,128]{1,0:T(8,128)(2,1)S(1)}, u32[]{:S(2)}, u32[]{:S(2)}) collective-permute-start(bf16[352,128]{1,0:T(8,128)(2,1)S(1)} %get-tuple-element.11.msg_own_ref), channel_id=1, source_target_pairs={{0,16},{8,24},{16,0},{24,8},{1,17},{9,25},{17,1},{25,9},{2,18},{10... | collective-permute-start | bytes 270344 | tf_op jit(solution)/shard_map/ppermute | solution.py:519
  18.7 7.7 %collective-permute-start.5 = (bf16[352,128]{1,0:T(8,128)(2,1)S(1)}, bf16[352,128]{1,0:T(8,128)(2,1)S(1)}, u32[]{:S(2)}, u32[]{:S(2)}) collective-permute-start(bf16[352,128]{1,0:T(8,128)(2,1)S(1)} %get-tuple-element.11.msg_own_ref), channel_id=1, source_target_pairs={{0,8},{8,0},{16,24},{24,16},{1,9},{9,1},{17,25},{25,17},{2,10},{10... | collective-permute-start | bytes 270344 | tf_op jit(solution)/shard_map/ppermute | solution.py:519

commit v2 on v1

v2 whole, which is shorter than its diff:
```python
import functools
import math

import jax
import jax.numpy as jnp
import ml_dtypes
import numpy as np
from jax import lax
from jax.experimental import pallas as pl
from jax.experimental.pallas import tpu as pltpu
from jax.sharding import PartitionSpec as P

NSHELL = 256
UNUSED = -(1 << 20)
TOP = 40
ROWS = 72
F32 = jnp.float32
BF16 = jnp.bfloat16

LATTICE = (
    (0, 0, 0),
    (1, 0, 0),
    (-1, 0, 0),
    (0, 1, 0),
    (0, -1, 0),
    (0, 0, 1),
    (0, 0, -1),
    (1, 1, 0),
    (-1, -1, 0),
    (1, -1, 0),
    (-1, 1, 0),
    (1, 0, 1),
    (-1, 0, -1),
    (1, 0, -1),
    (-1, 0, 1),
    (0, 1, 1),
    (0, -1, -1),
    (0, 1, -1),
    (0, -1, 1),
)
WEIGHTS = (1.0 / 3.0,) + (1.0 / 18.0,) * 6 + (1.0 / 36.0,) * 12


def xor_pairs(count, bits):
    return [(i, i ^ bits) for i in range(count)]


def shift_pairs(count, step):
    return [(i, (i + step) % count) for i in range(count)]


def ring_moves(count):
    if count == 2:
        return [xor_pairs(2, 1)]
    if count == 4:
        return [xor_pairs(4, 1), xor_pairs(4, 3)]
    return [shift_pairs(count, 1), shift_pairs(count, -1)]


def ring_pick(count, index):
    if count == 2:
        return 0, 0
    if count == 4:
        odd = lax.rem(index, 2)
        return 1 - odd, odd
    return 0, 1


def pair_product(first, second, count_second):
    return [
        (a * count_second + b, c * count_second + d) for a, c in first for b, d in second
    ]


def whole(rows):
    return 16 * (-(-rows // 16))


def choose(items, which):
    if isinstance(which, int):
        return items[which]
    value = items[0]
    for number in range(1, len(items)):
        value = jnp.where(which == number, items[number], value)
    return value


def bf16_table(values):
    return np.asarray(values, np.float32).astype(ml_dtypes.bfloat16)


def angle_table(freq, pos, full):
    step = np.float32(2.0 * math.pi / full)
    return ((freq * pos) % full).astype(np.float32) * step


@functools.lru_cache(maxsize=None)
def make_tables(full_x, full_y, n_row, n_sec, wx, wy):
    half_x, half_y = full_x // 2, full_y // 2
    lanes = half_y + 128
    freq_y = np.arange(lanes)[None, :]
    angles = angle_table(np.arange(full_y)[:, None], freq_y, full_y)
    live = freq_y <= half_y
    table_y = np.concatenate([np.cos(angles) * live, np.sin(angles) * live], 1)
    hrows = half_x + 8
    radius = np.arange(hrows)[:, None] ** 2 + np.arange(lanes)[None, :] ** 2
    base = np.minimum(np.floor(np.sqrt(radius.astype(np.float64))).astype(np.int64), NSHELL - 1)
    valid = (np.arange(hrows)[:, None] <= half_x) & (np.arange(lanes)[None, :] <= half_y)
    move = np.where(valid, base - np.arange(lanes)[None, :], UNUSED)
    mult_y = np.where(freq_y > half_y, 0, np.where((freq_y == 0) | (freq_y == half_y), 1, 2))
    signed_x = np.arange(full_x)
    signed_x = np.where(signed_x < half_x, signed_x, signed_x - full_x)
    signed_y = np.arange(full_y)
    signed_y = np.where(signed_y < half_y, signed_y, signed_y - full_y)
    square = signed_x[:, None] ** 2 + signed_y[None, :] ** 2
    root = np.floor(np.sqrt(square + 1.0) + 1e-9).astype(np.int64)
    special = (root * root == square + 1) & (root < NSHELL) & (square > 0)
    low_label = np.minimum(np.floor(np.sqrt(square.astype(np.float64))), NSHELL - 1)
    counts = np.bincount(low_label.astype(np.int64).ravel(), minlength=NSHELL)
    rank = np.zeros(special.shape, np.int64)
    for r in range(n_row):
        rows = special[r * wx : (r + 1) * wx]
        rank[r * wx : (r + 1) * wx] = np.cumsum(rows, axis=0) - rows
    per = int(rank[special].max()) + 1
    section = 8 * (-(-(n_row * per) // 8))
    total = 128 * (-(-int(special.sum()) // 128))
    put = np.zeros((n_row * per, total))
    lanes_of = np.zeros((total, full_y))
    mark_row = np.zeros((2, hrows, total))
    mark_col = np.zeros((lanes, total))
    step = np.zeros((total, NSHELL))
    for entry, (kx, ky) in enumerate(np.argwhere(special).tolist()):
        ax, ay = abs(int(signed_x[kx])), abs(int(signed_y[ky]))
        same = int(signed_x[kx]) * int(signed_y[ky]) >= 0 or ax == half_x or ay == half_y
        put[kx // wx * per + rank[kx, ky], entry] = 1
        lanes_of[entry, ky] = 1
        mark_row[0 if same else 1, ax, entry] = 1
        mark_col[ay, entry] = 1
        step[entry, root[kx, ky]] += 1
        step[entry, root[kx, ky] - 1] -= 1
    return dict(
        per=per,
        section=section,
        table_y=bf16_table(table_y),
        move=move,
        mult_y=mult_y.astype(np.float32),
        counts=counts.astype(np.float32)[None, :],
        put=np.asarray(put, np.float32),
        lanes_of=bf16_table(lanes_of.T),
        mark_row=np.asarray(mark_row, np.float32),
        mark_col=bf16_table(mark_col),
        step=np.asarray(step, np.float32),
    )


def x_table(n_row, wx):
    full_x = n_row * wx
    half_x = full_x // 2
    freq = lax.broadcasted_iota(jnp.int32, (n_row, full_x, wx), 1)
    block = lax.broadcasted_iota(jnp.int32, (n_row, full_x, wx), 0) ^ lax.axis_index("row")
    pos = block * wx + lax.broadcasted_iota(jnp.int32, (n_row, full_x, wx), 2)
    is_cos = freq <= half_x
    freq = jnp.where(is_cos, freq, freq - half_x)
    angles = (freq * pos % full_x).astype(F32) * (2.0 * math.pi / full_x)
    return jnp.where(is_cos, jnp.cos(angles), -jnp.sin(angles)).astype(BF16)


def pack_kernel(n_row, n_sec, per, own_ref, shells_ref, col_ref, row_ref, edge_ref):
    _, depth, wx, wy = own_ref.shape
    edges = []
    densities = [[own_ref[c, z] for z in range(depth)] for c in range(2)]
    for c in range(2):
        for z in range(depth):
            tile = densities[c][z]
            at = (c * depth + z) * wx
            col_ref[at : at + wx] = tile.astype(BF16)
            edges += [tile[0:2], tile[wx - 2 : wx]]
    for z in range(depth):
        row_ref[z * wx : (z + 1) * wx] = (densities[0][z] - densities[1][z]).astype(BF16)
    edge = jnp.concatenate(edges, axis=0).astype(BF16)
    edge_ref[...] = edge
    at = depth * wx
    count = edge.shape[0]
    row_ref[at : at + count] = edge

    row, sec = lax.axis_index("row"), lax.axis_index("sec")
    square, root = shell_root(row * wx, sec * wy, wx * n_row, wy * n_sec, wx, wy)
    special = (root * root == square + 1.0) & (root < NSHELL) & (square > 0.0)
    nudge = jnp.where(special, shells_ref[...].astype(F32) - (root - 1.0), 0.0)
    one = jnp.where(special, F32(1.0), F32(0.0)).astype(BF16)
    down = lax.broadcasted_iota(jnp.int32, (wx, wx), 0)
    above = (lax.broadcasted_iota(jnp.int32, (wx, wx), 1) < down).astype(F32).astype(BF16)
    rank = jnp.dot(above, one, preferred_element_type=F32)
    section = row_ref.shape[0] - at - count
    line = lax.broadcasted_iota(jnp.int32, (section, wy), 0)
    marks = jnp.zeros((section, wy), F32)
    for number in range(per):
        found = jnp.sum(jnp.where(rank == number, nudge, 0.0), axis=0, keepdims=True)
        marks = jnp.where(line == row * per + number, found, marks)
    row_ref[at + count :] = marks.astype(BF16)


def shell_root(first_x, first_y, full_x, full_y, wx, wy):
    kx = first_x + lax.broadcasted_iota(jnp.int32, (wx, wy), 0)
    ky = first_y + lax.broadcasted_iota(jnp.int32, (wx, wy), 1)
    kx = jnp.where(kx < full_x // 2, kx, kx - full_x)
    ky = jnp.where(ky < full_y // 2, ky, ky - full_y)
    square = (kx * kx + ky * ky).astype(F32)
    return square, jnp.floor(jnp.sqrt(square + 1.0) + 0.5)


def middle_kernel(n_row, n_col, section, own_ref, *refs):
    _, depth, wx, wy = own_ref.shape
    col_moves, row_moves = len(ring_moves(n_col)), len(ring_moves(n_row))
    col_refs, refs = refs[:col_moves], refs[col_moves:]
    row_refs, refs = refs[:n_row], refs[n_row:]
    diag_refs, refs = refs[: col_moves * row_moves], refs[col_moves * row_moves :]
    table_ref, msg_ref, short_ref, dens_ref, lanes_ref = refs
    row, col = lax.axis_index("row"), lax.axis_index("col")
    full_x = table_ref.shape[1]

    for z in range(depth):
        half = None
        for k in range(n_row):
            part = jnp.dot(
                table_ref[k],
                row_refs[k][z * wx : (z + 1) * wx],
                preferred_element_type=F32,
            )
            half = part if half is None else half + part
        half = half.astype(BF16)
        msg_ref[z * full_x : (z + 1) * full_x] = half
        short_ref[z * full_x : (z + 1) * full_x] = half

    at = depth * wx
    count = 8 * depth
    marks = sum(ref[at + count :].astype(F32) for ref in row_refs)[:section]

    col_prev, col_next = ring_pick(n_col, col)
    before = choose([r[...] for r in col_refs], col_prev).astype(F32)
    after = choose([r[...] for r in col_refs], col_next).astype(F32)
    edge_list = [r[at : at + count].astype(F32) for r in row_refs]
    edge_prev = choose(edge_list, row ^ lax.rem(row + n_row - 1, n_row)) if n_row > 2 else edge_list[1]
    edge_next = choose(edge_list, row ^ lax.rem(row + 1, n_row)) if n_row > 2 else edge_list[1]
    row_prev, row_next = ring_pick(n_row, row)
    diag = [r[...].astype(F32) for r in diag_refs]

    def diag_of(row_which, col_which):
        lines = [
            choose(diag[m * col_moves : (m + 1) * col_moves], col_which) for m in range(row_moves)
        ]
        return choose(lines, row_which)

    corner = {
        (0, -1): diag_of(row_prev, col_prev),
        (0, 1): diag_of(row_prev, col_next),
        (1, -1): diag_of(row_next, col_prev),
        (1, 1): diag_of(row_next, col_next),
    }
    lane = lax.broadcasted_iota(jnp.int32, (ROWS, wy), 1)
    gap = jnp.zeros((ROWS - wx - 4, wy), F32)
    strips = jnp.zeros((ROWS, wy), F32)
    layers = depth + 4
    for c in range(2):
        for layer in range(layers):
            z = layer - 2
            if z < 0:
                source, plane, low, high = before, depth + z, corner[0, -1], corner[1, -1]
            elif z >= depth:
                source, plane, low, high = after, z - depth, corner[0, 1], corner[1, 1]
            else:
                source, plane, low, high = None, z, edge_prev, edge_next
            where = c * depth + plane
            if source is None:
                body = own_ref[c, plane]
            else:
                body = source[where * wx : (where + 1) * wx]
            tail = jnp.concatenate(
                [high[where * 4 : where * 4 + 2], gap, low[where * 4 + 2 : where * 4 + 4]], axis=0
            )
            tile = jnp.concatenate([body, tail], axis=0)
            group = c * layers + layer
            dens_ref[group] = tile
            at_lane = 8 * group
            moved = pltpu.roll(tile, (at_lane + 2) % wy, 1)
            strips = jnp.where((lane >= at_lane) & (lane < at_lane + 4), moved, strips)
    lanes_ref[...] = strips + pltpu.roll(strips, 4, 1)
    at = depth * full_x
    lower = jnp.concatenate([strips[TOP:], jnp.zeros((2 * TOP - ROWS, wy), F32)], axis=0)
    folded = strips[:TOP] + pltpu.roll(lower, 4, 1)
    for ref, parts in ((msg_ref, [marks, folded]), (short_ref, [marks])):
        missing = ref.shape[0] - at - sum(p.shape[0] for p in parts)
        if missing:
            parts = parts + [jnp.zeros((missing, wy), F32)]
        ref[at:] = jnp.concatenate(parts, axis=0).astype(BF16)


def turn(tile, shift, axis):
    shift = shift % tile.shape[axis]
    return tile if shift == 0 else pltpu.roll(tile, shift, axis)


def pull_of(below, here, above):
    around = below + above
    line_y = turn(here, -1, 1) + turn(here, 1, 1)
    line_x = turn(here, -1, 0) + turn(here, 1, 0)
    flat = 2.0 * here + around
    mix = flat + line_y
    pull_x = turn(mix, -1, 0) - turn(mix, 1, 0)
    mix = flat + line_x
    pull_y = turn(mix, -1, 1) - turn(mix, 1, 1)
    gap = above - below
    pull_z = 2.0 * gap + turn(gap, -1, 0) + turn(gap, 1, 0) + turn(gap, -1, 1) + turn(gap, 1, 1)
    return pull_x, pull_y, pull_z


def relax_terms(density, velocity):
    vx, vy, vz = velocity
    squared = vx * vx + vy * vy + vz * vz
    rest = density * (1.0 - 1.875 * squared)
    terms = [WEIGHTS[0] * rest]
    for number in range(1, 19, 2):
        offsets = LATTICE[number]
        projected = None
        for axis in range(3):
            if offsets[axis]:
                part = velocity[axis] if offsets[axis] > 0 else -velocity[axis]
                projected = part if projected is None else projected + part
        weighted = density * projected
        even = WEIGHTS[number] * (rest + 5.625 * (weighted * projected))
        odd = (WEIGHTS[number] * 3.75) * weighted
        terms += [even + odd, even - odd]
    return terms


def cells_kernel(dens_ref, out_ref):
    _, depth, wx, _ = out_ref.shape
    layers = depth + 4
    scale = -1.6 / 36.0
    for layer in range(1, layers - 1):
        for c in range(2):
            other = (1 - c) * layers + layer
            pulls = pull_of(dens_ref[other - 1], dens_ref[other], dens_ref[other + 1])
            velocity = [scale * p for p in pulls]
            terms = relax_terms(dens_ref[c * layers + layer], velocity)
            for number in range(19):
                cx, cy, cz = LATTICE[number]
                z = layer - 2 + cz
                if 0 <= z < depth:
                    tile = turn(turn(terms[number], cx, 0), cy, 1)
                    out_ref[c * 19 + number, z] = tile[:wx]


def set_ends(n_sec, start, at, msg_refs, lanes_ref, cells_ref, out_hbm, out_ref, sems):
    _, depth, wx, wy = out_ref.shape
    layers = depth + 4
    strips = [r[start:].astype(F32)[at - start :][:TOP] for r in msg_refs]
    index = lax.axis_index("sec")
    prev_which, next_which = ring_pick(n_sec, index)
    before, after = choose(strips, prev_which), choose(strips, next_which)
    rest = ROWS - TOP
    before = jnp.concatenate([before, turn(before, -4, 1)[:rest]], axis=0)
    after = jnp.concatenate([turn(after, 4, 1), after[:rest]], axis=0)
    place = lax.rem(lax.broadcasted_iota(jnp.int32, (ROWS, wy), 1), 8)
    tile = jnp.where(place < 2, before, jnp.where(place >= 6, after, lanes_ref[...]))
    pulls = pull_of(turn(tile, 8, 1), tile, turn(tile, -8, 1))
    span = 8 * layers
    first = lax.broadcasted_iota(jnp.int32, (ROWS, wy), 1) < span
    scale = -1.6 / 36.0
    velocity = [scale * jnp.where(first, turn(p, -span, 1), turn(p, span, 1)) for p in pulls]
    terms = relax_terms(tile, velocity)
    lane = lax.broadcasted_iota(jnp.int32, (wx, wy), 1)
    copies = []
    for number in range(19):
        cx, cy, cz = LATTICE[number]
        term = turn(terms[number], cx, 0)[:wx]
        if cy == 0:
            term = jnp.where(place[:wx] == 1, turn(term, -4, 1), term)
            mask = (lane == 0) | (lane == wy - 1)
        else:
            mask = lane < 2 if cy > 0 else lane >= wy - 2
        for c in range(2):
            for z in range(depth):
                group = 8 * (c * layers + 2 + z - cz)
                back = {1: group + 1, -1: group + 5 - (wy - 2), 0: group + 2}[cy]
                q = c * 19 + number
                out_ref[q, z] = jnp.where(mask, turn(term, -back, 1), cells_ref[q, z])
            copy = pltpu.make_async_copy(out_ref.at[q], out_hbm.at[q], sems.at[q])
            copy.start()
            copies.append(copy)
    return copies


def final_kernel(n_sec, section, move, msg_own_ref, *refs):
    msg_refs = [msg_own_ref] + list(refs[: n_sec - 1])
    strips_ref, cells_ref = refs[n_sec - 1 : n_sec + 1]
    refs = refs[n_sec + 1 :]
    (table_ref, move_ref, mult_ref, counts_ref, put_ref, lanes_ref, row_ref, col_ref, step_ref,
     out_hbm, spec_ref, lhs_ref, mark_ref, part_ref, out_ref, sems) = refs
    depth = spec_ref.shape[0]
    sec = lax.axis_index("sec")
    full_y, lanes = table_ref.shape[0], table_ref.shape[1] // 2
    wy = full_y // n_sec
    full_x = lhs_ref.shape[0] // depth
    half_x = full_x // 2
    hrows = half_x + 8
    at = depth * full_x
    lines_used = put_ref.shape[0]
    ring = [msg_refs[move_[0][1]] for move_ in ring_moves(n_sec)]
    copies = set_ends(n_sec, at, at + section, ring, strips_ref, cells_ref, out_hbm, out_ref, sems)

    for k in range(n_sec):
        start = pl.multiple_of((sec ^ k) * wy, wy)
        lhs_ref[:, pl.ds(start, wy)] = msg_refs[k][:at]
        mark_ref[:, pl.ds(start, wy)] = msg_refs[k][at : at + mark_ref.shape[0]]
    transform = jnp.dot(lhs_ref[...], table_ref[...], preferred_element_type=F32)

    found = jnp.dot(mark_ref[...], lanes_ref[...], preferred_element_type=F32)
    nudge = jnp.sum(found[:lines_used] * put_ref[...], axis=0, keepdims=True)

    mult = mult_ref[...]
    row_zero = lax.broadcasted_iota(jnp.int32, (half_x, lanes), 0) == 0
    rest = jnp.zeros((7, lanes), F32)
    picks = []
    for z in range(depth):
        real = transform[z * full_x : z * full_x + half_x]
        imag = transform[z * full_x + half_x : (z + 1) * full_x]
        rc, rs = real[:, :lanes], real[:, lanes:]
        ic, is_ = imag[:, :lanes], imag[:, lanes:]
        top = rc * rc + rs * rs
        low = ic * ic + is_ * is_
        both = top + low
        cross = 2.0 * (rc * is_ - ic * rs)
        part_ref[z, :half_x] = mult * jnp.where(row_zero, top, 2.0 * both)
        part_ref[z, half_x:] = jnp.concatenate([mult * low[0:1], rest], axis=0)
        plus = jnp.concatenate([jnp.where(row_zero, top, both + cross), low[0:1], rest], axis=0)
        minus = jnp.concatenate([both - cross, low[0:1], rest], axis=0)
        value = 0.0
        for number, power in enumerate((plus, minus)):
            head = power.astype(BF16)
            tail = (power - head.astype(F32)).astype(BF16)
            found = jnp.dot(head, col_ref[...], preferred_element_type=F32) + jnp.dot(
                tail, col_ref[...], preferred_element_type=F32
            )
            value = value + jnp.sum(found * row_ref[number], axis=0, keepdims=True)
        picks.append(value)
    picks.append(jnp.ones_like(picks[0]))
    picks.append(jnp.zeros((8 - len(picks), picks[0].shape[1]), F32))
    moved = lax.dot_general(
        jnp.concatenate(picks, axis=0) * nudge, step_ref[...], (((1,), (0,)), ((), ())),
        precision=lax.Precision.HIGHEST, preferred_element_type=F32,
    )

    tiles = NSHELL // 128
    lane = lax.broadcasted_iota(jnp.int32, (8, 128), 1)
    sums = [[jnp.zeros((8, 128), F32) for _ in range(tiles)] for _ in range(depth)]
    for tile in range(lanes // 128):
        block = move[:, tile * 128 : (tile + 1) * 128]
        at_lanes = slice(tile * 128, (tile + 1) * 128)
        for value in np.unique(block):
            if value == UNUSED:
                continue
            value = int(value)
            totals = [None] * depth
            for group in range(hrows // 8):
                if not (block[group * 8 : group * 8 + 8] == value).any():
                    continue
                rows = slice(group * 8, group * 8 + 8)
                same = move_ref[rows, at_lanes] == value
                for z in range(depth):
                    term = jnp.where(same, part_ref[z, rows, at_lanes], 0.0)
                    totals[z] = term if totals[z] is None else totals[z] + term
            shift = value % 128
            goal = tile + value // 128
            for z in range(depth):
                total = turn(totals[z], shift, 1)
                if 0 <= goal < tiles:
                    sums[z][goal] += jnp.where(lane >= shift, total, 0.0)
                if shift and 0 <= goal + 1 < tiles:
                    sums[z][goal + 1] += jnp.where(lane < shift, total, 0.0)
    norm = (counts_ref[...] + moved[depth : depth + 1]) * float(full_x * full_y)
    lines = []
    for z in range(depth):
        line = jnp.sum(jnp.concatenate(sums[z], axis=1), axis=0, keepdims=True)
        lines.append((line + moved[z : z + 1]) / norm)
    spec_ref[...] = jnp.concatenate(lines, axis=0)
    for copy in copies:
        copy.wait()


def call(kernel, outs, scratch=(), flops=0, moved=0, limit=48 << 20, **specs):
    return pl.pallas_call(
        kernel,
        out_shape=outs,
        scratch_shapes=list(scratch),
        compiler_params=pltpu.CompilerParams(vmem_limit_bytes=limit),
        cost_estimate=pl.CostEstimate(flops=flops, bytes_accessed=moved, transcendentals=0),
        **specs,
    )


def on_device(n_sec, n_row, n_col, labels, jitter, shells):
    depth, wx, wy = labels.shape
    full_x, full_y = wx * n_row, wy * n_sec
    tables = make_tables(full_x, full_y, n_row, n_sec, wx, wy)
    per, section = tables["per"], tables["section"]
    layers = depth + 4
    count = 8 * depth
    shape = jax.ShapeDtypeStruct

    other = lax.broadcasted_iota(jnp.int32, jitter.shape, 0)
    own = jnp.where((labels[None] ^ other) == 1, F32(1.0), F32(0.2)) * jitter
    col_msg, row_msg, edge_msg = call(
        functools.partial(pack_kernel, n_row, n_sec, per),
        [
            shape((2 * depth * wx, wy), BF16),
            shape((depth * wx + count + whole(section), wy), BF16),
            shape((count, wy), BF16),
        ],
    )(own, shells)

    col_got = [lax.ppermute(col_msg, "col", m) for m in ring_moves(n_col)]
    row_got = [lax.ppermute(row_msg, "row", xor_pairs(n_row, k)) for k in range(1, n_row)]
    diag_got = [
        lax.ppermute(edge_msg, ("row", "col"), pair_product(a, b, n_col))
        for a in ring_moves(n_row)
        for b in ring_moves(n_col)
    ]

    at = depth * full_x
    msg, short, dens, lanes_own = call(
        functools.partial(middle_kernel, n_row, n_col, section),
        [
            shape((at + whole(section + TOP), wy), BF16),
            shape((at + whole(section), wy), BF16),
            shape((2 * layers, ROWS, wy), F32),
            shape((ROWS, wy), F32),
        ],
    )(own, *col_got, row_msg, *row_got, *diag_got, x_table(n_row, wx))

    ring = ring_moves(n_sec)
    sec_got = []
    for k in range(1, n_sec):
        move = xor_pairs(n_sec, k)
        sec_got.append(lax.ppermute(msg if move in ring else short, "sec", move))

    cells = call(
        cells_kernel,
        shape((38, depth, wx, wy), F32),
        flops=38 * depth * wx * wy * 40,
        moved=4 * 38 * depth * wx * wy,
    )(dens)

    hrows, lanes = full_x // 2 + 8, full_y // 2 + 128
    names = ("mult_y", "counts", "put", "lanes_of", "mark_row", "mark_col", "step")
    return call(
        functools.partial(final_kernel, n_sec, section, tables["move"]),
        (shape((38, depth, wx, wy), F32), shape((depth, NSHELL), F32)),
        [
            pltpu.VMEM((depth * full_x, full_y), BF16),
            pltpu.VMEM((whole(section), full_y), BF16),
            pltpu.VMEM((depth, hrows, lanes), F32),
            pltpu.VMEM((38, depth, wx, wy), F32),
            pltpu.SemaphoreType.DMA((38,)),
        ],
        out_specs=(
            pl.BlockSpec(memory_space=pltpu.HBM),
            pl.BlockSpec(memory_space=pltpu.VMEM),
        ),
    )(msg, *sec_got, lanes_own, cells, tables["table_y"], tables["move"].astype(np.int32),
      *[tables[name] for name in names])


def solution(mesh):
    in_specs = (P("col", "row", "sec"), P(None, "col", "row", "sec"), P("row", "sec"))
    out_specs = (P(None, "col", "row", "sec"), P("col", None))
    sizes = [mesh.shape[name] for name in ("sec", "row", "col")]
    return jax.shard_map(
        functools.partial(on_device, *sizes),
        mesh=mesh,
        in_specs=in_specs,
        out_specs=out_specs,
        check_vma=False,
    )
```

time: 33.7 us -> 24.8 us (0.74)
  local copies, waits for them, and re-layouts: 5.35 us -> 0.81 us
  Pallas kernels: 8.95 us -> 5.42 us
  waiting for transfers between devices: 7.46 us -> 4.98 us
  other arithmetic: 0 us -> 1.67 us
    unnamed x30 -> x20, local copies, waits for them, and re-layouts: 5.35 us -> 0.81 us
    pallas_call x3, Pallas kernels: 7.25 us -> 3.72 us  [the longest x1 3.29 us: on_device(): call(functools.partial(final_kernel, n_sec, section, tables['move']), (sh...]
    ppermute x2, starting transfers between devices: 3.11 us -> 0.14 us  [on_device(): col_got = [lax.ppermute(col_msg, 'col', m) for m in ring_moves(n_col)]]
    ppermute x2, starting transfers between devices: 1.72 us -> 4.18 us  [on_device(): lax.ppermute(edge_msg, ('row', 'col'), pair_product(a, b, n_col))]
    ppermute x2, waiting for transfers between devices: 2.22 us -> 0.01 us  [on_device(): lax.ppermute(edge_msg, ('row', 'col'), pair_product(a, b, n_col))]
    ppermute x3, waiting for transfers between devices: 5.24 us -> 3.5 us  [on_device(): sec_got.append(lax.ppermute(msg if move in ring else short, 'sec', move))]
    ppermute x1, waiting for transfers between devices: 0.01 us -> 1.31 us  [on_device(): lax.ppermute(row_msg, 'row', xor_pairs(n_row, k))]
    mul x0 -> x2, other arithmetic: none -> 1.03 us  [the longest x1 1.03 us: on_device(): own = jnp.where(labels[None] ^ other == 1, F32(1.0), F32(0.2)) * jitter]
  transfers between devices with their start and end apart: 8 -> 8, of which waited for: 3 -> 3; matrix products, arithmetic and copies ran while one was open for 0% -> 3% of each run, Pallas kernels for 5% -> 7%
where the time goes in v2:
time: 24.8 us; the launch traced here: 24.6 us
  starting transfers between devices  11 us (44%)
  Pallas kernels  5.42 us (22%)
  waiting for transfers between devices  4.98 us (20%)
  other arithmetic  1.67 us (7%)
  local copies, waits for them, and re-layouts  0.81 us (3%)
  between operations  0.79 us (3%)
    ppermute x3, starting transfers between devices, on_device(): sec_got.append(lax.ppermute(msg if move in ring else short, 'sec', move))  4.62 us
    ppermute x2, starting transfers between devices, on_device(): lax.ppermute(edge_msg, ('row', 'col'), pair_product(a, b, n_col))  4.18 us
    ppermute x3, waiting for transfers between devices, on_device(): sec_got.append(lax.ppermute(msg if move in ring else short, 'sec', move))  3.5 us
    pallas_call x1, Pallas kernels, on_device(): call(functools.partial(final_kernel, n_sec, section, tables['move']), (sh...  3.29 us
    ppermute x1, starting transfers between devices, on_device(): lax.ppermute(row_msg, 'row', xor_pairs(n_row, k))  2.03 us
    pallas_call x1, Pallas kernels, on_device(): call(cells_kernel, shape((38, depth, wx, wy), F32), flops=38 * depth * wx...  1.7 us
    ppermute x1, waiting for transfers between devices, on_device(): lax.ppermute(row_msg, 'row', xor_pairs(n_row, k))  1.31 us
    mul x1, other arithmetic, on_device(): own = jnp.where(labels[None] ^ other == 1, F32(1.0), F32(0.2)) * jitter  1.03 us
  transfers between devices with their start and end apart: 8, of which 3 were waited for; matrix products, arithmetic and copies ran while one was open for 3% of the time, Pallas kernels for 7%

profile of v2, /device:TPU:0, one launch (start us, length us, event | category | flops | bytes accessed | tf_op | source)
XLA Modules:
  0.0 24.6 jit_solution(11930238420360251119)
XLA Ops:
  0.6 0.0 copy-start.1
  0.6 0.0 copy-start.4
  0.7 0.0 copy-start.5
  0.7 0.0 copy-start.2
  0.7 0.0 copy-start.3
  0.7 0.0 copy-start
  0.7 1.0 %select_multiply_fusion.own_ref = f32[2,2,64,128]{3,2,1,0:T(8,128)S(1)} fusion(f32[2,2,64,128]{3,2,1,0:T(8,128)} %param.13, s32[2,64,128]{2,1,0:T(8,128)} %param.12), kind=kLoop, calls=%fused_computation.7 | loop fusion | flops 131072 | bytes 327680 | tf_op jit(solution)/shard_map/mul | solution.py:512
  1.7 0.0 copy-start.6
  1.7 0.7 %copy-done.6 = s32[64,128]{1,0:T(8,128)S(1)} copy-done((s32[64,128]{1,0:T(8,128)S(1)}, s32[64,128]{1,0:T(8,128)}, u32[]{:S(2)}) %copy-start.6) | copy-done | bytes 32792
  2.5 0.2 shard_map.131
  2.7 3.4 %collective-permute-start.4 = (bf16[16,128]{1,0:T(8,128)(2,1)S(1)}, bf16[16,128]{1,0:T(8,128)(2,1)S(1)}, u32[]{:S(2)}, u32[]{:S(2)}) collective-permute-start(bf16[16,128]{1,0:T(8,128)(2,1)S(1)} %get-tuple-element.11), channel_id=1, source_target_pairs={{0,7},{1,6},{2,5},{3,4},{4,3},{5,2},{6,1},{7,0},{8,15},{9,14},{10,... | collective-permute-start | bytes 12296 | tf_op jit(solution)/shard_map/ppermute | solution.py:525
  6.1 0.8 %collective-permute-start.3 = (bf16[16,128]{1,0:T(8,128)(2,1)S(1)}, bf16[16,128]{1,0:T(8,128)(2,1)S(1)}, u32[]{:S(2)}, u32[]{:S(2)}) collective-permute-start(bf16[16,128]{1,0:T(8,128)(2,1)S(1)} %get-tuple-element.11), channel_id=1, source_target_pairs={{0,5},{1,4},{2,7},{3,6},{4,1},{5,0},{6,3},{7,2},{8,13},{9,12},{10,... | collective-permute-start | bytes 12296 | tf_op jit(solution)/shard_map/ppermute | solution.py:525
  6.9 0.1 collective-permute-start.1
  7.0 0.0 collective-permute-start
  7.0 2.0 %collective-permute-start.2 = (bf16[160,128]{1,0:T(8,128)(2,1)S(1)}, bf16[160,128]{1,0:T(8,128)(2,1)S(1)}, u32[]{:S(2)}, u32[]{:S(2)}) collective-permute-start(bf16[160,128]{1,0:T(8,128)(2,1)S(1)} %get-tuple-element.10.refs_2_), channel_id=1, source_target_pairs={{0,4},{4,0},{1,5},{5,1},{2,6},{6,2},{3,7},{7,3},{8,12},{12,8},{9,1... | collective-permute-start | bytes 122888 | tf_op jit(solution)/shard_map/ppermute | solution.py:523
  9.0 0.6 %select_convert_fusion.refs_6_ = bf16[2,128,64]{2,1,0:T(8,128)(2,1)S(1)} fusion(s32[2]{0:T(128)S(1)} %xor_multiply_fusion, s32[128]{0:T(128)S(1)} %iota_add_fusion, pred[128]{0:T(512)(128)(4,1)S(1)} %iota_compare_fusion), kind=kLoop, calls=%fused_computation.6 | loop fusion | flops 311296 | bytes 33416 | tf_op jit(solution)/shard_map/convert_element_type | solution.py:165
  9.7 0.0 collective-permute-done.4.refs_5_
  9.7 0.0 collective-permute-done.3.refs_4_
  9.7 1.3 %collective-permute-done.2.refs_3_ = bf16[160,128]{1,0:T(8,128)(2,1)S(1)} collective-permute-done((bf16[160,128]{1,0:T(8,128)(2,1)S(1)}, bf16[160,128]{1,0:T(8,128)(2,1)S(1)}, u32[]{:S(2)}, u32[]{:S(2)}) %collective-permute-start.2) | collective-permute-done | bytes 40992 | tf_op jit(solution)/shard_map/ppermute | solution.py:523
  11.0 0.2 collective-permute-done.1.refs_1_
  11.2 0.0 collective-permute-done.refs_0_
  11.2 0.3 %shard_map.132 = (bf16[304,128]{1,0:T(8,128)(2,1)S(1)}, bf16[272,128]{1,0:T(8,128)(2,1)S(1)}, f32[12,72,128]{2,1,0:T(8,128)S(1)}, f32[72,128]{1,0:T(8,128)S(1)}) custom-call(f32[2,2,64,128]{3,2,1,0:T(8,128)S(1)} %select_multiply_fusion.own_ref, bf16[256,128]{1,0:T(8,128)(2,1)S(1)} %collective-permute-done.refs_0_, ...), custom_call_target="tpu_custom_call" | custom-call | tf_op jit(solution)/shard_map/pallas_call | solution.py:531
  11.4 4.0 %collective-permute-start.7 = (bf16[304,128]{1,0:T(8,128)(2,1)S(1)}, bf16[304,128]{1,0:T(8,128)(2,1)S(1)}, u32[]{:S(2)}, u32[]{:S(2)}) collective-permute-start(bf16[304,128]{1,0:T(8,128)(2,1)S(1)} %get-tuple-element.12.msg_own_ref), channel_id=1, source_target_pairs={{0,24},{8,16},{16,8},{24,0},{1,25},{9,17},{17,9},{25,1},{2,26},{10... | collective-permute-start | bytes 233480 | tf_op jit(solution)/shard_map/ppermute | solution.py:545
  15.4 0.0 collective-permute-start.5
  15.4 0.6 %collective-permute-start.6 = (bf16[272,128]{1,0:T(8,128)(2,1)S(1)}, bf16[272,128]{1,0:T(8,128)(2,1)S(1)}, u32[]{:S(2)}, u32[]{:S(2)}) collective-permute-start(bf16[272,128]{1,0:T(8,128)(2,1)S(1)} %get-tuple-element.13), channel_id=1, source_target_pairs={{0,16},{8,24},{16,0},{24,8},{1,17},{9,25},{17,1},{25,9},{2,18},{10... | collective-permute-start | bytes 208904 | tf_op jit(solution)/shard_map/ppermute | solution.py:545
  16.1 1.7 %shard_map.133.refs_4_ = f32[38,2,64,128]{3,2,1,0:T(8,128)S(1)} custom-call(f32[12,72,128]{2,1,0:T(8,128)S(1)} %get-tuple-element.15.dens_ref), custom_call_target="tpu_custom_call" | custom-call | flops 24903680 | bytes 2490368 | tf_op jit(solution)/shard_map/pallas_call | solution.py:547
  17.8 3.5 %collective-permute-done.6.refs_1_ = bf16[272,128]{1,0:T(8,128)(2,1)S(1)} collective-permute-done((bf16[272,128]{1,0:T(8,128)(2,1)S(1)}, bf16[272,128]{1,0:T(8,128)(2,1)S(1)}, u32[]{:S(2)}, u32[]{:S(2)}) %collective-permute-start.6) | collective-permute-done | bytes 69664 | tf_op jit(solution)/shard_map/ppermute | solution.py:545
  21.3 0.0 collective-permute-done.7.refs_2_
  21.3 0.0 collective-permute-done.5.refs_0_
  21.3 0.0 copy-done.1
  21.3 0.0 copy-done.4
  21.4 3.3 %shard_map.134 = (f32[38,2,64,128]{3,2,1,0:T(8,128)}, f32[2,256]{1,0:T(2,128)}) custom-call(bf16[304,128]{1,0:T(8,128)(2,1)S(1)} %get-tuple-element.12.msg_own_ref, bf16[304,128]{1,0:T(8,128)(2,1)S(1)} %collective-permute-done.5.refs_0_, bf16[272,128]{1,0:T(8,128)(2,1)S(1)} %collective-permute-done.6.refs_1_, ...), custom_call_target="tpu_custom_call" | custom-call | tf_op jit(solution)/shard_map/pallas_call | solution.py:556
  (13 shorter events, 0.0 us)
Async XLA Ops:
  0.6 20.6 %copy-start.1 = (f32[128,256]{1,0:T(8,128)S(1)}, f32[128,256]{1,0:T(8,128)}, u32[]{:S(2)}) copy-start(f32[128,256]{1,0:T(8,128)} %constant.59.clone.refs_13_) | copy-start | bytes 393220
  0.6 20.6 %copy-start.4 = (bf16[384,128]{1,0:T(8,128)(2,1)S(1)}, bf16[384,128]{1,0:T(8,128)(2,1)}, u32[]{:S(2)}) copy-start(bf16[384,128]{1,0:T(8,128)(2,1)} %constant.58.clone.refs_12_) | copy-start | bytes 294916
  0.7 20.6 %copy-start.5 = (f32[2,72,128]{2,1,0:T(8,128)S(1)}, f32[2,72,128]{2,1,0:T(8,128)}, u32[]{:S(2)}) copy-start(f32[2,72,128]{2,1,0:T(8,128)} %constant.57.clone.refs_11_) | copy-start | bytes 221188
  0.7 20.6 %copy-start.2 = (bf16[512,128]{1,0:T(8,128)(2,1)S(1)}, bf16[512,128]{1,0:T(8,128)(2,1)}, u32[]{:S(2)}) copy-start(bf16[512,128]{1,0:T(8,128)(2,1)} %constant.56.clone.refs_10_) | copy-start | bytes 393220
  0.7 20.6 %copy-start.3 = (s32[72,384]{1,0:T(8,128)S(1)}, s32[72,384]{1,0:T(8,128)}, u32[]{:S(2)}) copy-start(s32[72,384]{1,0:T(8,128)} %constant.52.clone.refs_6_) | copy-start | bytes 331780
  0.7 20.6 %copy-start = (bf16[512,768]{1,0:T(8,128)(2,1)S(1)}, bf16[512,768]{1,0:T(8,128)(2,1)}, u32[]{:S(2)}) copy-start(bf16[512,768]{1,0:T(8,128)(2,1)} %constant.51.clone.refs_5_) | copy-start | bytes 2359300
  1.7 0.8 %copy-start.6 = (s32[64,128]{1,0:T(8,128)S(1)}, s32[64,128]{1,0:T(8,128)}, u32[]{:S(2)}) copy-start(s32[64,128]{1,0:T(8,128)} %shells_ref.1) | copy-start | bytes 98308
  2.5 18.8 %copy-start.7 = (f32[4,128]{1,0:T(4,128)S(1)}, f32[4,128]{1,0:T(4,128)}, u32[]{:S(2)}) copy-start(f32[4,128]{1,0:T(4,128)} %constant.55.clone.refs_9_) | copy-start | bytes 6148
  2.5 18.8 %copy-start.8 = (f32[1,384]{1,0:T(1,128)S(1)}, f32[1,384]{1,0:T(1,128)}, u32[]{:S(2)}) copy-start(f32[1,384]{1,0:T(1,128)} %constant.53.clone.refs_7_) | copy-start | bytes 4612
  2.5 18.8 %copy-start.9 = (f32[1,256]{1,0:T(1,128)S(1)}, f32[1,256]{1,0:T(1,128)}, u32[]{:S(2)}) copy-start(f32[1,256]{1,0:T(1,128)} %constant.54.clone.refs_8_) | copy-start | bytes 3076
  2.7 7.0 %collective-permute-start.4 = (bf16[16,128]{1,0:T(8,128)(2,1)S(1)}, bf16[16,128]{1,0:T(8,128)(2,1)S(1)}, u32[]{:S(2)}, u32[]{:S(2)}) collective-permute-start(bf16[16,128]{1,0:T(8,128)(2,1)S(1)} %get-tuple-element.11), channel_id=1, source_target_pairs={{0,7},{1,6},{2,5},{3,4},{4,3},{5,2},{6,1},{7,0},{8,15},{9,14},{10,... | collective-permute-start | bytes 12296 | tf_op jit(solution)/shard_map/ppermute | solution.py:525
  6.1 3.6 %collective-permute-start.3 = (bf16[16,128]{1,0:T(8,128)(2,1)S(1)}, bf16[16,128]{1,0:T(8,128)(2,1)S(1)}, u32[]{:S(2)}, u32[]{:S(2)}) collective-permute-start(bf16[16,128]{1,0:T(8,128)(2,1)S(1)} %get-tuple-element.11), channel_id=1, source_target_pairs={{0,5},{1,4},{2,7},{3,6},{4,1},{5,0},{6,3},{7,2},{8,13},{9,12},{10,... | collective-permute-start | bytes 12296 | tf_op jit(solution)/shard_map/ppermute | solution.py:525
  6.9 4.3 %collective-permute-start.1 = (bf16[256,128]{1,0:T(8,128)(2,1)S(1)}, bf16[256,128]{1,0:T(8,128)(2,1)S(1)}, u32[]{:S(2)}, u32[]{:S(2)}) collective-permute-start(bf16[256,128]{1,0:T(8,128)(2,1)S(1)} %get-tuple-element.9), channel_id=1, source_target_pairs={{0,3},{1,2},{2,1},{3,0},{4,7},{5,6},{6,5},{7,4},{8,11},{9,10},{10,... | collective-permute-start | bytes 196616 | tf_op jit(solution)/shard_map/ppermute | solution.py:522
  7.0 4.2 %collective-permute-start = (bf16[256,128]{1,0:T(8,128)(2,1)S(1)}, bf16[256,128]{1,0:T(8,128)(2,1)S(1)}, u32[]{:S(2)}, u32[]{:S(2)}) collective-permute-start(bf16[256,128]{1,0:T(8,128)(2,1)S(1)} %get-tuple-element.9), channel_id=1, source_target_pairs={{0,1},{1,0},{2,3},{3,2},{4,5},{5,4},{6,7},{7,6},{8,9},{9,8},{10,11... | collective-permute-start | bytes 196616 | tf_op jit(solution)/shard_map/ppermute | solution.py:522
  7.0 4.0 %collective-permute-start.2 = (bf16[160,128]{1,0:T(8,128)(2,1)S(1)}, bf16[160,128]{1,0:T(8,128)(2,1)S(1)}, u32[]{:S(2)}, u32[]{:S(2)}) collective-permute-start(bf16[160,128]{1,0:T(8,128)(2,1)S(1)} %get-tuple-element.10.refs_2_), channel_id=1, source_target_pairs={{0,4},{4,0},{1,5},{5,1},{2,6},{6,2},{3,7},{7,3},{8,12},{12,8},{9,1... | collective-permute-start | bytes 122888 | tf_op jit(solution)/shard_map/ppermute | solution.py:523
  11.4 9.8 %collective-permute-start.7 = (bf16[304,128]{1,0:T(8,128)(2,1)S(1)}, bf16[304,128]{1,0:T(8,128)(2,1)S(1)}, u32[]{:S(2)}, u32[]{:S(2)}) collective-permute-start(bf16[304,128]{1,0:T(8,128)(2,1)S(1)} %get-tuple-element.12.msg_own_ref), channel_id=1, source_target_pairs={{0,24},{8,16},{16,8},{24,0},{1,25},{9,17},{17,9},{25,1},{2,26},{10... | collective-permute-start | bytes 233480 | tf_op jit(solution)/shard_map/ppermute | solution.py:545
  15.4 5.8 %collective-permute-start.5 = (bf16[304,128]{1,0:T(8,128)(2,1)S(1)}, bf16[304,128]{1,0:T(8,128)(2,1)S(1)}, u32[]{:S(2)}, u32[]{:S(2)}) collective-permute-start(bf16[304,128]{1,0:T(8,128)(2,1)S(1)} %get-tuple-element.12.msg_own_ref), channel_id=1, source_target_pairs={{0,8},{8,0},{16,24},{24,16},{1,9},{9,1},{17,25},{25,17},{2,10},{10... | collective-permute-start | bytes 233480 | tf_op jit(solution)/shard_map/ppermute | solution.py:545
  15.4 5.8 %collective-permute-start.6 = (bf16[272,128]{1,0:T(8,128)(2,1)S(1)}, bf16[272,128]{1,0:T(8,128)(2,1)S(1)}, u32[]{:S(2)}, u32[]{:S(2)}) collective-permute-start(bf16[272,128]{1,0:T(8,128)(2,1)S(1)} %get-tuple-element.13), channel_id=1, source_target_pairs={{0,16},{8,24},{16,0},{24,8},{1,17},{9,25},{17,1},{25,9},{2,18},{10... | collective-permute-start | bytes 208904 | tf_op jit(solution)/shard_map/ppermute | solution.py:545

commit v3 on v2

--- a/solution.py
+++ b/solution.py
@@ -12,6 +12,9 @@
 
 NSHELL = 256
 UNUSED = -(1 << 20)
+ENDS = (10, 19, 29, 38)
+FIRST_ROUND = (("col", 0), ("diag", 0), ("row", 1), ("col", 1), ("diag", 1))
+SWAPS = {4: (1, 3, 2)}
 TOP = 40
 ROWS = 72
 F32 = jnp.float32
@@ -64,6 +67,10 @@
         odd = lax.rem(index, 2)
         return 1 - odd, odd
     return 0, 1
+
+
+def swap_order(count):
+    return SWAPS.get(count, tuple(range(1, count)))
 
 
 def pair_product(first, second, count_second):
@@ -153,19 +160,33 @@
     )
 
 
-def x_table(n_row, wx):
+def turn_table(steps, full):
+    quarter = (4 * steps + full // 2) // full
+    rest = (steps - quarter * (full // 4)).astype(F32) * F32(2.0 * math.pi / full)
+    square = rest * rest
+    cos, sin = F32(1.0), F32(1.0)
+    for order in (8, 6, 4, 2):
+        cos = 1.0 - square * cos * F32(1.0 / (order * (order - 1)))
+        sin = 1.0 - square * sin * F32(1.0 / (order * (order + 1)))
+    sin = sin * rest
+    odd = quarter % 2 == 1
+    cos, sin = jnp.where(odd, sin, cos), jnp.where(odd, cos, sin)
+    cos = jnp.where((quarter == 1) | (quarter == 2), -cos, cos)
+    return cos, jnp.where((quarter == 2) | (quarter == 3), -sin, sin)
+
+
+def x_table(row, n_row, wx):
     full_x = n_row * wx
     half_x = full_x // 2
-    freq = lax.broadcasted_iota(jnp.int32, (n_row, full_x, wx), 1)
-    block = lax.broadcasted_iota(jnp.int32, (n_row, full_x, wx), 0) ^ lax.axis_index("row")
-    pos = block * wx + lax.broadcasted_iota(jnp.int32, (n_row, full_x, wx), 2)
+    freq = lax.broadcasted_iota(jnp.int32, (full_x, full_x), 0)
+    lane = lax.broadcasted_iota(jnp.int32, (full_x, full_x), 1)
+    pos = (lane // wx ^ row) * wx + lane % wx
     is_cos = freq <= half_x
-    freq = jnp.where(is_cos, freq, freq - half_x)
-    angles = (freq * pos % full_x).astype(F32) * (2.0 * math.pi / full_x)
-    return jnp.where(is_cos, jnp.cos(angles), -jnp.sin(angles)).astype(BF16)
-
-
-def pack_kernel(n_row, n_sec, per, own_ref, shells_ref, col_ref, row_ref, edge_ref):
+    cos, sin = turn_table(jnp.where(is_cos, freq, freq - half_x) * pos % full_x, full_x)
+    return jnp.where(is_cos, cos, -sin).astype(BF16)
+
+
+def pack_kernel(n_row, n_sec, per, own_ref, col_ref, row_ref, edge_ref, table_ref):
     _, depth, wx, wy = own_ref.shape
     edges = []
     densities = [[own_ref[c, z] for z in range(depth)] for c in range(2)]
@@ -183,10 +204,12 @@
     count = edge.shape[0]
     row_ref[at : at + count] = edge
 
+    table_ref[...] = x_table(lax.axis_index("row"), n_row, wx)
+
     row, sec = lax.axis_index("row"), lax.axis_index("sec")
     square, root = shell_root(row * wx, sec * wy, wx * n_row, wy * n_sec, wx, wy)
     special = (root * root == square + 1.0) & (root < NSHELL) & (square > 0.0)
-    nudge = jnp.where(special, shells_ref[...].astype(F32) - (root - 1.0), 0.0)
+    nudge = jnp.where(special, own_ref[2, 0] - (root - 1.0), 0.0)
     one = jnp.where(special, F32(1.0), F32(0.0)).astype(BF16)
     down = lax.broadcasted_iota(jnp.int32, (wx, wx), 0)
     above = (lax.broadcasted_iota(jnp.int32, (wx, wx), 1) < down).astype(F32).astype(BF16)
@@ -209,36 +232,32 @@
     return square, jnp.floor(jnp.sqrt(square + 1.0) + 0.5)
 
 
-def middle_kernel(n_row, n_col, section, own_ref, *refs):
+def half_kernel(depth, wx, n_row, *refs):
+    row_refs, table_ref, bulk_ref = refs[:n_row], refs[n_row], refs[n_row + 1]
+    full_x = table_ref.shape[0]
+    for z in range(depth):
+        lines = jnp.concatenate([r[z * wx : (z + 1) * wx] for r in row_refs], axis=0)
+        half = jnp.dot(table_ref[...], lines, preferred_element_type=F32)
+        bulk_ref[z * full_x : (z + 1) * full_x] = half.astype(BF16)
+    at = depth * wx + 8 * depth
+    marks = sum(ref[at:].astype(F32) for ref in row_refs)
+    bulk_ref[depth * full_x :] = marks.astype(BF16)
+
+
+def middle_kernel(n_row, n_col, names, own_ref, row_ref, *refs):
     _, depth, wx, wy = own_ref.shape
     col_moves, row_moves = len(ring_moves(n_col)), len(ring_moves(n_row))
-    col_refs, refs = refs[:col_moves], refs[col_moves:]
-    row_refs, refs = refs[:n_row], refs[n_row:]
-    diag_refs, refs = refs[: col_moves * row_moves], refs[col_moves * row_moves :]
-    table_ref, msg_ref, short_ref, dens_ref, lanes_ref = refs
+    by_name, refs = dict(zip(names, refs)), refs[len(names) :]
+    msg_ref, dens_ref, lanes_ref = refs
+    col_refs = [by_name["col", i] for i in range(col_moves)]
+    row_refs = [row_ref] + [by_name["row", k] for k in range(1, n_row)]
+    diag_refs = [by_name["diag", i] for i in range(col_moves * row_moves)]
     row, col = lax.axis_index("row"), lax.axis_index("col")
-    full_x = table_ref.shape[1]
-
-    for z in range(depth):
-        half = None
-        for k in range(n_row):
-            part = jnp.dot(
-                table_ref[k],
-                row_refs[k][z * wx : (z + 1) * wx],
-                preferred_element_type=F32,
-            )
-            half = part if half is None else half + part
-        half = half.astype(BF16)
-        msg_ref[z * full_x : (z + 1) * full_x] = half
-        short_ref[z * full_x : (z + 1) * full_x] = half
-
     at = depth * wx
     count = 8 * depth
-    marks = sum(ref[at + count :].astype(F32) for ref in row_refs)[:section]
-
     col_prev, col_next = ring_pick(n_col, col)
-    before = choose([r[...] for r in col_refs], col_prev).astype(F32)
-    after = choose([r[...] for r in col_refs], col_next).astype(F32)
+    before = choose([r[...].astype(F32) for r in col_refs], col_prev)
+    after = choose([r[...].astype(F32) for r in col_refs], col_next)
     edge_list = [r[at : at + count].astype(F32) for r in row_refs]
     edge_prev = choose(edge_list, row ^ lax.rem(row + n_row - 1, n_row)) if n_row > 2 else edge_list[1]
     edge_next = choose(edge_list, row ^ lax.rem(row + 1, n_row)) if n_row > 2 else edge_list[1]
@@ -285,14 +304,10 @@
             moved = pltpu.roll(tile, (at_lane + 2) % wy, 1)
             strips = jnp.where((lane >= at_lane) & (lane < at_lane + 4), moved, strips)
     lanes_ref[...] = strips + pltpu.roll(strips, 4, 1)
-    at = depth * full_x
     lower = jnp.concatenate([strips[TOP:], jnp.zeros((2 * TOP - ROWS, wy), F32)], axis=0)
     folded = strips[:TOP] + pltpu.roll(lower, 4, 1)
-    for ref, parts in ((msg_ref, [marks, folded]), (short_ref, [marks])):
-        missing = ref.shape[0] - at - sum(p.shape[0] for p in parts)
-        if missing:
-            parts = parts + [jnp.zeros((missing, wy), F32)]
-        ref[at:] = jnp.concatenate(parts, axis=0).astype(BF16)
+    gap = jnp.zeros((msg_ref.shape[0] - TOP, wy), F32)
+    msg_ref[...] = jnp.concatenate([folded, gap], axis=0).astype(BF16)
 
 
 def turn(tile, shift, axis):
@@ -351,10 +366,10 @@
                     out_ref[c * 19 + number, z] = tile[:wx]
 
 
-def set_ends(n_sec, start, at, msg_refs, lanes_ref, cells_ref, out_hbm, out_ref, sems):
+def set_ends(n_sec, msg_refs, lanes_ref, cells_ref, out_hbm, out_ref, sems):
     _, depth, wx, wy = out_ref.shape
     layers = depth + 4
-    strips = [r[start:].astype(F32)[at - start :][:TOP] for r in msg_refs]
+    strips = [r[...].astype(F32)[:TOP] for r in msg_refs]
     index = lax.axis_index("sec")
     prev_which, next_which = ring_pick(n_sec, index)
     before, after = choose(strips, prev_which), choose(strips, next_which)
@@ -371,32 +386,40 @@
     terms = relax_terms(tile, velocity)
     lane = lax.broadcasted_iota(jnp.int32, (wx, wy), 1)
     copies = []
+    moved = []
     for number in range(19):
         cx, cy, cz = LATTICE[number]
         term = turn(terms[number], cx, 0)[:wx]
         if cy == 0:
             term = jnp.where(place[:wx] == 1, turn(term, -4, 1), term)
-            mask = (lane == 0) | (lane == wy - 1)
-        else:
-            mask = lane < 2 if cy > 0 else lane >= wy - 2
-        for c in range(2):
-            for z in range(depth):
-                group = 8 * (c * layers + 2 + z - cz)
-                back = {1: group + 1, -1: group + 5 - (wy - 2), 0: group + 2}[cy]
-                q = c * 19 + number
-                out_ref[q, z] = jnp.where(mask, turn(term, -back, 1), cells_ref[q, z])
-            copy = pltpu.make_async_copy(out_ref.at[q], out_hbm.at[q], sems.at[q])
+        moved.append(term)
+    masks = {1: lane < 2, -1: lane >= wy - 2, 0: (lane == 0) | (lane == wy - 1)}
+    begin = 0
+    for q in range(38):
+        c, number = divmod(q, 19)
+        _, cy, cz = LATTICE[number]
+        for z in range(depth):
+            group = 8 * (c * layers + 2 + z - cz)
+            back = {1: group + 1, -1: group + 5 - (wy - 2), 0: group + 2}[cy]
+            out_ref[q, z] = jnp.where(masks[cy], turn(moved[number], -back, 1), cells_ref[q, z])
+        if q + 1 in ENDS:
+            span = pl.ds(begin, q + 1 - begin)
+            copy = pltpu.make_async_copy(
+                out_ref.at[span], out_hbm.at[span], sems.at[len(copies)]
+            )
             copy.start()
             copies.append(copy)
+            begin = q + 1
     return copies
 
 
 def final_kernel(n_sec, section, move, msg_own_ref, *refs):
-    msg_refs = [msg_own_ref] + list(refs[: n_sec - 1])
-    strips_ref, cells_ref = refs[n_sec - 1 : n_sec + 1]
-    refs = refs[n_sec + 1 :]
+    msg_refs = [msg_own_ref] + [refs[swap_order(n_sec).index(k)] for k in range(1, n_sec)]
+    refs = refs[n_sec - 1 :]
+    ring, refs = refs[: len(ring_moves(n_sec))], refs[len(ring_moves(n_sec)) :]
+    (strips_ref, cells_ref), refs = refs[:2], refs[2:]
     (table_ref, move_ref, mult_ref, counts_ref, put_ref, lanes_ref, row_ref, col_ref, step_ref,
-     out_hbm, spec_ref, lhs_ref, mark_ref, part_ref, out_ref, sems) = refs
+     out_hbm, spec_hbm, lhs_ref, mark_ref, part_ref, out_ref, spec_ref, sems) = refs
     depth = spec_ref.shape[0]
     sec = lax.axis_index("sec")
     full_y, lanes = table_ref.shape[0], table_ref.shape[1] // 2
@@ -406,8 +429,7 @@
     hrows = half_x + 8
     at = depth * full_x
     lines_used = put_ref.shape[0]
-    ring = [msg_refs[move_[0][1]] for move_ in ring_moves(n_sec)]
-    copies = set_ends(n_sec, at, at + section, ring, strips_ref, cells_ref, out_hbm, out_ref, sems)
+    copies = set_ends(n_sec, ring, strips_ref, cells_ref, out_hbm, out_ref, sems)
 
     for k in range(n_sec):
         start = pl.multiple_of((sec ^ k) * wy, wy)
@@ -484,6 +506,8 @@
         line = jnp.sum(jnp.concatenate(sums[z], axis=1), axis=0, keepdims=True)
         lines.append((line + moved[z : z + 1]) / norm)
     spec_ref[...] = jnp.concatenate(lines, axis=0)
+    copies.append(pltpu.make_async_copy(spec_ref, spec_hbm, sems.at[len(ENDS)]))
+    copies[-1].start()
     for copy in copies:
         copy.wait()
 
@@ -508,16 +532,21 @@
     count = 8 * depth
     shape = jax.ShapeDtypeStruct
 
-    other = lax.broadcasted_iota(jnp.int32, jitter.shape, 0)
-    own = jnp.where((labels[None] ^ other) == 1, F32(1.0), F32(0.2)) * jitter
-    col_msg, row_msg, edge_msg = call(
+    part = lax.broadcasted_iota(jnp.int32, (3, depth, wx, wy), 0)
+    none = (0, 0, 0)
+    factor = lax.pad(jitter, F32(0.0), ((0, 1, 0), none, none, none))
+    whole_numbers = jnp.where(part == 2, shells[None, None], labels[None] ^ part)
+    density = jnp.where(whole_numbers == 1, F32(1.0), F32(0.2)) * factor
+    own = jnp.where(part == 2, whole_numbers.astype(F32), density)
+    col_msg, row_msg, edge_msg, table_x = call(
         functools.partial(pack_kernel, n_row, n_sec, per),
         [
             shape((2 * depth * wx, wy), BF16),
             shape((depth * wx + count + whole(section), wy), BF16),
             shape((count, wy), BF16),
+            shape((full_x, full_x), BF16),
         ],
-    )(own, shells)
+    )(own)
 
     col_got = [lax.ppermute(col_msg, "col", m) for m in ring_moves(n_col)]
     row_got = [lax.ppermute(row_msg, "row", xor_pairs(n_row, k)) for k in range(1, n_row)]
@@ -528,21 +557,27 @@
     ]
 
     at = depth * full_x
-    msg, short, dens, lanes_own = call(
-        functools.partial(middle_kernel, n_row, n_col, section),
+    got = {("col", i): value for i, value in enumerate(col_got)}
+    got.update({("row", k + 1): value for k, value in enumerate(row_got)})
+    got.update({("diag", i): value for i, value in enumerate(diag_got)})
+    names = [name for name in FIRST_ROUND if name in got]
+    names += [name for name in got if name not in names]
+    bulk = call(
+        functools.partial(half_kernel, depth, wx, n_row), shape((at + whole(section), wy), BF16)
+    )(row_msg, *row_got, table_x)
+    strip, dens, lanes_own = call(
+        functools.partial(middle_kernel, n_row, n_col, tuple(names)),
         [
-            shape((at + whole(section + TOP), wy), BF16),
-            shape((at + whole(section), wy), BF16),
+            shape((whole(TOP), wy), BF16),
             shape((2 * layers, ROWS, wy), F32),
             shape((ROWS, wy), F32),
         ],
-    )(own, *col_got, row_msg, *row_got, *diag_got, x_table(n_row, wx))
-
-    ring = ring_moves(n_sec)
-    sec_got = []
-    for k in range(1, n_sec):
-        move = xor_pairs(n_sec, k)
-        sec_got.append(lax.ppermute(msg if move in ring else short, "sec", move))
+        flops=1 << 24,
+        moved=1 << 20,
+    )(own, row_msg, *[got[name] for name in names])
+
+    sec_got = [lax.ppermute(bulk, "sec", xor_pairs(n_sec, k)) for k in swap_order(n_sec)]
+    ring_got = [lax.ppermute(strip, "sec", move) for move in ring_moves(n_sec)]
 
     cells = call(
         cells_kernel,
@@ -555,19 +590,17 @@
     names = ("mult_y", "counts", "put", "lanes_of", "mark_row", "mark_col", "step")
     return call(
         functools.partial(final_kernel, n_sec, section, tables["move"]),
-        (shape((38, depth, wx, wy), F32), shape((depth, NSHELL), F32)),
+        [shape((38, depth, wx, wy), F32), shape((depth, NSHELL), F32)],
         [
             pltpu.VMEM((depth * full_x, full_y), BF16),
             pltpu.VMEM((whole(section), full_y), BF16),
             pltpu.VMEM((depth, hrows, lanes), F32),
             pltpu.VMEM((38, depth, wx, wy), F32),
-            pltpu.SemaphoreType.DMA((38,)),
+            pltpu.VMEM((depth, NSHELL), F32),
+            pltpu.SemaphoreType.DMA((len(ENDS) + 1,)),
         ],
-        out_specs=(
-            pl.BlockSpec(memory_space=pltpu.HBM),
-            pl.BlockSpec(memory_space=pltpu.VMEM),
-        ),
-    )(msg, *sec_got, lanes_own, cells, tables["table_y"], tables["move"].astype(np.int32),
+        out_specs=[pl.BlockSpec(memory_space=pltpu.HBM)] * 2,
+    )(bulk, *sec_got, *ring_got, lanes_own, cells, tables["table_y"], tables["move"].astype(np.int32),
       *[tables[name] for name in names])
 
 

time: 24.8 us -> 23 us (0.927)
  waiting for transfers between devices: 4.98 us -> 1.73 us
  starting transfers between devices: 11 us -> 14.1 us
  local copies, waits for them, and re-layouts: 0.81 us -> 0.06 us
  Pallas kernels: 5.42 us -> 4.8 us
  other arithmetic: 1.67 us -> 1.26 us
    ppermute x3 -> x5, starting transfers between devices: 4.62 us -> 7.79 us  [the longest x3 5.66 us: on_device(): lax.ppermute(bulk, 'sec', xor_pairs(n_sec, k))]
    ppermute x2, starting transfers between devices: 4.18 us -> 1.72 us  [on_device(): lax.ppermute(edge_msg, ('row', 'col'), pair_product(a, b, n_col))]
    ppermute x3 -> x5, waiting for transfers between devices: 3.5 us -> 1.71 us  [the longest x2 1.7 us: on_device(): ring_got = [lax.ppermute(strip, 'sec', move) for move in ring_moves(n_sec)]]
    ppermute x2, starting transfers between devices: 0.14 us -> 1.61 us  [on_device(): col_got = [lax.ppermute(col_msg, 'col', m) for m in ring_moves(n_col)]]
    ppermute x1, waiting for transfers between devices: 1.31 us -> 0.01 us  [on_device(): lax.ppermute(row_msg, 'row', xor_pairs(n_row, k))]
    select_n x0 -> x1, other arithmetic: none -> 1.25 us  [on_device(): own = jnp.where(part == 2, whole_numbers.astype(F32), density)]
    mul x2 -> x0, other arithmetic: 1.03 us -> none  [the longest x1 1.03 us: on_device(): own = jnp.where(labels[None] ^ other == 1, F32(1.0), F32(0.2)) * jitter]
    ppermute x1, starting transfers between devices: 2.03 us -> 3.03 us  [on_device(): lax.ppermute(row_msg, 'row', xor_pairs(n_row, k))]
  transfers between devices with their start and end apart: 8 -> 10, of which waited for: 3 -> 1; matrix products, arithmetic and copies ran while one was open for 3% -> 0% of each run, Pallas kernels for 7% -> 9%
where the time goes in v3:
time: 23 us; the launch traced here: 22.8 us
  starting transfers between devices  14.1 us (61%)
  Pallas kernels  4.8 us (21%)
  waiting for transfers between devices  1.73 us (8%)
  other arithmetic  1.26 us (5%)
  between operations  0.82 us (4%)
    ppermute x3, starting transfers between devices, on_device(): lax.ppermute(bulk, 'sec', xor_pairs(n_sec, k))  5.66 us
    ppermute x1, starting transfers between devices, on_device(): lax.ppermute(row_msg, 'row', xor_pairs(n_row, k))  3.03 us
    pallas_call x1, Pallas kernels, on_device(): call(functools.partial(final_kernel, n_sec, section, tables['move']), [sh...  2.34 us
    ppermute x2, starting transfers between devices, on_device(): ring_got = [lax.ppermute(strip, 'sec', move) for move in ring_moves(n_sec)]  2.13 us
    ppermute x2, starting transfers between devices, on_device(): lax.ppermute(edge_msg, ('row', 'col'), pair_product(a, b, n_col))  1.72 us
    ppermute x2, waiting for transfers between devices, on_device(): ring_got = [lax.ppermute(strip, 'sec', move) for move in ring_moves(n_sec)]  1.7 us
    pallas_call x1, Pallas kernels, on_device(): call(cells_kernel, shape((38, depth, wx, wy), F32), flops=38 * depth * wx...  1.7 us
    ppermute x2, starting transfers between devices, on_device(): col_got = [lax.ppermute(col_msg, 'col', m) for m in ring_moves(n_col)]  1.61 us
  transfers between devices with their start and end apart: 10, of which 1 were waited for; matrix products, arithmetic and copies ran while one was open for 0% of the time, Pallas kernels for 9%

profile of v3, /device:TPU:0, one launch (start us, length us, event | category | flops | bytes accessed | tf_op | source)
XLA Modules:
  0.0 22.8 jit_solution(7080931413166290372)
XLA Ops:
  0.6 0.0 copy-start.1
  0.6 0.0 copy-start.4
  0.7 0.0 copy-start.5
  0.7 0.0 copy-start.2
  0.7 0.0 copy-start.6
  0.7 0.0 copy-start.8
  0.7 0.0 copy-start.7
  0.7 0.0 copy-start.3
  0.7 0.0 copy-start
  0.8 1.3 %multiply_select_fusion.own_ref = f32[3,2,64,128]{3,2,1,0:T(8,128)S(1)} fusion(f32[2,2,64,128]{3,2,1,0:T(8,128)} %param.13, s32[2,64,128]{2,1,0:T(8,128)} %param.12, s32[64,128]{1,0:T(8,128)} %param.14, pred[3]{0:T(512)(128)(4,1)S(1)} %iota_compare_fusion), kind=kLoop, calls=%fused_computation | loop fusion | flops 344064 | bytes 425987 | tf_op jit(solution)/shard_map/jit(_where)/select_n | solution.py:540
  2.0 0.4 %shard_map.131 = (bf16[256,128]{1,0:T(8,128)(2,1)S(1)}, bf16[160,128]{1,0:T(8,128)(2,1)S(1)}, bf16[16,128]{1,0:T(8,128)(2,1)S(1)}, bf16[128,128]{1,0:T(8,128)(2,1)S(1)}) custom-call(f32[3,2,64,128]{3,2,1,0:T(8,128)S(1)} %multiply_select_fusion.own_ref), custom_call_target="tpu_custom_call" | custom-call | tf_op jit(solution)/shard_map/pallas_call | solution.py:541
  2.4 3.0 %collective-permute-start = (bf16[160,128]{1,0:T(8,128)(2,1)S(1)}, bf16[160,128]{1,0:T(8,128)(2,1)S(1)}, u32[]{:S(2)}, u32[]{:S(2)}) collective-permute-start(bf16[160,128]{1,0:T(8,128)(2,1)S(1)} %get-tuple-element.9.refs_0_.row_ref), channel_id=1, source_target_pairs={{0,4},{4,0},{1,5},{5,1},{2,6},{6,2},{3,7},{7,3},{8,12},{12,8},{9,1... | collective-permute-start | bytes 122888 | tf_op jit(solution)/shard_map/ppermute | solution.py:552
  5.4 0.7 %collective-permute-start.6 = (bf16[256,128]{1,0:T(8,128)(2,1)S(1)}, bf16[256,128]{1,0:T(8,128)(2,1)S(1)}, u32[]{:S(2)}, u32[]{:S(2)}) collective-permute-start(bf16[256,128]{1,0:T(8,128)(2,1)S(1)} %get-tuple-element.11), channel_id=1, source_target_pairs={{0,3},{1,2},{2,1},{3,0},{4,7},{5,6},{6,5},{7,4},{8,11},{9,10},{10,... | collective-permute-start | bytes 196616 | tf_op jit(solution)/shard_map/ppermute | solution.py:551
  6.1 1.0 %collective-permute-start.4 = (bf16[256,128]{1,0:T(8,128)(2,1)S(1)}, bf16[256,128]{1,0:T(8,128)(2,1)S(1)}, u32[]{:S(2)}, u32[]{:S(2)}) collective-permute-start(bf16[256,128]{1,0:T(8,128)(2,1)S(1)} %get-tuple-element.11), channel_id=1, source_target_pairs={{0,1},{1,0},{2,3},{3,2},{4,5},{5,4},{6,7},{7,6},{8,9},{9,8},{10,11... | collective-permute-start | bytes 196616 | tf_op jit(solution)/shard_map/ppermute | solution.py:551
  7.0 0.0 collective-permute-start.7
  7.0 1.7 %collective-permute-start.5 = (bf16[16,128]{1,0:T(8,128)(2,1)S(1)}, bf16[16,128]{1,0:T(8,128)(2,1)S(1)}, u32[]{:S(2)}, u32[]{:S(2)}) collective-permute-start(bf16[16,128]{1,0:T(8,128)(2,1)S(1)} %get-tuple-element.12), channel_id=1, source_target_pairs={{0,5},{1,4},{2,7},{3,6},{4,1},{5,0},{6,3},{7,2},{8,13},{9,12},{10,... | collective-permute-start | bytes 12296 | tf_op jit(solution)/shard_map/ppermute | solution.py:554
  8.7 0.0 collective-permute-done.refs_1_.refs_2_
  8.7 0.2 shard_map.132.msg_own_ref
  8.9 2.7 %collective-permute-start.3 = (bf16[272,128]{1,0:T(8,128)(2,1)S(1)}, bf16[272,128]{1,0:T(8,128)(2,1)S(1)}, u32[]{:S(2)}, u32[]{:S(2)}) collective-permute-start(bf16[272,128]{1,0:T(8,128)(2,1)S(1)} %shard_map.132.msg_own_ref), channel_id=1, source_target_pairs={{0,16},{8,24},{16,0},{24,8},{1,17},{9,25},{17,1},{25,9},{2,18},{10... | collective-permute-start | bytes 208904 | tf_op jit(solution)/shard_map/ppermute | solution.py:579
  11.6 0.0 collective-permute-done.7.refs_4_
  11.6 3.0 %collective-permute-start.2 = (bf16[272,128]{1,0:T(8,128)(2,1)S(1)}, bf16[272,128]{1,0:T(8,128)(2,1)S(1)}, u32[]{:S(2)}, u32[]{:S(2)}) collective-permute-start(bf16[272,128]{1,0:T(8,128)(2,1)S(1)} %shard_map.132.msg_own_ref), channel_id=1, source_target_pairs={{0,24},{8,16},{16,8},{24,0},{1,25},{9,17},{17,9},{25,1},{2,26},{10... | collective-permute-start | bytes 208904 | tf_op jit(solution)/shard_map/ppermute | solution.py:579
  14.6 0.0 collective-permute-done.5.refs_1_
  14.6 0.0 collective-permute-start.1
  14.6 0.0 collective-permute-done.6.refs_3_
  14.6 0.0 collective-permute-done.4.refs_0_
  14.6 0.2 %shard_map.133 = (bf16[48,128]{1,0:T(8,128)(2,1)S(1)}, f32[12,72,128]{2,1,0:T(8,128)S(1)}, f32[72,128]{1,0:T(8,128)S(1)}) custom-call(f32[3,2,64,128]{3,2,1,0:T(8,128)S(1)} %multiply_select_fusion.own_ref, bf16[160,128]{1,0:T(8,128)(2,1)S(1)} %get-tuple-element.9.refs_0_.row_ref, bf16[256,128]{1,0:T(8,128)(2,1)S(1)} %collective-permute-done.4.refs_0_, ...), custom_call_target="tpu_custom_call" | custom-call | flops 16777216 | bytes 1048576 | tf_op jit(solution)/shard_map/pallas_call | solution.py:568
  14.8 1.5 %collective-permute-start.9 = (bf16[48,128]{1,0:T(8,128)(2,1)S(1)}, bf16[48,128]{1,0:T(8,128)(2,1)S(1)}, u32[]{:S(2)}, u32[]{:S(2)}) collective-permute-start(bf16[48,128]{1,0:T(8,128)(2,1)S(1)} %get-tuple-element.13), channel_id=1, source_target_pairs={{0,24},{8,16},{16,8},{24,0},{1,25},{9,17},{17,9},{25,1},{2,26},{10... | collective-permute-start | bytes 36872 | tf_op jit(solution)/shard_map/ppermute | solution.py:580
  16.4 0.6 %collective-permute-start.8 = (bf16[48,128]{1,0:T(8,128)(2,1)S(1)}, bf16[48,128]{1,0:T(8,128)(2,1)S(1)}, u32[]{:S(2)}, u32[]{:S(2)}) collective-permute-start(bf16[48,128]{1,0:T(8,128)(2,1)S(1)} %get-tuple-element.13), channel_id=1, source_target_pairs={{0,8},{8,0},{16,24},{24,16},{1,9},{9,1},{17,25},{25,17},{2,10},{10... | collective-permute-start | bytes 36872 | tf_op jit(solution)/shard_map/ppermute | solution.py:580
  17.0 1.7 %shard_map.134.refs_6_ = f32[38,2,64,128]{3,2,1,0:T(8,128)S(1)} custom-call(f32[12,72,128]{2,1,0:T(8,128)S(1)} %get-tuple-element.15.dens_ref), custom_call_target="tpu_custom_call" | custom-call | flops 24903680 | bytes 2490368 | tf_op jit(solution)/shard_map/pallas_call | solution.py:582
  18.7 1.7 %collective-permute-done.9.refs_4_ = bf16[48,128]{1,0:T(8,128)(2,1)S(1)} collective-permute-done((bf16[48,128]{1,0:T(8,128)(2,1)S(1)}, bf16[48,128]{1,0:T(8,128)(2,1)S(1)}, u32[]{:S(2)}, u32[]{:S(2)}) %collective-permute-start.9) | collective-permute-done | bytes 12320 | tf_op jit(solution)/shard_map/ppermute | solution.py:580
  20.4 0.0 collective-permute-done.1.refs_0_
  20.5 2.3 %shard_map.135 = (f32[38,2,64,128]{3,2,1,0:T(8,128)}, f32[2,256]{1,0:T(2,128)}) custom-call(bf16[272,128]{1,0:T(8,128)(2,1)S(1)} %shard_map.132.msg_own_ref, bf16[272,128]{1,0:T(8,128)(2,1)S(1)} %collective-permute-done.1.refs_0_, bf16[272,128]{1,0:T(8,128)(2,1)S(1)} %collective-permute-done.2.refs_1_, bf16[272,128]{1,0:T(8,128)(2,1)S(1)} %collective-permute-done.3.refs_2_, ...), custom_call_target="tpu_custom_call" | custom-call | tf_op jit(solution)/shard_map/pallas_call | solution.py:591
  (13 shorter events, 0.0 us)
Async XLA Ops:
  0.6 19.8 %copy-start.1 = (f32[128,256]{1,0:T(8,128)S(1)}, f32[128,256]{1,0:T(8,128)}, u32[]{:S(2)}) copy-start(f32[128,256]{1,0:T(8,128)} %constant.36.clone.refs_15_) | copy-start | bytes 393220
  0.6 19.8 %copy-start.4 = (bf16[384,128]{1,0:T(8,128)(2,1)S(1)}, bf16[384,128]{1,0:T(8,128)(2,1)}, u32[]{:S(2)}) copy-start(bf16[384,128]{1,0:T(8,128)(2,1)} %constant.35.clone.refs_14_) | copy-start | bytes 294916
  0.7 19.7 %copy-start.5 = (f32[2,72,128]{2,1,0:T(8,128)S(1)}, f32[2,72,128]{2,1,0:T(8,128)}, u32[]{:S(2)}) copy-start(f32[2,72,128]{2,1,0:T(8,128)} %constant.34.clone.refs_13_) | copy-start | bytes 221188
  0.7 19.7 %copy-start.2 = (bf16[512,128]{1,0:T(8,128)(2,1)S(1)}, bf16[512,128]{1,0:T(8,128)(2,1)}, u32[]{:S(2)}) copy-start(bf16[512,128]{1,0:T(8,128)(2,1)} %constant.33.clone.refs_12_) | copy-start | bytes 393220
  0.7 19.7 %copy-start.6 = (f32[4,128]{1,0:T(4,128)S(1)}, f32[4,128]{1,0:T(4,128)}, u32[]{:S(2)}) copy-start(f32[4,128]{1,0:T(4,128)} %constant.32.clone.refs_11_) | copy-start | bytes 6148
  0.7 19.7 %copy-start.8 = (f32[1,256]{1,0:T(1,128)S(1)}, f32[1,256]{1,0:T(1,128)}, u32[]{:S(2)}) copy-start(f32[1,256]{1,0:T(1,128)} %constant.31.clone.refs_10_) | copy-start | bytes 3076
  0.7 19.7 %copy-start.7 = (f32[1,384]{1,0:T(1,128)S(1)}, f32[1,384]{1,0:T(1,128)}, u32[]{:S(2)}) copy-start(f32[1,384]{1,0:T(1,128)} %constant.30.clone.refs_9_) | copy-start | bytes 4612
  0.7 19.7 %copy-start.3 = (s32[72,384]{1,0:T(8,128)S(1)}, s32[72,384]{1,0:T(8,128)}, u32[]{:S(2)}) copy-start(s32[72,384]{1,0:T(8,128)} %constant.29.clone.refs_8_) | copy-start | bytes 331780
  0.7 19.7 %copy-start = (bf16[512,768]{1,0:T(8,128)(2,1)S(1)}, bf16[512,768]{1,0:T(8,128)(2,1)}, u32[]{:S(2)}) copy-start(bf16[512,768]{1,0:T(8,128)(2,1)} %constant.28.clone.refs_7_) | copy-start | bytes 2359300
  2.4 6.4 %collective-permute-start = (bf16[160,128]{1,0:T(8,128)(2,1)S(1)}, bf16[160,128]{1,0:T(8,128)(2,1)S(1)}, u32[]{:S(2)}, u32[]{:S(2)}) collective-permute-start(bf16[160,128]{1,0:T(8,128)(2,1)S(1)} %get-tuple-element.9.refs_0_.row_ref), channel_id=1, source_target_pairs={{0,4},{4,0},{1,5},{5,1},{2,6},{6,2},{3,7},{7,3},{8,12},{12,8},{9,1... | collective-permute-start | bytes 122888 | tf_op jit(solution)/shard_map/ppermute | solution.py:552
  5.4 9.2 %collective-permute-start.6 = (bf16[256,128]{1,0:T(8,128)(2,1)S(1)}, bf16[256,128]{1,0:T(8,128)(2,1)S(1)}, u32[]{:S(2)}, u32[]{:S(2)}) collective-permute-start(bf16[256,128]{1,0:T(8,128)(2,1)S(1)} %get-tuple-element.11), channel_id=1, source_target_pairs={{0,3},{1,2},{2,1},{3,0},{4,7},{5,6},{6,5},{7,4},{8,11},{9,10},{10,... | collective-permute-start | bytes 196616 | tf_op jit(solution)/shard_map/ppermute | solution.py:551
  6.1 8.5 %collective-permute-start.4 = (bf16[256,128]{1,0:T(8,128)(2,1)S(1)}, bf16[256,128]{1,0:T(8,128)(2,1)S(1)}, u32[]{:S(2)}, u32[]{:S(2)}) collective-permute-start(bf16[256,128]{1,0:T(8,128)(2,1)S(1)} %get-tuple-element.11), channel_id=1, source_target_pairs={{0,1},{1,0},{2,3},{3,2},{4,5},{5,4},{6,7},{7,6},{8,9},{9,8},{10,11... | collective-permute-start | bytes 196616 | tf_op jit(solution)/shard_map/ppermute | solution.py:551
  7.0 4.5 %collective-permute-start.7 = (bf16[16,128]{1,0:T(8,128)(2,1)S(1)}, bf16[16,128]{1,0:T(8,128)(2,1)S(1)}, u32[]{:S(2)}, u32[]{:S(2)}) collective-permute-start(bf16[16,128]{1,0:T(8,128)(2,1)S(1)} %get-tuple-element.12), channel_id=1, source_target_pairs={{0,7},{1,6},{2,5},{3,4},{4,3},{5,2},{6,1},{7,0},{8,15},{9,14},{10,... | collective-permute-start | bytes 12296 | tf_op jit(solution)/shard_map/ppermute | solution.py:554
  7.0 7.5 %collective-permute-start.5 = (bf16[16,128]{1,0:T(8,128)(2,1)S(1)}, bf16[16,128]{1,0:T(8,128)(2,1)S(1)}, u32[]{:S(2)}, u32[]{:S(2)}) collective-permute-start(bf16[16,128]{1,0:T(8,128)(2,1)S(1)} %get-tuple-element.12), channel_id=1, source_target_pairs={{0,5},{1,4},{2,7},{3,6},{4,1},{5,0},{6,3},{7,2},{8,13},{9,12},{10,... | collective-permute-start | bytes 12296 | tf_op jit(solution)/shard_map/ppermute | solution.py:554
  8.9 11.5 %collective-permute-start.3 = (bf16[272,128]{1,0:T(8,128)(2,1)S(1)}, bf16[272,128]{1,0:T(8,128)(2,1)S(1)}, u32[]{:S(2)}, u32[]{:S(2)}) collective-permute-start(bf16[272,128]{1,0:T(8,128)(2,1)S(1)} %shard_map.132.msg_own_ref), channel_id=1, source_target_pairs={{0,16},{8,24},{16,0},{24,8},{1,17},{9,25},{17,1},{25,9},{2,18},{10... | collective-permute-start | bytes 208904 | tf_op jit(solution)/shard_map/ppermute | solution.py:579
  11.6 8.8 %collective-permute-start.2 = (bf16[272,128]{1,0:T(8,128)(2,1)S(1)}, bf16[272,128]{1,0:T(8,128)(2,1)S(1)}, u32[]{:S(2)}, u32[]{:S(2)}) collective-permute-start(bf16[272,128]{1,0:T(8,128)(2,1)S(1)} %shard_map.132.msg_own_ref), channel_id=1, source_target_pairs={{0,24},{8,16},{16,8},{24,0},{1,25},{9,17},{17,9},{25,1},{2,26},{10... | collective-permute-start | bytes 208904 | tf_op jit(solution)/shard_map/ppermute | solution.py:579
  14.6 5.8 %collective-permute-start.1 = (bf16[272,128]{1,0:T(8,128)(2,1)S(1)}, bf16[272,128]{1,0:T(8,128)(2,1)S(1)}, u32[]{:S(2)}, u32[]{:S(2)}) collective-permute-start(bf16[272,128]{1,0:T(8,128)(2,1)S(1)} %shard_map.132.msg_own_ref), channel_id=1, source_target_pairs={{0,8},{8,0},{16,24},{24,16},{1,9},{9,1},{17,25},{25,17},{2,10},{10... | collective-permute-start | bytes 208904 | tf_op jit(solution)/shard_map/ppermute | solution.py:579
  14.8 5.5 %collective-permute-start.9 = (bf16[48,128]{1,0:T(8,128)(2,1)S(1)}, bf16[48,128]{1,0:T(8,128)(2,1)S(1)}, u32[]{:S(2)}, u32[]{:S(2)}) collective-permute-start(bf16[48,128]{1,0:T(8,128)(2,1)S(1)} %get-tuple-element.13), channel_id=1, source_target_pairs={{0,24},{8,16},{16,8},{24,0},{1,25},{9,17},{17,9},{25,1},{2,26},{10... | collective-permute-start | bytes 36872 | tf_op jit(solution)/shard_map/ppermute | solution.py:580
  16.4 4.0 %collective-permute-start.8 = (bf16[48,128]{1,0:T(8,128)(2,1)S(1)}, bf16[48,128]{1,0:T(8,128)(2,1)S(1)}, u32[]{:S(2)}, u32[]{:S(2)}) collective-permute-start(bf16[48,128]{1,0:T(8,128)(2,1)S(1)} %get-tuple-element.13), channel_id=1, source_target_pairs={{0,8},{8,0},{16,24},{24,16},{1,9},{9,1},{17,25},{25,17},{2,10},{10... | collective-permute-start | bytes 36872 | tf_op jit(solution)/shard_map/ppermute | solution.py:580

commit v4 on v3

--- a/solution.py
+++ b/solution.py
@@ -12,6 +12,8 @@
 
 NSHELL = 256
 UNUSED = -(1 << 20)
+MID = 1 << 24
+LBM = 1 << 10
 ENDS = (10, 19, 29, 38)
 FIRST_ROUND = (("col", 0), ("diag", 0), ("row", 1), ("col", 1), ("diag", 1))
 SWAPS = {4: (1, 3, 2)}
@@ -186,7 +188,7 @@
     return jnp.where(is_cos, cos, -sin).astype(BF16)
 
 
-def pack_kernel(n_row, n_sec, per, own_ref, col_ref, row_ref, edge_ref, table_ref):
+def pack_kernel(n_row, n_sec, per, own_ref, col_ref, row_ref, table_ref):
     _, depth, wx, wy = own_ref.shape
     edges = []
     densities = [[own_ref[c, z] for z in range(depth)] for c in range(2)]
@@ -199,7 +201,6 @@
     for z in range(depth):
         row_ref[z * wx : (z + 1) * wx] = (densities[0][z] - densities[1][z]).astype(BF16)
     edge = jnp.concatenate(edges, axis=0).astype(BF16)
-    edge_ref[...] = edge
     at = depth * wx
     count = edge.shape[0]
     row_ref[at : at + count] = edge
@@ -241,14 +242,25 @@
         bulk_ref[z * full_x : (z + 1) * full_x] = half.astype(BF16)
     at = depth * wx + 8 * depth
     marks = sum(ref[at:].astype(F32) for ref in row_refs)
-    bulk_ref[depth * full_x :] = marks.astype(BF16)
-
-
-def middle_kernel(n_row, n_col, names, own_ref, row_ref, *refs):
+    bulk_ref[depth * full_x : depth * full_x + marks.shape[0]] = marks.astype(BF16)
+    rest = depth * full_x + marks.shape[0]
+    if rest < bulk_ref.shape[0]:
+        bulk_ref[rest:] = jnp.zeros((bulk_ref.shape[0] - rest, bulk_ref.shape[1]), BF16)
+
+
+def edges_of(col_ref, wx):
+    lines = []
+    for start in range(0, col_ref.shape[0], wx):
+        lines.append(col_ref[start : start + 16].astype(F32)[:2])
+        lines.append(col_ref[start + wx - 16 : start + wx].astype(F32)[14:])
+    return jnp.concatenate(lines, axis=0)
+
+
+def middle_kernel(n_row, n_col, section, names, own_ref, row_ref, *refs):
     _, depth, wx, wy = own_ref.shape
     col_moves, row_moves = len(ring_moves(n_col)), len(ring_moves(n_row))
     by_name, refs = dict(zip(names, refs)), refs[len(names) :]
-    msg_ref, dens_ref, lanes_ref = refs
+    bulk_ref, msg_ref, dens_ref, lanes_ref = refs
     col_refs = [by_name["col", i] for i in range(col_moves)]
     row_refs = [row_ref] + [by_name["row", k] for k in range(1, n_row)]
     diag_refs = [by_name["diag", i] for i in range(col_moves * row_moves)]
@@ -262,7 +274,10 @@
     edge_prev = choose(edge_list, row ^ lax.rem(row + n_row - 1, n_row)) if n_row > 2 else edge_list[1]
     edge_next = choose(edge_list, row ^ lax.rem(row + 1, n_row)) if n_row > 2 else edge_list[1]
     row_prev, row_next = ring_pick(n_row, row)
-    diag = [r[...].astype(F32) for r in diag_refs]
+    diag = [
+        r[at : at + count].astype(F32) if r.shape == row_ref.shape else edges_of(r, wx)
+        for r in diag_refs
+    ]
 
     def diag_of(row_which, col_which):
         lines = [
@@ -306,8 +321,13 @@
     lanes_ref[...] = strips + pltpu.roll(strips, 4, 1)
     lower = jnp.concatenate([strips[TOP:], jnp.zeros((2 * TOP - ROWS, wy), F32)], axis=0)
     folded = strips[:TOP] + pltpu.roll(lower, 4, 1)
-    gap = jnp.zeros((msg_ref.shape[0] - TOP, wy), F32)
-    msg_ref[...] = jnp.concatenate([folded, gap], axis=0).astype(BF16)
+    at = msg_ref.shape[0] - whole(section + TOP)
+    msg_ref[:at] = bulk_ref[:at]
+    parts = [bulk_ref[at : at + whole(section)].astype(F32)[:section], folded]
+    missing = msg_ref.shape[0] - at - section - TOP
+    if missing:
+        parts.append(jnp.zeros((missing, wy), F32))
+    msg_ref[at:] = jnp.concatenate(parts, axis=0).astype(BF16)
 
 
 def turn(tile, shift, axis):
@@ -366,10 +386,10 @@
                     out_ref[c * 19 + number, z] = tile[:wx]
 
 
-def set_ends(n_sec, msg_refs, lanes_ref, cells_ref, out_hbm, out_ref, sems):
+def set_ends(n_sec, start, at, msg_refs, lanes_ref, cells_ref, out_hbm, out_ref, sems):
     _, depth, wx, wy = out_ref.shape
     layers = depth + 4
-    strips = [r[...].astype(F32)[:TOP] for r in msg_refs]
+    strips = [r[start:].astype(F32)[at - start :][:TOP] for r in msg_refs]
     index = lax.axis_index("sec")
     prev_which, next_which = ring_pick(n_sec, index)
     before, after = choose(strips, prev_which), choose(strips, next_which)
@@ -416,7 +436,7 @@
 def final_kernel(n_sec, section, move, msg_own_ref, *refs):
     msg_refs = [msg_own_ref] + [refs[swap_order(n_sec).index(k)] for k in range(1, n_sec)]
     refs = refs[n_sec - 1 :]
-    ring, refs = refs[: len(ring_moves(n_sec))], refs[len(ring_moves(n_sec)) :]
+    ring = [msg_refs[move_[0][1]] for move_ in ring_moves(n_sec)]
     (strips_ref, cells_ref), refs = refs[:2], refs[2:]
     (table_ref, move_ref, mult_ref, counts_ref, put_ref, lanes_ref, row_ref, col_ref, step_ref,
      out_hbm, spec_hbm, lhs_ref, mark_ref, part_ref, out_ref, spec_ref, sems) = refs
@@ -429,7 +449,7 @@
     hrows = half_x + 8
     at = depth * full_x
     lines_used = put_ref.shape[0]
-    copies = set_ends(n_sec, ring, strips_ref, cells_ref, out_hbm, out_ref, sems)
+    copies = set_ends(n_sec, at, at + section, ring, strips_ref, cells_ref, out_hbm, out_ref, sems)
 
     for k in range(n_sec):
         start = pl.multiple_of((sec ^ k) * wy, wy)
@@ -538,23 +558,26 @@
     whole_numbers = jnp.where(part == 2, shells[None, None], labels[None] ^ part)
     density = jnp.where(whole_numbers == 1, F32(1.0), F32(0.2)) * factor
     own = jnp.where(part == 2, whole_numbers.astype(F32), density)
-    col_msg, row_msg, edge_msg, table_x = call(
+    col_msg, row_msg, table_x = call(
         functools.partial(pack_kernel, n_row, n_sec, per),
         [
             shape((2 * depth * wx, wy), BF16),
             shape((depth * wx + count + whole(section), wy), BF16),
-            shape((count, wy), BF16),
             shape((full_x, full_x), BF16),
         ],
     )(own)
 
     col_got = [lax.ppermute(col_msg, "col", m) for m in ring_moves(n_col)]
     row_got = [lax.ppermute(row_msg, "row", xor_pairs(n_row, k)) for k in range(1, n_row)]
-    diag_got = [
-        lax.ppermute(edge_msg, ("row", "col"), pair_product(a, b, n_col))
-        for a in ring_moves(n_row)
-        for b in ring_moves(n_col)
-    ]
+    relay = n_row == 2 and n_col == 4
+    diag_got = []
+    for a in ring_moves(n_row):
+        for b in ring_moves(n_col):
+            if relay and b == xor_pairs(n_col, 1):
+                diag_got.append(lax.ppermute(row_got[0], "col", b))
+            else:
+                move = pair_product(a, b, n_col)
+                diag_got.append(lax.ppermute(col_msg, ("row", "col"), move))
 
     at = depth * full_x
     got = {("col", i): value for i, value in enumerate(col_got)}
@@ -563,27 +586,31 @@
     names = [name for name in FIRST_ROUND if name in got]
     names += [name for name in got if name not in names]
     bulk = call(
-        functools.partial(half_kernel, depth, wx, n_row), shape((at + whole(section), wy), BF16)
+        functools.partial(half_kernel, depth, wx, n_row), shape((at + whole(section + TOP), wy), BF16),
+        flops=1 << 27, moved=1 << 24
     )(row_msg, *row_got, table_x)
-    strip, dens, lanes_own = call(
-        functools.partial(middle_kernel, n_row, n_col, tuple(names)),
+    msg, dens, lanes_own = call(
+        functools.partial(middle_kernel, n_row, n_col, section, tuple(names)),
         [
-            shape((whole(TOP), wy), BF16),
+            shape((at + whole(section + TOP), wy), BF16),
             shape((2 * layers, ROWS, wy), F32),
             shape((ROWS, wy), F32),
         ],
-        flops=1 << 24,
-        moved=1 << 20,
-    )(own, row_msg, *[got[name] for name in names])
-
-    sec_got = [lax.ppermute(bulk, "sec", xor_pairs(n_sec, k)) for k in swap_order(n_sec)]
-    ring_got = [lax.ppermute(strip, "sec", move) for move in ring_moves(n_sec)]
+        flops=MID,
+        moved=MID,
+    )(own, row_msg, *[got[name] for name in names], bulk)
+
+    ring = ring_moves(n_sec)
+    sec_got = []
+    for k in swap_order(n_sec):
+        move = xor_pairs(n_sec, k)
+        sec_got.append(lax.ppermute(msg if move in ring else bulk, "sec", move))
 
     cells = call(
         cells_kernel,
         shape((38, depth, wx, wy), F32),
-        flops=38 * depth * wx * wy * 40,
-        moved=4 * 38 * depth * wx * wy,
+        flops=LBM,
+        moved=LBM,
     )(dens)
 
     hrows, lanes = full_x // 2 + 8, full_y // 2 + 128
@@ -600,7 +627,7 @@
             pltpu.SemaphoreType.DMA((len(ENDS) + 1,)),
         ],
         out_specs=[pl.BlockSpec(memory_space=pltpu.HBM)] * 2,
-    )(bulk, *sec_got, *ring_got, lanes_own, cells, tables["table_y"], tables["move"].astype(np.int32),
+    )(bulk, *sec_got, lanes_own, cells, tables["table_y"], tables["move"].astype(np.int32),
       *[tables[name] for name in names])
 
 

time: 23 us -> 21.9 us (0.952)
  starting transfers between devices: 14.1 us -> 11.4 us
  waiting for transfers between devices: 1.73 us -> 3.36 us
    ppermute x7 -> x5, starting transfers between devices: 9.51 us -> 7.4 us  [the longest x3 6.8 us: on_device(): sec_got.append(lax.ppermute(msg if move in ring else bulk, 'sec', move))]
    ppermute x7 -> x5, waiting for transfers between devices: 1.72 us -> 2.98 us  [the longest x3 2.98 us: on_device(): sec_got.append(lax.ppermute(msg if move in ring else bulk, 'sec', move))]
    ppermute x2, starting transfers between devices: 1.61 us -> 1.02 us  [on_device(): col_got = [lax.ppermute(col_msg, 'col', m) for m in ring_moves(n_col)]]
    ppermute x1, waiting for transfers between devices: 0.01 us -> 0.37 us  [on_device(): lax.ppermute(row_msg, 'row', xor_pairs(n_row, k))]
  transfers between devices with their start and end apart: 10 -> 8, of which waited for: 1 -> 3; matrix products, arithmetic and copies ran while one was open for 0% -> 0% of each run, Pallas kernels for 9% -> 10%
where the time goes in v4:
time: 21.9 us; the launch traced here: 21.7 us
  starting transfers between devices  11.4 us (52%)
  Pallas kernels  4.81 us (22%)
  waiting for transfers between devices  3.36 us (15%)
  other arithmetic  1.26 us (6%)
  between operations  0.79 us (4%)
    ppermute x3, starting transfers between devices, on_device(): sec_got.append(lax.ppermute(msg if move in ring else bulk, 'sec', move))  6.8 us
    ppermute x1, starting transfers between devices, on_device(): lax.ppermute(row_msg, 'row', xor_pairs(n_row, k))  3.03 us
    ppermute x3, waiting for transfers between devices, on_device(): sec_got.append(lax.ppermute(msg if move in ring else bulk, 'sec', move))  2.98 us
    pallas_call x1, Pallas kernels, on_device(): call(functools.partial(final_kernel, n_sec, section, tables['move']), [sh...  2.35 us
    pallas_call x1, Pallas kernels, on_device(): call(cells_kernel, shape((38, depth, wx, wy), F32), flops=LBM, moved=LBM)  1.7 us
    select_n x1, other arithmetic, on_device(): own = jnp.where(part == 2, whole_numbers.astype(F32), density)  1.25 us
    ppermute x2, starting transfers between devices, on_device(): col_got = [lax.ppermute(col_msg, 'col', m) for m in ring_moves(n_col)]  1.02 us
    ppermute x1, starting transfers between devices, on_device(): diag_got.append(lax.ppermute(col_msg, ('row', 'col'), move))  0.59 us
  transfers between devices with their start and end apart: 8, of which 3 were waited for; matrix products, arithmetic and copies ran while one was open for 0% of the time, Pallas kernels for 10%

profile of v4, /device:TPU:0, one launch (start us, length us, event | category | flops | bytes accessed | tf_op | source)
XLA Modules:
  0.0 21.7 jit_solution(3844198388721758902)
XLA Ops:
  0.6 0.0 copy-start.1
  0.6 0.0 copy-start.4
  0.7 0.0 copy-start.5
  0.7 0.0 copy-start.2
  0.7 0.0 copy-start.6
  0.7 0.0 copy-start.8
  0.7 0.0 copy-start.7
  0.7 0.0 copy-start.3
  0.7 0.0 copy-start
  0.8 1.3 %multiply_select_fusion.own_ref = f32[3,2,64,128]{3,2,1,0:T(8,128)S(1)} fusion(f32[2,2,64,128]{3,2,1,0:T(8,128)} %param.13, s32[2,64,128]{2,1,0:T(8,128)} %param.12, s32[64,128]{1,0:T(8,128)} %param.14, pred[3]{0:T(512)(128)(4,1)S(1)} %iota_compare_fusion), kind=kLoop, calls=%fused_computation | loop fusion | flops 344064 | bytes 425987 | tf_op jit(solution)/shard_map/jit(_where)/select_n | solution.py:560
  2.0 0.4 %shard_map.131 = (bf16[256,128]{1,0:T(8,128)(2,1)S(1)}, bf16[160,128]{1,0:T(8,128)(2,1)S(1)}, bf16[128,128]{1,0:T(8,128)(2,1)S(1)}) custom-call(f32[3,2,64,128]{3,2,1,0:T(8,128)S(1)} %multiply_select_fusion.own_ref), custom_call_target="tpu_custom_call" | custom-call | tf_op jit(solution)/shard_map/pallas_call | solution.py:561
  2.4 3.0 %collective-permute-start = (bf16[160,128]{1,0:T(8,128)(2,1)S(1)}, bf16[160,128]{1,0:T(8,128)(2,1)S(1)}, u32[]{:S(2)}, u32[]{:S(2)}) collective-permute-start(bf16[160,128]{1,0:T(8,128)(2,1)S(1)} %get-tuple-element.8.refs_0_.row_ref), channel_id=1, source_target_pairs={{0,4},{4,0},{1,5},{5,1},{2,6},{6,2},{3,7},{7,3},{8,12},{12,8},{9,1... | collective-permute-start | bytes 122888 | tf_op jit(solution)/shard_map/ppermute | solution.py:571
  5.4 0.6 %collective-permute-start.4 = (bf16[256,128]{1,0:T(8,128)(2,1)S(1)}, bf16[256,128]{1,0:T(8,128)(2,1)S(1)}, u32[]{:S(2)}, u32[]{:S(2)}) collective-permute-start(bf16[256,128]{1,0:T(8,128)(2,1)S(1)} %get-tuple-element.10), channel_id=1, source_target_pairs={{0,7},{1,6},{2,5},{3,4},{4,3},{5,2},{6,1},{7,0},{8,15},{9,14},{10,... | collective-permute-start | bytes 196616 | tf_op jit(solution)/shard_map/ppermute | solution.py:580
  6.0 0.7 %collective-permute-start.3 = (bf16[256,128]{1,0:T(8,128)(2,1)S(1)}, bf16[256,128]{1,0:T(8,128)(2,1)S(1)}, u32[]{:S(2)}, u32[]{:S(2)}) collective-permute-start(bf16[256,128]{1,0:T(8,128)(2,1)S(1)} %get-tuple-element.10), channel_id=1, source_target_pairs={{0,3},{1,2},{2,1},{3,0},{4,7},{5,6},{6,5},{7,4},{8,11},{9,10},{10,... | collective-permute-start | bytes 196616 | tf_op jit(solution)/shard_map/ppermute | solution.py:570
  6.7 0.3 %collective-permute-start.1 = (bf16[256,128]{1,0:T(8,128)(2,1)S(1)}, bf16[256,128]{1,0:T(8,128)(2,1)S(1)}, u32[]{:S(2)}, u32[]{:S(2)}) collective-permute-start(bf16[256,128]{1,0:T(8,128)(2,1)S(1)} %get-tuple-element.10), channel_id=1, source_target_pairs={{0,1},{1,0},{2,3},{3,2},{4,5},{5,4},{6,7},{7,6},{8,9},{9,8},{10,11... | collective-permute-start | bytes 196616 | tf_op jit(solution)/shard_map/ppermute | solution.py:570
  7.0 0.4 %collective-permute-done.refs_1_.refs_2_ = bf16[160,128]{1,0:T(8,128)(2,1)S(1)} collective-permute-done((bf16[160,128]{1,0:T(8,128)(2,1)S(1)}, bf16[160,128]{1,0:T(8,128)(2,1)S(1)}, u32[]{:S(2)}, u32[]{:S(2)}) %collective-permute-start) | collective-permute-done | bytes 40992 | tf_op jit(solution)/shard_map/ppermute | solution.py:571
  7.4 0.0 collective-permute-start.2
  7.4 0.2 shard_map.132.refs_5_.msg_own_ref
  7.6 3.2 %collective-permute-start.7 = (bf16[304,128]{1,0:T(8,128)(2,1)S(1)}, bf16[304,128]{1,0:T(8,128)(2,1)S(1)}, u32[]{:S(2)}, u32[]{:S(2)}) collective-permute-start(bf16[304,128]{1,0:T(8,128)(2,1)S(1)} %shard_map.132.refs_5_.msg_own_ref), channel_id=1, source_target_pairs={{0,16},{8,24},{16,0},{24,8},{1,17},{9,25},{17,1},{25,9},{2,18},{10... | collective-permute-start | bytes 233480 | tf_op jit(solution)/shard_map/ppermute | solution.py:607
  10.7 0.0 collective-permute-done.4.refs_4_
  10.7 0.0 collective-permute-done.3.refs_3_
  10.7 0.0 collective-permute-done.1.refs_0_
  10.7 0.0 collective-permute-done.2.refs_1_
  10.7 0.2 %shard_map.133 = (bf16[304,128]{1,0:T(8,128)(2,1)S(1)}, f32[12,72,128]{2,1,0:T(8,128)S(1)}, f32[72,128]{1,0:T(8,128)S(1)}) custom-call(f32[3,2,64,128]{3,2,1,0:T(8,128)S(1)} %multiply_select_fusion.own_ref, bf16[160,128]{1,0:T(8,128)(2,1)S(1)} %get-tuple-element.8.refs_0_.row_ref, bf16[256,128]{1,0:T(8,128)(2,1)S(1)} %collective-permute-done.1.refs_0_, ...), custom_call_target="tpu_custom_call" | custom-call | flops 16777216 | bytes 16777216 | tf_op jit(solution)/shard_map/pallas_call | solution.py:592
  11.0 3.6 %collective-permute-start.6 = (bf16[304,128]{1,0:T(8,128)(2,1)S(1)}, bf16[304,128]{1,0:T(8,128)(2,1)S(1)}, u32[]{:S(2)}, u32[]{:S(2)}) collective-permute-start(bf16[304,128]{1,0:T(8,128)(2,1)S(1)} %get-tuple-element.11), channel_id=1, source_target_pairs={{0,24},{8,16},{16,8},{24,0},{1,25},{9,17},{17,9},{25,1},{2,26},{10... | collective-permute-start | bytes 233480 | tf_op jit(solution)/shard_map/ppermute | solution.py:607
  14.6 0.0 collective-permute-start.5
  14.6 1.7 %shard_map.134.refs_4_ = f32[38,2,64,128]{3,2,1,0:T(8,128)S(1)} custom-call(f32[12,72,128]{2,1,0:T(8,128)S(1)} %get-tuple-element.13.dens_ref), custom_call_target="tpu_custom_call" | custom-call | flops 1024 | bytes 1024 | tf_op jit(solution)/shard_map/pallas_call | solution.py:609
  16.3 0.0 collective-permute-done.7.refs_2_
  16.3 1.7 %collective-permute-done.6.refs_1_ = bf16[304,128]{1,0:T(8,128)(2,1)S(1)} collective-permute-done((bf16[304,128]{1,0:T(8,128)(2,1)S(1)}, bf16[304,128]{1,0:T(8,128)(2,1)S(1)}, u32[]{:S(2)}, u32[]{:S(2)}) %collective-permute-start.6) | collective-permute-done | bytes 77856 | tf_op jit(solution)/shard_map/ppermute | solution.py:607
  18.1 1.2 %collective-permute-done.5.refs_0_ = bf16[304,128]{1,0:T(8,128)(2,1)S(1)} collective-permute-done((bf16[304,128]{1,0:T(8,128)(2,1)S(1)}, bf16[304,128]{1,0:T(8,128)(2,1)S(1)}, u32[]{:S(2)}, u32[]{:S(2)}) %collective-permute-start.5) | collective-permute-done | bytes 77856 | tf_op jit(solution)/shard_map/ppermute | solution.py:607
  19.3 0.0 copy-done.1
  19.4 2.3 %shard_map.135 = (f32[38,2,64,128]{3,2,1,0:T(8,128)}, f32[2,256]{1,0:T(2,128)}) custom-call(bf16[304,128]{1,0:T(8,128)(2,1)S(1)} %shard_map.132.refs_5_.msg_own_ref, bf16[304,128]{1,0:T(8,128)(2,1)S(1)} %collective-permute-done.5.refs_0_, bf16[304,128]{1,0:T(8,128)(2,1)S(1)} %collective-permute-done.6.refs_1_, ...), custom_call_target="tpu_custom_call" | custom-call | tf_op jit(solution)/shard_map/pallas_call | solution.py:618
  (9 shorter events, 0.0 us)
Async XLA Ops:
  0.6 18.7 %copy-start.1 = (f32[128,256]{1,0:T(8,128)S(1)}, f32[128,256]{1,0:T(8,128)}, u32[]{:S(2)}) copy-start(f32[128,256]{1,0:T(8,128)} %constant.36.clone.refs_13_) | copy-start | bytes 393220
  0.6 18.7 %copy-start.4 = (bf16[384,128]{1,0:T(8,128)(2,1)S(1)}, bf16[384,128]{1,0:T(8,128)(2,1)}, u32[]{:S(2)}) copy-start(bf16[384,128]{1,0:T(8,128)(2,1)} %constant.35.clone.refs_12_) | copy-start | bytes 294916
  0.7 18.7 %copy-start.5 = (f32[2,72,128]{2,1,0:T(8,128)S(1)}, f32[2,72,128]{2,1,0:T(8,128)}, u32[]{:S(2)}) copy-start(f32[2,72,128]{2,1,0:T(8,128)} %constant.34.clone.refs_11_) | copy-start | bytes 221188
  0.7 18.7 %copy-start.2 = (bf16[512,128]{1,0:T(8,128)(2,1)S(1)}, bf16[512,128]{1,0:T(8,128)(2,1)}, u32[]{:S(2)}) copy-start(bf16[512,128]{1,0:T(8,128)(2,1)} %constant.33.clone.refs_10_) | copy-start | bytes 393220
  0.7 18.7 %copy-start.6 = (f32[4,128]{1,0:T(4,128)S(1)}, f32[4,128]{1,0:T(4,128)}, u32[]{:S(2)}) copy-start(f32[4,128]{1,0:T(4,128)} %constant.32.clone.refs_9_) | copy-start | bytes 6148
  0.7 18.7 %copy-start.8 = (f32[1,256]{1,0:T(1,128)S(1)}, f32[1,256]{1,0:T(1,128)}, u32[]{:S(2)}) copy-start(f32[1,256]{1,0:T(1,128)} %constant.31.clone.refs_8_) | copy-start | bytes 3076
  0.7 18.6 %copy-start.7 = (f32[1,384]{1,0:T(1,128)S(1)}, f32[1,384]{1,0:T(1,128)}, u32[]{:S(2)}) copy-start(f32[1,384]{1,0:T(1,128)} %constant.30.clone.refs_7_) | copy-start | bytes 4612
  0.7 18.6 %copy-start.3 = (s32[72,384]{1,0:T(8,128)S(1)}, s32[72,384]{1,0:T(8,128)}, u32[]{:S(2)}) copy-start(s32[72,384]{1,0:T(8,128)} %constant.29.clone.refs_6_) | copy-start | bytes 331780
  0.7 18.6 %copy-start = (bf16[512,768]{1,0:T(8,128)(2,1)S(1)}, bf16[512,768]{1,0:T(8,128)(2,1)}, u32[]{:S(2)}) copy-start(bf16[512,768]{1,0:T(8,128)(2,1)} %constant.28.clone.refs_5_) | copy-start | bytes 2359300
  2.4 5.0 %collective-permute-start = (bf16[160,128]{1,0:T(8,128)(2,1)S(1)}, bf16[160,128]{1,0:T(8,128)(2,1)S(1)}, u32[]{:S(2)}, u32[]{:S(2)}) collective-permute-start(bf16[160,128]{1,0:T(8,128)(2,1)S(1)} %get-tuple-element.8.refs_0_.row_ref), channel_id=1, source_target_pairs={{0,4},{4,0},{1,5},{5,1},{2,6},{6,2},{3,7},{7,3},{8,12},{12,8},{9,1... | collective-permute-start | bytes 122888 | tf_op jit(solution)/shard_map/ppermute | solution.py:571
  5.4 5.3 %collective-permute-start.4 = (bf16[256,128]{1,0:T(8,128)(2,1)S(1)}, bf16[256,128]{1,0:T(8,128)(2,1)S(1)}, u32[]{:S(2)}, u32[]{:S(2)}) collective-permute-start(bf16[256,128]{1,0:T(8,128)(2,1)S(1)} %get-tuple-element.10), channel_id=1, source_target_pairs={{0,7},{1,6},{2,5},{3,4},{4,3},{5,2},{6,1},{7,0},{8,15},{9,14},{10,... | collective-permute-start | bytes 196616 | tf_op jit(solution)/shard_map/ppermute | solution.py:580
  6.0 4.7 %collective-permute-start.3 = (bf16[256,128]{1,0:T(8,128)(2,1)S(1)}, bf16[256,128]{1,0:T(8,128)(2,1)S(1)}, u32[]{:S(2)}, u32[]{:S(2)}) collective-permute-start(bf16[256,128]{1,0:T(8,128)(2,1)S(1)} %get-tuple-element.10), channel_id=1, source_target_pairs={{0,3},{1,2},{2,1},{3,0},{4,7},{5,6},{6,5},{7,4},{8,11},{9,10},{10,... | collective-permute-start | bytes 196616 | tf_op jit(solution)/shard_map/ppermute | solution.py:570
  6.7 4.0 %collective-permute-start.1 = (bf16[256,128]{1,0:T(8,128)(2,1)S(1)}, bf16[256,128]{1,0:T(8,128)(2,1)S(1)}, u32[]{:S(2)}, u32[]{:S(2)}) collective-permute-start(bf16[256,128]{1,0:T(8,128)(2,1)S(1)} %get-tuple-element.10), channel_id=1, source_target_pairs={{0,1},{1,0},{2,3},{3,2},{4,5},{5,4},{6,7},{7,6},{8,9},{9,8},{10,11... | collective-permute-start | bytes 196616 | tf_op jit(solution)/shard_map/ppermute | solution.py:570
  7.4 3.3 %collective-permute-start.2 = (bf16[160,128]{1,0:T(8,128)(2,1)S(1)}, bf16[160,128]{1,0:T(8,128)(2,1)S(1)}, u32[]{:S(2)}, u32[]{:S(2)}) collective-permute-start(bf16[160,128]{1,0:T(8,128)(2,1)S(1)} %collective-permute-done.refs_1_.refs_2_), channel_id=1, source_target_pairs={{0,1},{1,0},{2,3},{3,2},{4,5},{5,4},{6,7},{7,6},{8,9},{9,8},{10,11... | collective-permute-start | bytes 122888 | tf_op jit(solution)/shard_map/ppermute | solution.py:577
  7.6 8.8 %collective-permute-start.7 = (bf16[304,128]{1,0:T(8,128)(2,1)S(1)}, bf16[304,128]{1,0:T(8,128)(2,1)S(1)}, u32[]{:S(2)}, u32[]{:S(2)}) collective-permute-start(bf16[304,128]{1,0:T(8,128)(2,1)S(1)} %shard_map.132.refs_5_.msg_own_ref), channel_id=1, source_target_pairs={{0,16},{8,24},{16,0},{24,8},{1,17},{9,25},{17,1},{25,9},{2,18},{10... | collective-permute-start | bytes 233480 | tf_op jit(solution)/shard_map/ppermute | solution.py:607
  11.0 7.1 %collective-permute-start.6 = (bf16[304,128]{1,0:T(8,128)(2,1)S(1)}, bf16[304,128]{1,0:T(8,128)(2,1)S(1)}, u32[]{:S(2)}, u32[]{:S(2)}) collective-permute-start(bf16[304,128]{1,0:T(8,128)(2,1)S(1)} %get-tuple-element.11), channel_id=1, source_target_pairs={{0,24},{8,16},{16,8},{24,0},{1,25},{9,17},{17,9},{25,1},{2,26},{10... | collective-permute-start | bytes 233480 | tf_op jit(solution)/shard_map/ppermute | solution.py:607
  14.6 4.7 %collective-permute-start.5 = (bf16[304,128]{1,0:T(8,128)(2,1)S(1)}, bf16[304,128]{1,0:T(8,128)(2,1)S(1)}, u32[]{:S(2)}, u32[]{:S(2)}) collective-permute-start(bf16[304,128]{1,0:T(8,128)(2,1)S(1)} %get-tuple-element.11), channel_id=1, source_target_pairs={{0,8},{8,0},{16,24},{24,16},{1,9},{9,1},{17,25},{25,17},{2,10},{10... | collective-permute-start | bytes 233480 | tf_op jit(solution)/shard_map/ppermute | solution.py:607

commit v5 on v4

--- a/solution.py
+++ b/solution.py
@@ -16,7 +16,8 @@
 LBM = 1 << 10
 ENDS = (10, 19, 29, 38)
 FIRST_ROUND = (("col", 0), ("diag", 0), ("row", 1), ("col", 1), ("diag", 1))
-SWAPS = {4: (1, 3, 2)}
+SWAPS = {4: (3, 1, 2)}
+EARLY = {4: (1, 2)}
 TOP = 40
 ROWS = 72
 F32 = jnp.float32
@@ -188,15 +189,22 @@
     return jnp.where(is_cos, cos, -sin).astype(BF16)
 
 
-def pack_kernel(n_row, n_sec, per, own_ref, col_ref, row_ref, table_ref):
+def planes_kernel(n_row, own_ref, col_ref, table_ref):
+    _, depth, wx, _ = own_ref.shape
+    for c in range(2):
+        for z in range(depth):
+            at = (c * depth + z) * wx
+            col_ref[at : at + wx] = own_ref[c, z].astype(BF16)
+    table_ref[...] = x_table(lax.axis_index("row"), n_row, wx)
+
+
+def pack_kernel(n_row, n_sec, per, own_ref, row_ref):
     _, depth, wx, wy = own_ref.shape
     edges = []
     densities = [[own_ref[c, z] for z in range(depth)] for c in range(2)]
     for c in range(2):
         for z in range(depth):
             tile = densities[c][z]
-            at = (c * depth + z) * wx
-            col_ref[at : at + wx] = tile.astype(BF16)
             edges += [tile[0:2], tile[wx - 2 : wx]]
     for z in range(depth):
         row_ref[z * wx : (z + 1) * wx] = (densities[0][z] - densities[1][z]).astype(BF16)
@@ -204,8 +212,6 @@
     at = depth * wx
     count = edge.shape[0]
     row_ref[at : at + count] = edge
-
-    table_ref[...] = x_table(lax.axis_index("row"), n_row, wx)
 
     row, sec = lax.axis_index("row"), lax.axis_index("sec")
     square, root = shell_root(row * wx, sec * wy, wx * n_row, wy * n_sec, wx, wy)
@@ -260,7 +266,7 @@
     _, depth, wx, wy = own_ref.shape
     col_moves, row_moves = len(ring_moves(n_col)), len(ring_moves(n_row))
     by_name, refs = dict(zip(names, refs)), refs[len(names) :]
-    bulk_ref, msg_ref, dens_ref, lanes_ref = refs
+    bulk_ref, msg_ref, strip_ref, dens_ref, lanes_ref = refs
     col_refs = [by_name["col", i] for i in range(col_moves)]
     row_refs = [row_ref] + [by_name["row", k] for k in range(1, n_row)]
     diag_refs = [by_name["diag", i] for i in range(col_moves * row_moves)]
@@ -321,6 +327,8 @@
     lanes_ref[...] = strips + pltpu.roll(strips, 4, 1)
     lower = jnp.concatenate([strips[TOP:], jnp.zeros((2 * TOP - ROWS, wy), F32)], axis=0)
     folded = strips[:TOP] + pltpu.roll(lower, 4, 1)
+    gap = jnp.zeros((strip_ref.shape[0] - TOP, wy), F32)
+    strip_ref[...] = jnp.concatenate([folded, gap], axis=0).astype(BF16)
     at = msg_ref.shape[0] - whole(section + TOP)
     msg_ref[:at] = bulk_ref[:at]
     parts = [bulk_ref[at : at + whole(section)].astype(F32)[:section], folded]
@@ -389,7 +397,10 @@
 def set_ends(n_sec, start, at, msg_refs, lanes_ref, cells_ref, out_hbm, out_ref, sems):
     _, depth, wx, wy = out_ref.shape
     layers = depth + 4
-    strips = [r[start:].astype(F32)[at - start :][:TOP] for r in msg_refs]
+    strips = [
+        r[:].astype(F32)[:TOP] if r.shape[0] < start else r[start:].astype(F32)[at - start :][:TOP]
+        for r in msg_refs
+    ]
     index = lax.axis_index("sec")
     prev_which, next_which = ring_pick(n_sec, index)
     before, after = choose(strips, prev_which), choose(strips, next_which)
@@ -436,7 +447,14 @@
 def final_kernel(n_sec, section, move, msg_own_ref, *refs):
     msg_refs = [msg_own_ref] + [refs[swap_order(n_sec).index(k)] for k in range(1, n_sec)]
     refs = refs[n_sec - 1 :]
-    ring = [msg_refs[move_[0][1]] for move_ in ring_moves(n_sec)]
+    ring = []
+    for move_ in ring_moves(n_sec):
+        k = move_[0][1]
+        if k in EARLY.get(n_sec, ()):
+            ring.append(refs[0])
+            refs = refs[1:]
+        else:
+            ring.append(msg_refs[k])
     (strips_ref, cells_ref), refs = refs[:2], refs[2:]
     (table_ref, move_ref, mult_ref, counts_ref, put_ref, lanes_ref, row_ref, col_ref, step_ref,
      out_hbm, spec_hbm, lhs_ref, mark_ref, part_ref, out_ref, spec_ref, sems) = refs
@@ -558,13 +576,13 @@
     whole_numbers = jnp.where(part == 2, shells[None, None], labels[None] ^ part)
     density = jnp.where(whole_numbers == 1, F32(1.0), F32(0.2)) * factor
     own = jnp.where(part == 2, whole_numbers.astype(F32), density)
-    col_msg, row_msg, table_x = call(
+    row_msg = call(
         functools.partial(pack_kernel, n_row, n_sec, per),
-        [
-            shape((2 * depth * wx, wy), BF16),
-            shape((depth * wx + count + whole(section), wy), BF16),
-            shape((full_x, full_x), BF16),
-        ],
+        shape((depth * wx + count + whole(section), wy), BF16),
+    )(own)
+    col_msg, table_x = call(
+        functools.partial(planes_kernel, n_row),
+        [shape((2 * depth * wx, wy), BF16), shape((full_x, full_x), BF16)],
     )(own)
 
     col_got = [lax.ppermute(col_msg, "col", m) for m in ring_moves(n_col)]
@@ -589,10 +607,11 @@
         functools.partial(half_kernel, depth, wx, n_row), shape((at + whole(section + TOP), wy), BF16),
         flops=1 << 27, moved=1 << 24
     )(row_msg, *row_got, table_x)
-    msg, dens, lanes_own = call(
+    msg, strip, dens, lanes_own = call(
         functools.partial(middle_kernel, n_row, n_col, section, tuple(names)),
         [
             shape((at + whole(section + TOP), wy), BF16),
+            shape((whole(TOP), wy), BF16),
             shape((2 * layers, ROWS, wy), F32),
             shape((ROWS, wy), F32),
         ],
@@ -601,10 +620,15 @@
     )(own, row_msg, *[got[name] for name in names], bulk)
 
     ring = ring_moves(n_sec)
-    sec_got = []
+    early = EARLY.get(n_sec, ())
+    sec_got, strip_got = [], []
     for k in swap_order(n_sec):
         move = xor_pairs(n_sec, k)
-        sec_got.append(lax.ppermute(msg if move in ring else bulk, "sec", move))
+        with_columns = move in ring and k not in early
+        sec_got.append(lax.ppermute(msg if with_columns else bulk, "sec", move))
+    for move in ring:
+        if move[0][1] in early:
+            strip_got.append(lax.ppermute(strip, "sec", move))
 
     cells = call(
         cells_kernel,
@@ -627,7 +651,7 @@
             pltpu.SemaphoreType.DMA((len(ENDS) + 1,)),
         ],
         out_specs=[pl.BlockSpec(memory_space=pltpu.HBM)] * 2,
-    )(bulk, *sec_got, lanes_own, cells, tables["table_y"], tables["move"].astype(np.int32),
+    )(bulk, *sec_got, *strip_got, lanes_own, cells, tables["table_y"], tables["move"].astype(np.int32),
       *[tables[name] for name in names])
 
 

time: 21.9 us -> 21.5 us (0.982)
  waiting for transfers between devices: 3.36 us -> 1.7 us
  starting transfers between devices: 11.4 us -> 12.7 us
    ppermute x3 -> x4, waiting for transfers between devices: 2.98 us -> 1.65 us  [the longest x1 1.64 us: on_device(): strip_got.append(lax.ppermute(strip, 'sec', move))]
    ppermute x3 -> x4, starting transfers between devices: 6.8 us -> 7.94 us  [the longest x3 7.26 us: on_device(): sec_got.append(lax.ppermute(msg if with_columns else bulk, 'sec', move))]
    ppermute x1, waiting for transfers between devices: 0.37 us -> 0.04 us  [on_device(): lax.ppermute(row_msg, 'row', xor_pairs(n_row, k))]
  transfers between devices with their start and end apart: 8 -> 9, of which waited for: 3 -> 1; matrix products, arithmetic and copies ran while one was open for 0% -> 0% of each run, Pallas kernels for 10% -> 11%
where the time goes in v5:
time: 21.5 us; the launch traced here: 21.3 us
  starting transfers between devices  12.7 us (59%)
  Pallas kernels  4.78 us (22%)
  waiting for transfers between devices  1.7 us (8%)
  other arithmetic  1.26 us (6%)
  between operations  0.8 us (4%)
    ppermute x3, starting transfers between devices, on_device(): sec_got.append(lax.ppermute(msg if with_columns else bulk, 'sec', move))  7.26 us
    ppermute x1, starting transfers between devices, on_device(): lax.ppermute(row_msg, 'row', xor_pairs(n_row, k))  3.03 us
    pallas_call x1, Pallas kernels, on_device(): call(functools.partial(final_kernel, n_sec, section, tables['move']), [sh...  2.31 us
    pallas_call x1, Pallas kernels, on_device(): call(cells_kernel, shape((38, depth, wx, wy), F32), flops=LBM, moved=LBM)  1.7 us
    ppermute x1, waiting for transfers between devices, on_device(): strip_got.append(lax.ppermute(strip, 'sec', move))  1.64 us
    select_n x1, other arithmetic, on_device(): own = jnp.where(part == 2, whole_numbers.astype(F32), density)  1.25 us
    ppermute x2, starting transfers between devices, on_device(): col_got = [lax.ppermute(col_msg, 'col', m) for m in ring_moves(n_col)]  1.09 us
    ppermute x1, starting transfers between devices, on_device(): strip_got.append(lax.ppermute(strip, 'sec', move))  0.68 us
  transfers between devices with their start and end apart: 9, of which 1 were waited for; matrix products, arithmetic and copies ran while one was open for 0% of the time, Pallas kernels for 11%

profile of v5, /device:TPU:0, one launch (start us, length us, event | category | flops | bytes accessed | tf_op | source)
XLA Modules:
  0.0 21.3 jit_solution(11828610018427491094)
XLA Ops:
  0.6 0.0 copy-start.1
  0.6 0.0 copy-start.4
  0.7 0.0 copy-start.5
  0.7 0.0 copy-start.2
  0.7 0.0 copy-start.6
  0.7 0.0 copy-start.8
  0.7 0.0 copy-start.7
  0.7 0.0 copy-start.3
  0.7 0.0 copy-start
  0.8 1.3 %multiply_select_fusion.own_ref = f32[3,2,64,128]{3,2,1,0:T(8,128)S(1)} fusion(f32[2,2,64,128]{3,2,1,0:T(8,128)} %param.13, s32[2,64,128]{2,1,0:T(8,128)} %param.12, s32[64,128]{1,0:T(8,128)} %param.14, pred[3]{0:T(512)(128)(4,1)S(1)} %iota_compare_fusion), kind=kLoop, calls=%fused_computation | loop fusion | flops 344064 | bytes 425987 | tf_op jit(solution)/shard_map/jit(_where)/select_n | solution.py:578
  2.0 0.2 shard_map.131.refs_0_.row_ref
  2.2 3.0 %collective-permute-start = (bf16[160,128]{1,0:T(8,128)(2,1)S(1)}, bf16[160,128]{1,0:T(8,128)(2,1)S(1)}, u32[]{:S(2)}, u32[]{:S(2)}) collective-permute-start(bf16[160,128]{1,0:T(8,128)(2,1)S(1)} %shard_map.131.refs_0_.row_ref), channel_id=1, source_target_pairs={{0,4},{4,0},{1,5},{5,1},{2,6},{6,2},{3,7},{7,3},{8,12},{12,8},{9,1... | collective-permute-start | bytes 122888 | tf_op jit(solution)/shard_map/ppermute | solution.py:589
  5.2 0.2 shard_map.132
  5.4 0.7 %collective-permute-start.4 = (bf16[256,128]{1,0:T(8,128)(2,1)S(1)}, bf16[256,128]{1,0:T(8,128)(2,1)S(1)}, u32[]{:S(2)}, u32[]{:S(2)}) collective-permute-start(bf16[256,128]{1,0:T(8,128)(2,1)S(1)} %get-tuple-element.9), channel_id=1, source_target_pairs={{0,7},{1,6},{2,5},{3,4},{4,3},{5,2},{6,1},{7,0},{8,15},{9,14},{10,... | collective-permute-start | bytes 196616 | tf_op jit(solution)/shard_map/ppermute | solution.py:598
  6.1 0.6 %collective-permute-start.3 = (bf16[256,128]{1,0:T(8,128)(2,1)S(1)}, bf16[256,128]{1,0:T(8,128)(2,1)S(1)}, u32[]{:S(2)}, u32[]{:S(2)}) collective-permute-start(bf16[256,128]{1,0:T(8,128)(2,1)S(1)} %get-tuple-element.9), channel_id=1, source_target_pairs={{0,3},{1,2},{2,1},{3,0},{4,7},{5,6},{6,5},{7,4},{8,11},{9,10},{10,... | collective-permute-start | bytes 196616 | tf_op jit(solution)/shard_map/ppermute | solution.py:588
  6.7 0.5 %collective-permute-start.1 = (bf16[256,128]{1,0:T(8,128)(2,1)S(1)}, bf16[256,128]{1,0:T(8,128)(2,1)S(1)}, u32[]{:S(2)}, u32[]{:S(2)}) collective-permute-start(bf16[256,128]{1,0:T(8,128)(2,1)S(1)} %get-tuple-element.9), channel_id=1, source_target_pairs={{0,1},{1,0},{2,3},{3,2},{4,5},{5,4},{6,7},{7,6},{8,9},{9,8},{10,11... | collective-permute-start | bytes 196616 | tf_op jit(solution)/shard_map/ppermute | solution.py:588
  7.2 0.0 collective-permute-done.refs_1_.refs_2_
  7.2 0.0 collective-permute-start.2
  7.2 0.2 shard_map.133.refs_5_.msg_own_ref
  7.4 3.2 %collective-permute-start.7 = (bf16[304,128]{1,0:T(8,128)(2,1)S(1)}, bf16[304,128]{1,0:T(8,128)(2,1)S(1)}, u32[]{:S(2)}, u32[]{:S(2)}) collective-permute-start(bf16[304,128]{1,0:T(8,128)(2,1)S(1)} %shard_map.133.refs_5_.msg_own_ref), channel_id=1, source_target_pairs={{0,16},{8,24},{16,0},{24,8},{1,17},{9,25},{17,1},{25,9},{2,18},{10... | collective-permute-start | bytes 233480 | tf_op jit(solution)/shard_map/ppermute | solution.py:628
  10.5 0.0 collective-permute-done.4.refs_4_
  10.5 1.6 %collective-permute-start.6 = (bf16[304,128]{1,0:T(8,128)(2,1)S(1)}, bf16[304,128]{1,0:T(8,128)(2,1)S(1)}, u32[]{:S(2)}, u32[]{:S(2)}) collective-permute-start(bf16[304,128]{1,0:T(8,128)(2,1)S(1)} %shard_map.133.refs_5_.msg_own_ref), channel_id=1, source_target_pairs={{0,8},{8,0},{16,24},{24,16},{1,9},{9,1},{17,25},{25,17},{2,10},{10... | collective-permute-start | bytes 233480 | tf_op jit(solution)/shard_map/ppermute | solution.py:628
  12.1 0.0 collective-permute-done.3.refs_3_
  12.1 0.2 %shard_map.134 = (bf16[304,128]{1,0:T(8,128)(2,1)S(1)}, bf16[48,128]{1,0:T(8,128)(2,1)S(1)}, f32[12,72,128]{2,1,0:T(8,128)S(1)}, f32[72,128]{1,0:T(8,128)S(1)}) custom-call(f32[3,2,64,128]{3,2,1,0:T(8,128)S(1)} %multiply_select_fusion.own_ref, bf16[160,128]{1,0:T(8,128)(2,1)S(1)} %shard_map.131.refs_0_.row_ref, ...), custom_call_target="tpu_custom_call" | custom-call | flops 16777216 | bytes 16777216 | tf_op jit(solution)/shard_map/pallas_call | solution.py:610
  12.3 2.5 %collective-permute-start.5 = (bf16[304,128]{1,0:T(8,128)(2,1)S(1)}, bf16[304,128]{1,0:T(8,128)(2,1)S(1)}, u32[]{:S(2)}, u32[]{:S(2)}) collective-permute-start(bf16[304,128]{1,0:T(8,128)(2,1)S(1)} %get-tuple-element.10), channel_id=1, source_target_pairs={{0,24},{8,16},{16,8},{24,0},{1,25},{9,17},{17,9},{25,1},{2,26},{10... | collective-permute-start | bytes 233480 | tf_op jit(solution)/shard_map/ppermute | solution.py:628
  14.9 0.7 %collective-permute-start.8 = (bf16[48,128]{1,0:T(8,128)(2,1)S(1)}, bf16[48,128]{1,0:T(8,128)(2,1)S(1)}, u32[]{:S(2)}, u32[]{:S(2)}) collective-permute-start(bf16[48,128]{1,0:T(8,128)(2,1)S(1)} %get-tuple-element.11), channel_id=1, source_target_pairs={{0,8},{8,0},{16,24},{24,16},{1,9},{9,1},{17,25},{25,17},{2,10},{10... | collective-permute-start | bytes 36872 | tf_op jit(solution)/shard_map/ppermute | solution.py:631
  15.6 1.7 %shard_map.135.refs_5_ = f32[38,2,64,128]{3,2,1,0:T(8,128)S(1)} custom-call(f32[12,72,128]{2,1,0:T(8,128)S(1)} %get-tuple-element.13.dens_ref), custom_call_target="tpu_custom_call" | custom-call | flops 1024 | bytes 1024 | tf_op jit(solution)/shard_map/pallas_call | solution.py:633
  17.3 1.6 %collective-permute-done.8.refs_3_ = bf16[48,128]{1,0:T(8,128)(2,1)S(1)} collective-permute-done((bf16[48,128]{1,0:T(8,128)(2,1)S(1)}, bf16[48,128]{1,0:T(8,128)(2,1)S(1)}, u32[]{:S(2)}, u32[]{:S(2)}) %collective-permute-start.8) | collective-permute-done | bytes 12320 | tf_op jit(solution)/shard_map/ppermute | solution.py:631
  18.9 0.0 collective-permute-done.7.refs_2_
  18.9 0.0 collective-permute-done.6.refs_1_
  18.9 0.0 collective-permute-done.5.refs_0_
  19.0 2.3 %shard_map.136 = (f32[38,2,64,128]{3,2,1,0:T(8,128)}, f32[2,256]{1,0:T(2,128)}) custom-call(bf16[304,128]{1,0:T(8,128)(2,1)S(1)} %shard_map.133.refs_5_.msg_own_ref, bf16[304,128]{1,0:T(8,128)(2,1)S(1)} %collective-permute-done.5.refs_0_, bf16[304,128]{1,0:T(8,128)(2,1)S(1)} %collective-permute-done.6.refs_1_, ...), custom_call_target="tpu_custom_call" | custom-call | tf_op jit(solution)/shard_map/pallas_call | solution.py:642
  (12 shorter events, 0.0 us)
Async XLA Ops:
  0.6 18.3 %copy-start.1 = (f32[128,256]{1,0:T(8,128)S(1)}, f32[128,256]{1,0:T(8,128)}, u32[]{:S(2)}) copy-start(f32[128,256]{1,0:T(8,128)} %constant.36.clone.refs_14_) | copy-start | bytes 393220
  0.6 18.3 %copy-start.4 = (bf16[384,128]{1,0:T(8,128)(2,1)S(1)}, bf16[384,128]{1,0:T(8,128)(2,1)}, u32[]{:S(2)}) copy-start(bf16[384,128]{1,0:T(8,128)(2,1)} %constant.35.clone.refs_13_) | copy-start | bytes 294916
  0.7 18.3 %copy-start.5 = (f32[2,72,128]{2,1,0:T(8,128)S(1)}, f32[2,72,128]{2,1,0:T(8,128)}, u32[]{:S(2)}) copy-start(f32[2,72,128]{2,1,0:T(8,128)} %constant.34.clone.refs_12_) | copy-start | bytes 221188
  0.7 18.3 %copy-start.2 = (bf16[512,128]{1,0:T(8,128)(2,1)S(1)}, bf16[512,128]{1,0:T(8,128)(2,1)}, u32[]{:S(2)}) copy-start(bf16[512,128]{1,0:T(8,128)(2,1)} %constant.33.clone.refs_11_) | copy-start | bytes 393220
  0.7 18.3 %copy-start.6 = (f32[4,128]{1,0:T(4,128)S(1)}, f32[4,128]{1,0:T(4,128)}, u32[]{:S(2)}) copy-start(f32[4,128]{1,0:T(4,128)} %constant.32.clone.refs_10_) | copy-start | bytes 6148
  0.7 18.3 %copy-start.8 = (f32[1,256]{1,0:T(1,128)S(1)}, f32[1,256]{1,0:T(1,128)}, u32[]{:S(2)}) copy-start(f32[1,256]{1,0:T(1,128)} %constant.31.clone.refs_9_) | copy-start | bytes 3076
  0.7 18.3 %copy-start.7 = (f32[1,384]{1,0:T(1,128)S(1)}, f32[1,384]{1,0:T(1,128)}, u32[]{:S(2)}) copy-start(f32[1,384]{1,0:T(1,128)} %constant.30.clone.refs_8_) | copy-start | bytes 4612
  0.7 18.3 %copy-start.3 = (s32[72,384]{1,0:T(8,128)S(1)}, s32[72,384]{1,0:T(8,128)}, u32[]{:S(2)}) copy-start(s32[72,384]{1,0:T(8,128)} %constant.29.clone.refs_7_) | copy-start | bytes 331780
  0.7 18.3 %copy-start = (bf16[512,768]{1,0:T(8,128)(2,1)S(1)}, bf16[512,768]{1,0:T(8,128)(2,1)}, u32[]{:S(2)}) copy-start(bf16[512,768]{1,0:T(8,128)(2,1)} %constant.28.clone.refs_6_) | copy-start | bytes 2359300
  2.2 5.0 %collective-permute-start = (bf16[160,128]{1,0:T(8,128)(2,1)S(1)}, bf16[160,128]{1,0:T(8,128)(2,1)S(1)}, u32[]{:S(2)}, u32[]{:S(2)}) collective-permute-start(bf16[160,128]{1,0:T(8,128)(2,1)S(1)} %shard_map.131.refs_0_.row_ref), channel_id=1, source_target_pairs={{0,4},{4,0},{1,5},{5,1},{2,6},{6,2},{3,7},{7,3},{8,12},{12,8},{9,1... | collective-permute-start | bytes 122888 | tf_op jit(solution)/shard_map/ppermute | solution.py:589
  5.4 5.1 %collective-permute-start.4 = (bf16[256,128]{1,0:T(8,128)(2,1)S(1)}, bf16[256,128]{1,0:T(8,128)(2,1)S(1)}, u32[]{:S(2)}, u32[]{:S(2)}) collective-permute-start(bf16[256,128]{1,0:T(8,128)(2,1)S(1)} %get-tuple-element.9), channel_id=1, source_target_pairs={{0,7},{1,6},{2,5},{3,4},{4,3},{5,2},{6,1},{7,0},{8,15},{9,14},{10,... | collective-permute-start | bytes 196616 | tf_op jit(solution)/shard_map/ppermute | solution.py:598
  6.1 6.0 %collective-permute-start.3 = (bf16[256,128]{1,0:T(8,128)(2,1)S(1)}, bf16[256,128]{1,0:T(8,128)(2,1)S(1)}, u32[]{:S(2)}, u32[]{:S(2)}) collective-permute-start(bf16[256,128]{1,0:T(8,128)(2,1)S(1)} %get-tuple-element.9), channel_id=1, source_target_pairs={{0,3},{1,2},{2,1},{3,0},{4,7},{5,6},{6,5},{7,4},{8,11},{9,10},{10,... | collective-permute-start | bytes 196616 | tf_op jit(solution)/shard_map/ppermute | solution.py:588
  6.7 5.4 %collective-permute-start.1 = (bf16[256,128]{1,0:T(8,128)(2,1)S(1)}, bf16[256,128]{1,0:T(8,128)(2,1)S(1)}, u32[]{:S(2)}, u32[]{:S(2)}) collective-permute-start(bf16[256,128]{1,0:T(8,128)(2,1)S(1)} %get-tuple-element.9), channel_id=1, source_target_pairs={{0,1},{1,0},{2,3},{3,2},{4,5},{5,4},{6,7},{7,6},{8,9},{9,8},{10,11... | collective-permute-start | bytes 196616 | tf_op jit(solution)/shard_map/ppermute | solution.py:588
  7.2 4.9 %collective-permute-start.2 = (bf16[160,128]{1,0:T(8,128)(2,1)S(1)}, bf16[160,128]{1,0:T(8,128)(2,1)S(1)}, u32[]{:S(2)}, u32[]{:S(2)}) collective-permute-start(bf16[160,128]{1,0:T(8,128)(2,1)S(1)} %collective-permute-done.refs_1_.refs_2_), channel_id=1, source_target_pairs={{0,1},{1,0},{2,3},{3,2},{4,5},{5,4},{6,7},{7,6},{8,9},{9,8},{10,11... | collective-permute-start | bytes 122888 | tf_op jit(solution)/shard_map/ppermute | solution.py:595
  7.4 11.5 %collective-permute-start.7 = (bf16[304,128]{1,0:T(8,128)(2,1)S(1)}, bf16[304,128]{1,0:T(8,128)(2,1)S(1)}, u32[]{:S(2)}, u32[]{:S(2)}) collective-permute-start(bf16[304,128]{1,0:T(8,128)(2,1)S(1)} %shard_map.133.refs_5_.msg_own_ref), channel_id=1, source_target_pairs={{0,16},{8,24},{16,0},{24,8},{1,17},{9,25},{17,1},{25,9},{2,18},{10... | collective-permute-start | bytes 233480 | tf_op jit(solution)/shard_map/ppermute | solution.py:628
  10.5 8.4 %collective-permute-start.6 = (bf16[304,128]{1,0:T(8,128)(2,1)S(1)}, bf16[304,128]{1,0:T(8,128)(2,1)S(1)}, u32[]{:S(2)}, u32[]{:S(2)}) collective-permute-start(bf16[304,128]{1,0:T(8,128)(2,1)S(1)} %shard_map.133.refs_5_.msg_own_ref), channel_id=1, source_target_pairs={{0,8},{8,0},{16,24},{24,16},{1,9},{9,1},{17,25},{25,17},{2,10},{10... | collective-permute-start | bytes 233480 | tf_op jit(solution)/shard_map/ppermute | solution.py:628
  12.3 6.6 %collective-permute-start.5 = (bf16[304,128]{1,0:T(8,128)(2,1)S(1)}, bf16[304,128]{1,0:T(8,128)(2,1)S(1)}, u32[]{:S(2)}, u32[]{:S(2)}) collective-permute-start(bf16[304,128]{1,0:T(8,128)(2,1)S(1)} %get-tuple-element.10), channel_id=1, source_target_pairs={{0,24},{8,16},{16,8},{24,0},{1,25},{9,17},{17,9},{25,1},{2,26},{10... | collective-permute-start | bytes 233480 | tf_op jit(solution)/shard_map/ppermute | solution.py:628
  14.9 4.0 %collective-permute-start.8 = (bf16[48,128]{1,0:T(8,128)(2,1)S(1)}, bf16[48,128]{1,0:T(8,128)(2,1)S(1)}, u32[]{:S(2)}, u32[]{:S(2)}) collective-permute-start(bf16[48,128]{1,0:T(8,128)(2,1)S(1)} %get-tuple-element.11), channel_id=1, source_target_pairs={{0,8},{8,0},{16,24},{24,16},{1,9},{9,1},{17,25},{25,17},{2,10},{10... | collective-permute-start | bytes 36872 | tf_op jit(solution)/shard_map/ppermute | solution.py:631

commit v6 on v5

--- a/solution.py
+++ b/solution.py
@@ -148,18 +148,25 @@
         mark_col[ay, entry] = 1
         step[entry, root[kx, ky]] += 1
         step[entry, root[kx, ky] - 1] -= 1
+    parts = (mult_y, counts[None, :], put, mark_row.reshape(2 * hrows, total), step, move)
+    wide = max(p.shape[1] for p in parts)
+    small, places = [], []
+    for part in parts:
+        rows = 8 * (-(-part.shape[0] // 8))
+        places.append(sum(p.shape[0] for p in small))
+        filled = np.zeros((rows, wide), np.float32)
+        filled[: part.shape[0], : part.shape[1]] = part
+        small.append(filled)
+    columns = np.zeros((full_y, total))
+    columns[:lanes] = mark_col
     return dict(
         per=per,
         section=section,
-        table_y=bf16_table(table_y),
+        total=total,
         move=move,
-        mult_y=mult_y.astype(np.float32),
-        counts=counts.astype(np.float32)[None, :],
-        put=np.asarray(put, np.float32),
-        lanes_of=bf16_table(lanes_of.T),
-        mark_row=np.asarray(mark_row, np.float32),
-        mark_col=bf16_table(mark_col),
-        step=np.asarray(step, np.float32),
+        places=tuple(places),
+        small=np.concatenate(small, axis=0),
+        large=np.concatenate([table_y, lanes_of.T, columns], axis=1).astype(ml_dtypes.bfloat16),
     )
 
 
@@ -444,7 +451,7 @@
     return copies
 
 
-def final_kernel(n_sec, section, move, msg_own_ref, *refs):
+def final_kernel(n_sec, section, places, total, move, msg_own_ref, *refs):
     msg_refs = [msg_own_ref] + [refs[swap_order(n_sec).index(k)] for k in range(1, n_sec)]
     refs = refs[n_sec - 1 :]
     ring = []
@@ -456,29 +463,31 @@
         else:
             ring.append(msg_refs[k])
     (strips_ref, cells_ref), refs = refs[:2], refs[2:]
-    (table_ref, move_ref, mult_ref, counts_ref, put_ref, lanes_ref, row_ref, col_ref, step_ref,
+    (large_ref, small_ref,
      out_hbm, spec_hbm, lhs_ref, mark_ref, part_ref, out_ref, spec_ref, sems) = refs
     depth = spec_ref.shape[0]
     sec = lax.axis_index("sec")
-    full_y, lanes = table_ref.shape[0], table_ref.shape[1] // 2
+    full_y, lanes = large_ref.shape[0], move.shape[1]
     wy = full_y // n_sec
     full_x = lhs_ref.shape[0] // depth
     half_x = full_x // 2
     hrows = half_x + 8
     at = depth * full_x
-    lines_used = put_ref.shape[0]
+    at_mult, at_counts, at_put, at_row, at_step, at_move = places
     copies = set_ends(n_sec, at, at + section, ring, strips_ref, cells_ref, out_hbm, out_ref, sems)
 
     for k in range(n_sec):
         start = pl.multiple_of((sec ^ k) * wy, wy)
         lhs_ref[:, pl.ds(start, wy)] = msg_refs[k][:at]
         mark_ref[:, pl.ds(start, wy)] = msg_refs[k][at : at + mark_ref.shape[0]]
-    transform = jnp.dot(lhs_ref[...], table_ref[...], preferred_element_type=F32)
-
-    found = jnp.dot(mark_ref[...], lanes_ref[...], preferred_element_type=F32)
-    nudge = jnp.sum(found[:lines_used] * put_ref[...], axis=0, keepdims=True)
-
-    mult = mult_ref[...]
+    transform = jnp.dot(lhs_ref[...], large_ref[:, : 2 * lanes], preferred_element_type=F32)
+
+    find = large_ref[:, 2 * lanes : 2 * lanes + total]
+    found = jnp.dot(mark_ref[...], find, preferred_element_type=F32)[:section]
+    nudge = jnp.sum(found * small_ref[at_put:at_row, :total], axis=0, keepdims=True)
+
+    mult = small_ref[at_mult : at_mult + 1, :lanes]
+    columns = large_ref[:lanes, 2 * lanes + total :]
     row_zero = lax.broadcasted_iota(jnp.int32, (half_x, lanes), 0) == 0
     rest = jnp.zeros((7, lanes), F32)
     picks = []
@@ -499,15 +508,19 @@
         for number, power in enumerate((plus, minus)):
             head = power.astype(BF16)
             tail = (power - head.astype(F32)).astype(BF16)
-            found = jnp.dot(head, col_ref[...], preferred_element_type=F32) + jnp.dot(
-                tail, col_ref[...], preferred_element_type=F32
+            found = jnp.dot(head, columns, preferred_element_type=F32) + jnp.dot(
+                tail, columns, preferred_element_type=F32
             )
-            value = value + jnp.sum(found * row_ref[number], axis=0, keepdims=True)
+            start = at_row + number * hrows
+            rows = small_ref[start : start + hrows, :total]
+            value = value + jnp.sum(found * rows, axis=0, keepdims=True)
         picks.append(value)
     picks.append(jnp.ones_like(picks[0]))
     picks.append(jnp.zeros((8 - len(picks), picks[0].shape[1]), F32))
     moved = lax.dot_general(
-        jnp.concatenate(picks, axis=0) * nudge, step_ref[...], (((1,), (0,)), ((), ())),
+        jnp.concatenate(picks, axis=0) * nudge,
+        small_ref[at_step : at_step + total, :NSHELL],
+        (((1,), (0,)), ((), ())),
         precision=lax.Precision.HIGHEST, preferred_element_type=F32,
     )
 
@@ -526,7 +539,8 @@
                 if not (block[group * 8 : group * 8 + 8] == value).any():
                     continue
                 rows = slice(group * 8, group * 8 + 8)
-                same = move_ref[rows, at_lanes] == value
+                line = slice(at_move + group * 8, at_move + group * 8 + 8)
+                same = small_ref[line, at_lanes] == F32(value)
                 for z in range(depth):
                     term = jnp.where(same, part_ref[z, rows, at_lanes], 0.0)
                     totals[z] = term if totals[z] is None else totals[z] + term
@@ -538,7 +552,8 @@
                     sums[z][goal] += jnp.where(lane >= shift, total, 0.0)
                 if shift and 0 <= goal + 1 < tiles:
                     sums[z][goal + 1] += jnp.where(lane < shift, total, 0.0)
-    norm = (counts_ref[...] + moved[depth : depth + 1]) * float(full_x * full_y)
+    counts = small_ref[at_counts : at_counts + 1, :NSHELL]
+    norm = (counts + moved[depth : depth + 1]) * float(full_x * full_y)
     lines = []
     for z in range(depth):
         line = jnp.sum(jnp.concatenate(sums[z], axis=1), axis=0, keepdims=True)
@@ -638,9 +653,10 @@
     )(dens)
 
     hrows, lanes = full_x // 2 + 8, full_y // 2 + 128
-    names = ("mult_y", "counts", "put", "lanes_of", "mark_row", "mark_col", "step")
     return call(
-        functools.partial(final_kernel, n_sec, section, tables["move"]),
+        functools.partial(
+            final_kernel, n_sec, section, tables["places"], tables["total"], tables["move"]
+        ),
         [shape((38, depth, wx, wy), F32), shape((depth, NSHELL), F32)],
         [
             pltpu.VMEM((depth * full_x, full_y), BF16),
@@ -651,8 +667,7 @@
             pltpu.SemaphoreType.DMA((len(ENDS) + 1,)),
         ],
         out_specs=[pl.BlockSpec(memory_space=pltpu.HBM)] * 2,
-    )(bulk, *sec_got, *strip_got, lanes_own, cells, tables["table_y"], tables["move"].astype(np.int32),
-      *[tables[name] for name in names])
+    )(bulk, *sec_got, *strip_got, lanes_own, cells, tables["large"], tables["small"])
 
 
 def solution(mesh):

time: 21.5 us -> 21.3 us (level)
  no operation moved by 1% of the time
where the time goes in v6:
time: 21.3 us; the launch traced here: 21.1 us
  starting transfers between devices  12.7 us (60%)
  Pallas kernels  4.83 us (23%)
  waiting for transfers between devices  1.7 us (8%)
  other arithmetic  1.17 us (5%)
  between operations  0.69 us (3%)
    ppermute x3, starting transfers between devices, on_device(): sec_got.append(lax.ppermute(msg if with_columns else bulk, 'sec', move))  7.26 us
    ppermute x1, starting transfers between devices, on_device(): lax.ppermute(row_msg, 'row', xor_pairs(n_row, k))  3.03 us
    pallas_call x1, Pallas kernels, on_device(): call(functools.partial(final_kernel, n_sec, section, tables['places'], ta...  2.36 us
    pallas_call x1, Pallas kernels, on_device(): call(cells_kernel, shape((38, depth, wx, wy), F32), flops=LBM, moved=LBM)  1.7 us
    ppermute x1, waiting for transfers between devices, on_device(): strip_got.append(lax.ppermute(strip, 'sec', move))  1.64 us
    select_n x1, other arithmetic, on_device(): own = jnp.where(part == 2, whole_numbers.astype(F32), density)  1.16 us
    ppermute x2, starting transfers between devices, on_device(): col_got = [lax.ppermute(col_msg, 'col', m) for m in ring_moves(n_col)]  1.09 us
    ppermute x1, starting transfers between devices, on_device(): strip_got.append(lax.ppermute(strip, 'sec', move))  0.68 us
  transfers between devices with their start and end apart: 9, of which 1 were waited for; matrix products, arithmetic and copies ran while one was open for 0% of the time, Pallas kernels for 11%

profile of v6, /device:TPU:0, one launch (start us, length us, event | category | flops | bytes accessed | tf_op | source)
XLA Modules:
  0.0 21.1 jit_solution(453229796521476136)
XLA Ops:
  0.6 0.0 copy-start.1
  0.6 0.0 copy-start
  0.7 1.2 %multiply_select_fusion.own_ref = f32[3,2,64,128]{3,2,1,0:T(8,128)S(1)} fusion(f32[2,2,64,128]{3,2,1,0:T(8,128)} %param.6, s32[2,64,128]{2,1,0:T(8,128)} %param.5, s32[64,128]{1,0:T(8,128)} %param.7, pred[3]{0:T(512)(128)(4,1)S(1)} %iota_compare_fusion), kind=kLoop, calls=%fused_computation | loop fusion | flops 344064 | bytes 425987 | tf_op jit(solution)/shard_map/jit(_where)/select_n | solution.py:593
  1.8 0.2 shard_map.68.refs_0_.row_ref
  2.0 3.0 %collective-permute-start = (bf16[160,128]{1,0:T(8,128)(2,1)S(1)}, bf16[160,128]{1,0:T(8,128)(2,1)S(1)}, u32[]{:S(2)}, u32[]{:S(2)}) collective-permute-start(bf16[160,128]{1,0:T(8,128)(2,1)S(1)} %shard_map.68.refs_0_.row_ref), channel_id=1, source_target_pairs={{0,4},{4,0},{1,5},{5,1},{2,6},{6,2},{3,7},{7,3},{8,12},{12,8},{9,1... | collective-permute-start | bytes 122888 | tf_op jit(solution)/shard_map/ppermute | solution.py:604
  5.0 0.2 shard_map.69
  5.2 0.7 %collective-permute-start.4 = (bf16[256,128]{1,0:T(8,128)(2,1)S(1)}, bf16[256,128]{1,0:T(8,128)(2,1)S(1)}, u32[]{:S(2)}, u32[]{:S(2)}) collective-permute-start(bf16[256,128]{1,0:T(8,128)(2,1)S(1)} %get-tuple-element.9), channel_id=1, source_target_pairs={{0,7},{1,6},{2,5},{3,4},{4,3},{5,2},{6,1},{7,0},{8,15},{9,14},{10,... | collective-permute-start | bytes 196616 | tf_op jit(solution)/shard_map/ppermute | solution.py:613
  5.9 0.6 %collective-permute-start.3 = (bf16[256,128]{1,0:T(8,128)(2,1)S(1)}, bf16[256,128]{1,0:T(8,128)(2,1)S(1)}, u32[]{:S(2)}, u32[]{:S(2)}) collective-permute-start(bf16[256,128]{1,0:T(8,128)(2,1)S(1)} %get-tuple-element.9), channel_id=1, source_target_pairs={{0,3},{1,2},{2,1},{3,0},{4,7},{5,6},{6,5},{7,4},{8,11},{9,10},{10,... | collective-permute-start | bytes 196616 | tf_op jit(solution)/shard_map/ppermute | solution.py:603
  6.5 0.5 %collective-permute-start.1 = (bf16[256,128]{1,0:T(8,128)(2,1)S(1)}, bf16[256,128]{1,0:T(8,128)(2,1)S(1)}, u32[]{:S(2)}, u32[]{:S(2)}) collective-permute-start(bf16[256,128]{1,0:T(8,128)(2,1)S(1)} %get-tuple-element.9), channel_id=1, source_target_pairs={{0,1},{1,0},{2,3},{3,2},{4,5},{5,4},{6,7},{7,6},{8,9},{9,8},{10,11... | collective-permute-start | bytes 196616 | tf_op jit(solution)/shard_map/ppermute | solution.py:603
  7.0 0.0 collective-permute-done.refs_1_.refs_2_
  7.0 0.0 collective-permute-start.2
  7.0 0.2 shard_map.70.refs_5_.msg_own_ref
  7.2 3.2 %collective-permute-start.7 = (bf16[304,128]{1,0:T(8,128)(2,1)S(1)}, bf16[304,128]{1,0:T(8,128)(2,1)S(1)}, u32[]{:S(2)}, u32[]{:S(2)}) collective-permute-start(bf16[304,128]{1,0:T(8,128)(2,1)S(1)} %shard_map.70.refs_5_.msg_own_ref), channel_id=1, source_target_pairs={{0,16},{8,24},{16,0},{24,8},{1,17},{9,25},{17,1},{25,9},{2,18},{10... | collective-permute-start | bytes 233480 | tf_op jit(solution)/shard_map/ppermute | solution.py:643
  10.3 0.0 collective-permute-done.4.refs_4_
  10.3 1.6 %collective-permute-start.6 = (bf16[304,128]{1,0:T(8,128)(2,1)S(1)}, bf16[304,128]{1,0:T(8,128)(2,1)S(1)}, u32[]{:S(2)}, u32[]{:S(2)}) collective-permute-start(bf16[304,128]{1,0:T(8,128)(2,1)S(1)} %shard_map.70.refs_5_.msg_own_ref), channel_id=1, source_target_pairs={{0,8},{8,0},{16,24},{24,16},{1,9},{9,1},{17,25},{25,17},{2,10},{10... | collective-permute-start | bytes 233480 | tf_op jit(solution)/shard_map/ppermute | solution.py:643
  11.9 0.0 collective-permute-done.3.refs_3_
  11.9 0.0 collective-permute-done.1.refs_0_
  11.9 0.0 collective-permute-done.2.refs_1_
  11.9 0.2 %shard_map.71 = (bf16[304,128]{1,0:T(8,128)(2,1)S(1)}, bf16[48,128]{1,0:T(8,128)(2,1)S(1)}, f32[12,72,128]{2,1,0:T(8,128)S(1)}, f32[72,128]{1,0:T(8,128)S(1)}) custom-call(f32[3,2,64,128]{3,2,1,0:T(8,128)S(1)} %multiply_select_fusion.own_ref, bf16[160,128]{1,0:T(8,128)(2,1)S(1)} %shard_map.68.refs_0_.row_ref, ...), custom_call_target="tpu_custom_call" | custom-call | flops 16777216 | bytes 16777216 | tf_op jit(solution)/shard_map/pallas_call | solution.py:625
  12.2 2.5 %collective-permute-start.5 = (bf16[304,128]{1,0:T(8,128)(2,1)S(1)}, bf16[304,128]{1,0:T(8,128)(2,1)S(1)}, u32[]{:S(2)}, u32[]{:S(2)}) collective-permute-start(bf16[304,128]{1,0:T(8,128)(2,1)S(1)} %get-tuple-element.10), channel_id=1, source_target_pairs={{0,24},{8,16},{16,8},{24,0},{1,25},{9,17},{17,9},{25,1},{2,26},{10... | collective-permute-start | bytes 233480 | tf_op jit(solution)/shard_map/ppermute | solution.py:643
  14.7 0.7 %collective-permute-start.8 = (bf16[48,128]{1,0:T(8,128)(2,1)S(1)}, bf16[48,128]{1,0:T(8,128)(2,1)S(1)}, u32[]{:S(2)}, u32[]{:S(2)}) collective-permute-start(bf16[48,128]{1,0:T(8,128)(2,1)S(1)} %get-tuple-element.11), channel_id=1, source_target_pairs={{0,8},{8,0},{16,24},{24,16},{1,9},{9,1},{17,25},{25,17},{2,10},{10... | collective-permute-start | bytes 36872 | tf_op jit(solution)/shard_map/ppermute | solution.py:646
  15.4 1.7 %shard_map.72.refs_5_ = f32[38,2,64,128]{3,2,1,0:T(8,128)S(1)} custom-call(f32[12,72,128]{2,1,0:T(8,128)S(1)} %get-tuple-element.13.dens_ref), custom_call_target="tpu_custom_call" | custom-call | flops 1024 | bytes 1024 | tf_op jit(solution)/shard_map/pallas_call | solution.py:648
  17.1 1.6 %collective-permute-done.8.refs_3_ = bf16[48,128]{1,0:T(8,128)(2,1)S(1)} collective-permute-done((bf16[48,128]{1,0:T(8,128)(2,1)S(1)}, bf16[48,128]{1,0:T(8,128)(2,1)S(1)}, u32[]{:S(2)}, u32[]{:S(2)}) %collective-permute-start.8) | collective-permute-done | bytes 12320 | tf_op jit(solution)/shard_map/ppermute | solution.py:646
  18.7 0.0 collective-permute-done.7.refs_2_
  18.7 0.0 collective-permute-done.6.refs_1_
  18.7 0.0 collective-permute-done.5.refs_0_
  18.7 0.0 copy-done.1
  18.7 0.0 copy-done
  18.8 2.4 %shard_map.73 = (f32[38,2,64,128]{3,2,1,0:T(8,128)}, f32[2,256]{1,0:T(2,128)}) custom-call(bf16[304,128]{1,0:T(8,128)(2,1)S(1)} %shard_map.70.refs_5_.msg_own_ref, bf16[304,128]{1,0:T(8,128)(2,1)S(1)} %collective-permute-done.5.refs_0_, bf16[304,128]{1,0:T(8,128)(2,1)S(1)} %collective-permute-done.6.refs_1_, ...), custom_call_target="tpu_custom_call" | custom-call | tf_op jit(solution)/shard_map/pallas_call | solution.py:656
  (1 shorter events, 0.0 us)
Async XLA Ops:
  0.6 18.1 %copy-start.1 = (f32[368,384]{1,0:T(8,128)S(1)}, f32[368,384]{1,0:T(8,128)}, u32[]{:S(2)}) copy-start(f32[368,384]{1,0:T(8,128)} %constant.15.clone.refs_7_) | copy-start | bytes 1695748
  0.6 18.1 %copy-start = (bf16[512,1024]{1,0:T(8,128)(2,1)S(1)}, bf16[512,1024]{1,0:T(8,128)(2,1)}, u32[]{:S(2)}) copy-start(bf16[512,1024]{1,0:T(8,128)(2,1)} %constant.14.clone.refs_6_) | copy-start | bytes 3145732
  2.0 5.0 %collective-permute-start = (bf16[160,128]{1,0:T(8,128)(2,1)S(1)}, bf16[160,128]{1,0:T(8,128)(2,1)S(1)}, u32[]{:S(2)}, u32[]{:S(2)}) collective-permute-start(bf16[160,128]{1,0:T(8,128)(2,1)S(1)} %shard_map.68.refs_0_.row_ref), channel_id=1, source_target_pairs={{0,4},{4,0},{1,5},{5,1},{2,6},{6,2},{3,7},{7,3},{8,12},{12,8},{9,1... | collective-permute-start | bytes 122888 | tf_op jit(solution)/shard_map/ppermute | solution.py:604
  5.2 5.1 %collective-permute-start.4 = (bf16[256,128]{1,0:T(8,128)(2,1)S(1)}, bf16[256,128]{1,0:T(8,128)(2,1)S(1)}, u32[]{:S(2)}, u32[]{:S(2)}) collective-permute-start(bf16[256,128]{1,0:T(8,128)(2,1)S(1)} %get-tuple-element.9), channel_id=1, source_target_pairs={{0,7},{1,6},{2,5},{3,4},{4,3},{5,2},{6,1},{7,0},{8,15},{9,14},{10,... | collective-permute-start | bytes 196616 | tf_op jit(solution)/shard_map/ppermute | solution.py:613
  5.9 6.0 %collective-permute-start.3 = (bf16[256,128]{1,0:T(8,128)(2,1)S(1)}, bf16[256,128]{1,0:T(8,128)(2,1)S(1)}, u32[]{:S(2)}, u32[]{:S(2)}) collective-permute-start(bf16[256,128]{1,0:T(8,128)(2,1)S(1)} %get-tuple-element.9), channel_id=1, source_target_pairs={{0,3},{1,2},{2,1},{3,0},{4,7},{5,6},{6,5},{7,4},{8,11},{9,10},{10,... | collective-permute-start | bytes 196616 | tf_op jit(solution)/shard_map/ppermute | solution.py:603
  6.5 5.4 %collective-permute-start.1 = (bf16[256,128]{1,0:T(8,128)(2,1)S(1)}, bf16[256,128]{1,0:T(8,128)(2,1)S(1)}, u32[]{:S(2)}, u32[]{:S(2)}) collective-permute-start(bf16[256,128]{1,0:T(8,128)(2,1)S(1)} %get-tuple-element.9), channel_id=1, source_target_pairs={{0,1},{1,0},{2,3},{3,2},{4,5},{5,4},{6,7},{7,6},{8,9},{9,8},{10,11... | collective-permute-start | bytes 196616 | tf_op jit(solution)/shard_map/ppermute | solution.py:603
  7.0 4.9 %collective-permute-start.2 = (bf16[160,128]{1,0:T(8,128)(2,1)S(1)}, bf16[160,128]{1,0:T(8,128)(2,1)S(1)}, u32[]{:S(2)}, u32[]{:S(2)}) collective-permute-start(bf16[160,128]{1,0:T(8,128)(2,1)S(1)} %collective-permute-done.refs_1_.refs_2_), channel_id=1, source_target_pairs={{0,1},{1,0},{2,3},{3,2},{4,5},{5,4},{6,7},{7,6},{8,9},{9,8},{10,11... | collective-permute-start | bytes 122888 | tf_op jit(solution)/shard_map/ppermute | solution.py:610
  7.2 11.5 %collective-permute-start.7 = (bf16[304,128]{1,0:T(8,128)(2,1)S(1)}, bf16[304,128]{1,0:T(8,128)(2,1)S(1)}, u32[]{:S(2)}, u32[]{:S(2)}) collective-permute-start(bf16[304,128]{1,0:T(8,128)(2,1)S(1)} %shard_map.70.refs_5_.msg_own_ref), channel_id=1, source_target_pairs={{0,16},{8,24},{16,0},{24,8},{1,17},{9,25},{17,1},{25,9},{2,18},{10... | collective-permute-start | bytes 233480 | tf_op jit(solution)/shard_map/ppermute | solution.py:643
  10.3 8.4 %collective-permute-start.6 = (bf16[304,128]{1,0:T(8,128)(2,1)S(1)}, bf16[304,128]{1,0:T(8,128)(2,1)S(1)}, u32[]{:S(2)}, u32[]{:S(2)}) collective-permute-start(bf16[304,128]{1,0:T(8,128)(2,1)S(1)} %shard_map.70.refs_5_.msg_own_ref), channel_id=1, source_target_pairs={{0,8},{8,0},{16,24},{24,16},{1,9},{9,1},{17,25},{25,17},{2,10},{10... | collective-permute-start | bytes 233480 | tf_op jit(solution)/shard_map/ppermute | solution.py:643
  12.2 6.6 %collective-permute-start.5 = (bf16[304,128]{1,0:T(8,128)(2,1)S(1)}, bf16[304,128]{1,0:T(8,128)(2,1)S(1)}, u32[]{:S(2)}, u32[]{:S(2)}) collective-permute-start(bf16[304,128]{1,0:T(8,128)(2,1)S(1)} %get-tuple-element.10), channel_id=1, source_target_pairs={{0,24},{8,16},{16,8},{24,0},{1,25},{9,17},{17,9},{25,1},{2,26},{10... | collective-permute-start | bytes 233480 | tf_op jit(solution)/shard_map/ppermute | solution.py:643
  14.7 4.0 %collective-permute-start.8 = (bf16[48,128]{1,0:T(8,128)(2,1)S(1)}, bf16[48,128]{1,0:T(8,128)(2,1)S(1)}, u32[]{:S(2)}, u32[]{:S(2)}) collective-permute-start(bf16[48,128]{1,0:T(8,128)(2,1)S(1)} %get-tuple-element.11), channel_id=1, source_target_pairs={{0,8},{8,0},{16,24},{24,16},{1,9},{9,1},{17,25},{25,17},{2,10},{10... | collective-permute-start | bytes 36872 | tf_op jit(solution)/shard_map/ppermute | solution.py:646

commit v7 on v6

--- a/solution.py
+++ b/solution.py
@@ -74,6 +74,10 @@
 
 def swap_order(count):
     return SWAPS.get(count, tuple(range(1, count)))
+
+
+def late_swaps(count):
+    return tuple(k for k in range(1, count) if k not in EARLY.get(count, ()))
 
 
 def pair_product(first, second, count_second):
@@ -451,6 +455,22 @@
     return copies
 
 
+def early_kernel(n_sec, lanes, taken, *refs):
+    msg_refs, (large_ref, out_ref) = refs[:-2], refs[-2:]
+    wy = large_ref.shape[0] // n_sec
+    sec = lax.axis_index("sec")
+    total = None
+    for k, ref in zip(taken, msg_refs):
+        start = pl.multiple_of((sec ^ k) * wy, wy)
+        part = jnp.dot(
+            ref[: out_ref.shape[0]],
+            large_ref[pl.ds(start, wy), : 2 * lanes],
+            preferred_element_type=F32,
+        )
+        total = part if total is None else total + part
+    out_ref[...] = total
+
+
 def final_kernel(n_sec, section, places, total, move, msg_own_ref, *refs):
     msg_refs = [msg_own_ref] + [refs[swap_order(n_sec).index(k)] for k in range(1, n_sec)]
     refs = refs[n_sec - 1 :]
@@ -463,13 +483,13 @@
         else:
             ring.append(msg_refs[k])
     (strips_ref, cells_ref), refs = refs[:2], refs[2:]
-    (large_ref, small_ref,
-     out_hbm, spec_hbm, lhs_ref, mark_ref, part_ref, out_ref, spec_ref, sems) = refs
+    (early_ref, large_ref, small_ref,
+     out_hbm, spec_hbm, mark_ref, part_ref, out_ref, spec_ref, sems) = refs
     depth = spec_ref.shape[0]
     sec = lax.axis_index("sec")
     full_y, lanes = large_ref.shape[0], move.shape[1]
     wy = full_y // n_sec
-    full_x = lhs_ref.shape[0] // depth
+    full_x = early_ref.shape[0] // depth
     half_x = full_x // 2
     hrows = half_x + 8
     at = depth * full_x
@@ -478,9 +498,15 @@
 
     for k in range(n_sec):
         start = pl.multiple_of((sec ^ k) * wy, wy)
-        lhs_ref[:, pl.ds(start, wy)] = msg_refs[k][:at]
         mark_ref[:, pl.ds(start, wy)] = msg_refs[k][at : at + mark_ref.shape[0]]
-    transform = jnp.dot(lhs_ref[...], large_ref[:, : 2 * lanes], preferred_element_type=F32)
+    transform = early_ref[...]
+    for k in late_swaps(n_sec):
+        start = pl.multiple_of((sec ^ k) * wy, wy)
+        transform = transform + jnp.dot(
+            msg_refs[k][:at],
+            large_ref[pl.ds(start, wy), : 2 * lanes],
+            preferred_element_type=F32,
+        )
 
     find = large_ref[:, 2 * lanes : 2 * lanes + total]
     found = jnp.dot(mark_ref[...], find, preferred_element_type=F32)[:section]
@@ -653,13 +679,18 @@
     )(dens)
 
     hrows, lanes = full_x // 2 + 8, full_y // 2 + 128
+    taken = (0,) + EARLY.get(n_sec, ())
+    blocks = [bulk if k == 0 else sec_got[swap_order(n_sec).index(k)] for k in taken]
+    early_part = call(
+        functools.partial(early_kernel, n_sec, lanes, taken),
+        shape((depth * full_x, 2 * lanes), F32),
+    )(*blocks, tables["large"])
     return call(
         functools.partial(
             final_kernel, n_sec, section, tables["places"], tables["total"], tables["move"]
         ),
         [shape((38, depth, wx, wy), F32), shape((depth, NSHELL), F32)],
         [
-            pltpu.VMEM((depth * full_x, full_y), BF16),
             pltpu.VMEM((whole(section), full_y), BF16),
             pltpu.VMEM((depth, hrows, lanes), F32),
             pltpu.VMEM((38, depth, wx, wy), F32),
@@ -667,7 +698,7 @@
             pltpu.SemaphoreType.DMA((len(ENDS) + 1,)),
         ],
         out_specs=[pl.BlockSpec(memory_space=pltpu.HBM)] * 2,
-    )(bulk, *sec_got, *strip_got, lanes_own, cells, tables["large"], tables["small"])
+    )(bulk, *sec_got, *strip_got, lanes_own, cells, early_part, tables["large"], tables["small"])
 
 
 def solution(mesh):

time: 21.3 us -> 21.2 us (level)
  waiting for transfers between devices: 1.7 us -> 1.19 us
  Pallas kernels: 4.83 us -> 5.34 us
    ppermute x1, waiting for transfers between devices: 1.64 us -> 1.14 us  [on_device(): strip_got.append(lax.ppermute(strip, 'sec', move))]
    pallas_call x0 -> x1, Pallas kernels: none -> 0.47 us  [on_device(): call(functools.partial(early_kernel, n_sec, lanes, taken), shape((depth *...]
  transfers between devices with their start and end apart: 9 -> 9, of which waited for: 1 -> 1; matrix products, arithmetic and copies ran while one was open for 0% -> 0% of each run, Pallas kernels for 11% -> 13%
where the time goes in v7:
time: 21.2 us; the launch traced here: 21.1 us
  starting transfers between devices  12.7 us (60%)
  Pallas kernels  5.34 us (25%)
  waiting for transfers between devices  1.19 us (6%)
  other arithmetic  1.14 us (5%)
  between operations  0.69 us (3%)
    ppermute x3, starting transfers between devices, on_device(): sec_got.append(lax.ppermute(msg if with_columns else bulk, 'sec', move))  7.26 us
    ppermute x1, starting transfers between devices, on_device(): lax.ppermute(row_msg, 'row', xor_pairs(n_row, k))  3.03 us
    pallas_call x1, Pallas kernels, on_device(): call(functools.partial(final_kernel, n_sec, section, tables['places'], ta...  2.41 us
    pallas_call x1, Pallas kernels, on_device(): call(cells_kernel, shape((38, depth, wx, wy), F32), flops=LBM, moved=LBM)  1.7 us
    ppermute x1, waiting for transfers between devices, on_device(): strip_got.append(lax.ppermute(strip, 'sec', move))  1.14 us
    select_n x1, other arithmetic, on_device(): own = jnp.where(part == 2, whole_numbers.astype(F32), density)  1.13 us
    ppermute x2, starting transfers between devices, on_device(): col_got = [lax.ppermute(col_msg, 'col', m) for m in ring_moves(n_col)]  1.09 us
    ppermute x1, starting transfers between devices, on_device(): strip_got.append(lax.ppermute(strip, 'sec', move))  0.68 us
  transfers between devices with their start and end apart: 9, of which 1 were waited for; matrix products, arithmetic and copies ran while one was open for 0% of the time, Pallas kernels for 13%

profile of v7, /device:TPU:0, one launch (start us, length us, event | category | flops | bytes accessed | tf_op | source)
XLA Modules:
  0.0 21.1 jit_solution(8111044472381848035)
XLA Ops:
  0.6 0.0 copy-start
  0.7 1.1 %multiply_select_fusion.own_ref = f32[3,2,64,128]{3,2,1,0:T(8,128)S(1)} fusion(f32[2,2,64,128]{3,2,1,0:T(8,128)} %param.6, s32[2,64,128]{2,1,0:T(8,128)} %param.5, s32[64,128]{1,0:T(8,128)} %param.7, pred[3]{0:T(512)(128)(4,1)S(1)} %iota_compare_fusion), kind=kLoop, calls=%fused_computation | loop fusion | flops 344064 | bytes 425987 | tf_op jit(solution)/shard_map/jit(_where)/select_n | solution.py:619
  1.8 0.2 shard_map.68.refs_0_.row_ref
  2.0 3.0 %collective-permute-start = (bf16[160,128]{1,0:T(8,128)(2,1)S(1)}, bf16[160,128]{1,0:T(8,128)(2,1)S(1)}, u32[]{:S(2)}, u32[]{:S(2)}) collective-permute-start(bf16[160,128]{1,0:T(8,128)(2,1)S(1)} %shard_map.68.refs_0_.row_ref), channel_id=1, source_target_pairs={{0,4},{4,0},{1,5},{5,1},{2,6},{6,2},{3,7},{7,3},{8,12},{12,8},{9,1... | collective-permute-start | bytes 122888 | tf_op jit(solution)/shard_map/ppermute | solution.py:630
  5.0 0.2 shard_map.69
  5.2 0.7 %collective-permute-start.4 = (bf16[256,128]{1,0:T(8,128)(2,1)S(1)}, bf16[256,128]{1,0:T(8,128)(2,1)S(1)}, u32[]{:S(2)}, u32[]{:S(2)}) collective-permute-start(bf16[256,128]{1,0:T(8,128)(2,1)S(1)} %get-tuple-element.9), channel_id=1, source_target_pairs={{0,7},{1,6},{2,5},{3,4},{4,3},{5,2},{6,1},{7,0},{8,15},{9,14},{10,... | collective-permute-start | bytes 196616 | tf_op jit(solution)/shard_map/ppermute | solution.py:639
  5.9 0.6 %collective-permute-start.3 = (bf16[256,128]{1,0:T(8,128)(2,1)S(1)}, bf16[256,128]{1,0:T(8,128)(2,1)S(1)}, u32[]{:S(2)}, u32[]{:S(2)}) collective-permute-start(bf16[256,128]{1,0:T(8,128)(2,1)S(1)} %get-tuple-element.9), channel_id=1, source_target_pairs={{0,3},{1,2},{2,1},{3,0},{4,7},{5,6},{6,5},{7,4},{8,11},{9,10},{10,... | collective-permute-start | bytes 196616 | tf_op jit(solution)/shard_map/ppermute | solution.py:629
  6.5 0.5 %collective-permute-start.1 = (bf16[256,128]{1,0:T(8,128)(2,1)S(1)}, bf16[256,128]{1,0:T(8,128)(2,1)S(1)}, u32[]{:S(2)}, u32[]{:S(2)}) collective-permute-start(bf16[256,128]{1,0:T(8,128)(2,1)S(1)} %get-tuple-element.9), channel_id=1, source_target_pairs={{0,1},{1,0},{2,3},{3,2},{4,5},{5,4},{6,7},{7,6},{8,9},{9,8},{10,11... | collective-permute-start | bytes 196616 | tf_op jit(solution)/shard_map/ppermute | solution.py:629
  6.9 0.0 collective-permute-done.refs_1_.refs_2_
  7.0 0.0 collective-permute-start.2
  7.0 0.2 shard_map.70.refs_5_.refs_0_.msg_own_ref
  7.1 3.2 %collective-permute-start.7 = (bf16[304,128]{1,0:T(8,128)(2,1)S(1)}, bf16[304,128]{1,0:T(8,128)(2,1)S(1)}, u32[]{:S(2)}, u32[]{:S(2)}) collective-permute-start(bf16[304,128]{1,0:T(8,128)(2,1)S(1)} %shard_map.70.refs_5_.refs_0_.msg_own_ref), channel_id=1, source_target_pairs={{0,16},{8,24},{16,0},{24,8},{1,17},{9,25},{17,1},{25,9},{2,18},{10... | collective-permute-start | bytes 233480 | tf_op jit(solution)/shard_map/ppermute | solution.py:669
  10.3 0.0 collective-permute-done.4.refs_4_
  10.3 1.6 %collective-permute-start.6 = (bf16[304,128]{1,0:T(8,128)(2,1)S(1)}, bf16[304,128]{1,0:T(8,128)(2,1)S(1)}, u32[]{:S(2)}, u32[]{:S(2)}) collective-permute-start(bf16[304,128]{1,0:T(8,128)(2,1)S(1)} %shard_map.70.refs_5_.refs_0_.msg_own_ref), channel_id=1, source_target_pairs={{0,8},{8,0},{16,24},{24,16},{1,9},{9,1},{17,25},{25,17},{2,10},{10... | collective-permute-start | bytes 233480 | tf_op jit(solution)/shard_map/ppermute | solution.py:669
  11.9 0.0 collective-permute-done.3.refs_3_
  11.9 0.0 collective-permute-done.1.refs_0_
  11.9 0.0 collective-permute-done.2.refs_1_
  11.9 0.2 %shard_map.71 = (bf16[304,128]{1,0:T(8,128)(2,1)S(1)}, bf16[48,128]{1,0:T(8,128)(2,1)S(1)}, f32[12,72,128]{2,1,0:T(8,128)S(1)}, f32[72,128]{1,0:T(8,128)S(1)}) custom-call(f32[3,2,64,128]{3,2,1,0:T(8,128)S(1)} %multiply_select_fusion.own_ref, bf16[160,128]{1,0:T(8,128)(2,1)S(1)} %shard_map.68.refs_0_.row_ref, ...), custom_call_target="tpu_custom_call" | custom-call | flops 16777216 | bytes 16777216 | tf_op jit(solution)/shard_map/pallas_call | solution.py:651
  12.1 2.5 %collective-permute-start.5 = (bf16[304,128]{1,0:T(8,128)(2,1)S(1)}, bf16[304,128]{1,0:T(8,128)(2,1)S(1)}, u32[]{:S(2)}, u32[]{:S(2)}) collective-permute-start(bf16[304,128]{1,0:T(8,128)(2,1)S(1)} %get-tuple-element.10), channel_id=1, source_target_pairs={{0,24},{8,16},{16,8},{24,0},{1,25},{9,17},{17,9},{25,1},{2,26},{10... | collective-permute-start | bytes 233480 | tf_op jit(solution)/shard_map/ppermute | solution.py:669
  14.7 0.7 %collective-permute-start.8 = (bf16[48,128]{1,0:T(8,128)(2,1)S(1)}, bf16[48,128]{1,0:T(8,128)(2,1)S(1)}, u32[]{:S(2)}, u32[]{:S(2)}) collective-permute-start(bf16[48,128]{1,0:T(8,128)(2,1)S(1)} %get-tuple-element.11), channel_id=1, source_target_pairs={{0,8},{8,0},{16,24},{24,16},{1,9},{9,1},{17,25},{25,17},{2,10},{10... | collective-permute-start | bytes 36872 | tf_op jit(solution)/shard_map/ppermute | solution.py:672
  15.3 0.0 copy-start.1
  15.3 1.7 %shard_map.72.refs_5_ = f32[38,2,64,128]{3,2,1,0:T(8,128)S(1)} custom-call(f32[12,72,128]{2,1,0:T(8,128)S(1)} %get-tuple-element.13.dens_ref), custom_call_target="tpu_custom_call" | custom-call | flops 1024 | bytes 1024 | tf_op jit(solution)/shard_map/pallas_call | solution.py:674
  17.0 0.0 collective-permute-done.7.refs_2_
  17.0 0.0 collective-permute-done.6.refs_1_
  17.1 0.0 copy-done
  17.1 0.5 %shard_map.73.refs_6_ = f32[256,768]{1,0:T(8,128)S(1)} custom-call(bf16[304,128]{1,0:T(8,128)(2,1)S(1)} %shard_map.70.refs_5_.refs_0_.msg_own_ref, bf16[304,128]{1,0:T(8,128)(2,1)S(1)} %collective-permute-done.6.refs_1_, bf16[304,128]{1,0:T(8,128)(2,1)S(1)} %collective-permute-done.7.refs_2_, bf16[512,1024]{1,0:T(8,128)(2,1)S(1)} %copy-done), custom_call_target="tpu_custom_call" | custom-call | tf_op jit(solution)/shard_map/pallas_call | solution.py:684
  17.5 1.1 %collective-permute-done.8.refs_3_ = bf16[48,128]{1,0:T(8,128)(2,1)S(1)} collective-permute-done((bf16[48,128]{1,0:T(8,128)(2,1)S(1)}, bf16[48,128]{1,0:T(8,128)(2,1)S(1)}, u32[]{:S(2)}, u32[]{:S(2)}) %collective-permute-start.8) | collective-permute-done | bytes 12320 | tf_op jit(solution)/shard_map/ppermute | solution.py:672
  18.7 0.0 collective-permute-done.5.refs_0_
  18.7 0.0 copy-done.1
  18.7 2.4 %shard_map.74 = (f32[38,2,64,128]{3,2,1,0:T(8,128)}, f32[2,256]{1,0:T(2,128)}) custom-call(bf16[304,128]{1,0:T(8,128)(2,1)S(1)} %shard_map.70.refs_5_.refs_0_.msg_own_ref, bf16[304,128]{1,0:T(8,128)(2,1)S(1)} %collective-permute-done.5.refs_0_, bf16[304,128]{1,0:T(8,128)(2,1)S(1)} %collective-permute-done.6.refs_1_, ...), custom_call_target="tpu_custom_call" | custom-call | tf_op jit(solution)/shard_map/pallas_call | solution.py:688
  (1 shorter events, 0.0 us)
Async XLA Ops:
  0.6 16.4 %copy-start = (bf16[512,1024]{1,0:T(8,128)(2,1)S(1)}, bf16[512,1024]{1,0:T(8,128)(2,1)}, u32[]{:S(2)}) copy-start(bf16[512,1024]{1,0:T(8,128)(2,1)} %constant.14.clone.refs_3_.refs_7_) | copy-start | bytes 3145732
  2.0 5.0 %collective-permute-start = (bf16[160,128]{1,0:T(8,128)(2,1)S(1)}, bf16[160,128]{1,0:T(8,128)(2,1)S(1)}, u32[]{:S(2)}, u32[]{:S(2)}) collective-permute-start(bf16[160,128]{1,0:T(8,128)(2,1)S(1)} %shard_map.68.refs_0_.row_ref), channel_id=1, source_target_pairs={{0,4},{4,0},{1,5},{5,1},{2,6},{6,2},{3,7},{7,3},{8,12},{12,8},{9,1... | collective-permute-start | bytes 122888 | tf_op jit(solution)/shard_map/ppermute | solution.py:630
  5.2 5.1 %collective-permute-start.4 = (bf16[256,128]{1,0:T(8,128)(2,1)S(1)}, bf16[256,128]{1,0:T(8,128)(2,1)S(1)}, u32[]{:S(2)}, u32[]{:S(2)}) collective-permute-start(bf16[256,128]{1,0:T(8,128)(2,1)S(1)} %get-tuple-element.9), channel_id=1, source_target_pairs={{0,7},{1,6},{2,5},{3,4},{4,3},{5,2},{6,1},{7,0},{8,15},{9,14},{10,... | collective-permute-start | bytes 196616 | tf_op jit(solution)/shard_map/ppermute | solution.py:639
  5.9 6.0 %collective-permute-start.3 = (bf16[256,128]{1,0:T(8,128)(2,1)S(1)}, bf16[256,128]{1,0:T(8,128)(2,1)S(1)}, u32[]{:S(2)}, u32[]{:S(2)}) collective-permute-start(bf16[256,128]{1,0:T(8,128)(2,1)S(1)} %get-tuple-element.9), channel_id=1, source_target_pairs={{0,3},{1,2},{2,1},{3,0},{4,7},{5,6},{6,5},{7,4},{8,11},{9,10},{10,... | collective-permute-start | bytes 196616 | tf_op jit(solution)/shard_map/ppermute | solution.py:629
  6.5 5.4 %collective-permute-start.1 = (bf16[256,128]{1,0:T(8,128)(2,1)S(1)}, bf16[256,128]{1,0:T(8,128)(2,1)S(1)}, u32[]{:S(2)}, u32[]{:S(2)}) collective-permute-start(bf16[256,128]{1,0:T(8,128)(2,1)S(1)} %get-tuple-element.9), channel_id=1, source_target_pairs={{0,1},{1,0},{2,3},{3,2},{4,5},{5,4},{6,7},{7,6},{8,9},{9,8},{10,11... | collective-permute-start | bytes 196616 | tf_op jit(solution)/shard_map/ppermute | solution.py:629
  7.0 4.9 %collective-permute-start.2 = (bf16[160,128]{1,0:T(8,128)(2,1)S(1)}, bf16[160,128]{1,0:T(8,128)(2,1)S(1)}, u32[]{:S(2)}, u32[]{:S(2)}) collective-permute-start(bf16[160,128]{1,0:T(8,128)(2,1)S(1)} %collective-permute-done.refs_1_.refs_2_), channel_id=1, source_target_pairs={{0,1},{1,0},{2,3},{3,2},{4,5},{5,4},{6,7},{7,6},{8,9},{9,8},{10,11... | collective-permute-start | bytes 122888 | tf_op jit(solution)/shard_map/ppermute | solution.py:636
  7.1 9.9 %collective-permute-start.7 = (bf16[304,128]{1,0:T(8,128)(2,1)S(1)}, bf16[304,128]{1,0:T(8,128)(2,1)S(1)}, u32[]{:S(2)}, u32[]{:S(2)}) collective-permute-start(bf16[304,128]{1,0:T(8,128)(2,1)S(1)} %shard_map.70.refs_5_.refs_0_.msg_own_ref), channel_id=1, source_target_pairs={{0,16},{8,24},{16,0},{24,8},{1,17},{9,25},{17,1},{25,9},{2,18},{10... | collective-permute-start | bytes 233480 | tf_op jit(solution)/shard_map/ppermute | solution.py:669
  10.3 6.8 %collective-permute-start.6 = (bf16[304,128]{1,0:T(8,128)(2,1)S(1)}, bf16[304,128]{1,0:T(8,128)(2,1)S(1)}, u32[]{:S(2)}, u32[]{:S(2)}) collective-permute-start(bf16[304,128]{1,0:T(8,128)(2,1)S(1)} %shard_map.70.refs_5_.refs_0_.msg_own_ref), channel_id=1, source_target_pairs={{0,8},{8,0},{16,24},{24,16},{1,9},{9,1},{17,25},{25,17},{2,10},{10... | collective-permute-start | bytes 233480 | tf_op jit(solution)/shard_map/ppermute | solution.py:669
  12.1 6.6 %collective-permute-start.5 = (bf16[304,128]{1,0:T(8,128)(2,1)S(1)}, bf16[304,128]{1,0:T(8,128)(2,1)S(1)}, u32[]{:S(2)}, u32[]{:S(2)}) collective-permute-start(bf16[304,128]{1,0:T(8,128)(2,1)S(1)} %get-tuple-element.10), channel_id=1, source_target_pairs={{0,24},{8,16},{16,8},{24,0},{1,25},{9,17},{17,9},{25,1},{2,26},{10... | collective-permute-start | bytes 233480 | tf_op jit(solution)/shard_map/ppermute | solution.py:669
  14.7 4.0 %collective-permute-start.8 = (bf16[48,128]{1,0:T(8,128)(2,1)S(1)}, bf16[48,128]{1,0:T(8,128)(2,1)S(1)}, u32[]{:S(2)}, u32[]{:S(2)}) collective-permute-start(bf16[48,128]{1,0:T(8,128)(2,1)S(1)} %get-tuple-element.11), channel_id=1, source_target_pairs={{0,8},{8,0},{16,24},{24,16},{1,9},{9,1},{17,25},{25,17},{2,10},{10... | collective-permute-start | bytes 36872 | tf_op jit(solution)/shard_map/ppermute | solution.py:672
  15.3 3.3 %copy-start.1 = (f32[368,384]{1,0:T(8,128)S(1)}, f32[368,384]{1,0:T(8,128)}, u32[]{:S(2)}) copy-start(f32[368,384]{1,0:T(8,128)} %constant.15.clone.refs_8_) | copy-start | bytes 1695748

commit v8 on v7

--- a/solution.py
+++ b/solution.py
@@ -253,10 +253,17 @@
 def half_kernel(depth, wx, n_row, *refs):
     row_refs, table_ref, bulk_ref = refs[:n_row], refs[n_row], refs[n_row + 1]
     full_x = table_ref.shape[0]
+    lines = jnp.concatenate(
+        [
+            jnp.concatenate([r[z * wx : (z + 1) * wx] for r in row_refs], axis=0)
+            for z in range(depth)
+        ],
+        axis=1,
+    )
+    half = jnp.dot(table_ref[...], lines, preferred_element_type=F32).astype(BF16)
+    wy = bulk_ref.shape[1]
     for z in range(depth):
-        lines = jnp.concatenate([r[z * wx : (z + 1) * wx] for r in row_refs], axis=0)
-        half = jnp.dot(table_ref[...], lines, preferred_element_type=F32)
-        bulk_ref[z * full_x : (z + 1) * full_x] = half.astype(BF16)
+        bulk_ref[z * full_x : (z + 1) * full_x] = half[:, z * wy : (z + 1) * wy]
     at = depth * wx + 8 * depth
     marks = sum(ref[at:].astype(F32) for ref in row_refs)
     bulk_ref[depth * full_x : depth * full_x + marks.shape[0]] = marks.astype(BF16)

time: 21.2 us -> 21.2 us (level)
  no operation moved by 1% of the time
where the time goes in v8:
time: 21.2 us; the launch traced here: 21.1 us
  starting transfers between devices  12.7 us (60%)
  Pallas kernels  5.33 us (25%)
  waiting for transfers between devices  1.19 us (6%)
  other arithmetic  1.14 us (5%)
  between operations  0.7 us (3%)
    ppermute x3, starting transfers between devices, on_device(): sec_got.append(lax.ppermute(msg if with_columns else bulk, 'sec', move))  7.26 us
    ppermute x1, starting transfers between devices, on_device(): lax.ppermute(row_msg, 'row', xor_pairs(n_row, k))  3.03 us
    pallas_call x1, Pallas kernels, on_device(): call(functools.partial(final_kernel, n_sec, section, tables['places'], ta...  2.41 us
    pallas_call x1, Pallas kernels, on_device(): call(cells_kernel, shape((38, depth, wx, wy), F32), flops=LBM, moved=LBM)  1.7 us
    ppermute x1, waiting for transfers between devices, on_device(): strip_got.append(lax.ppermute(strip, 'sec', move))  1.14 us
    select_n x1, other arithmetic, on_device(): own = jnp.where(part == 2, whole_numbers.astype(F32), density)  1.13 us
    ppermute x2, starting transfers between devices, on_device(): col_got = [lax.ppermute(col_msg, 'col', m) for m in ring_moves(n_col)]  1.09 us
    ppermute x1, starting transfers between devices, on_device(): strip_got.append(lax.ppermute(strip, 'sec', move))  0.68 us
  transfers between devices with their start and end apart: 9, of which 1 were waited for; matrix products, arithmetic and copies ran while one was open for 0% of the time, Pallas kernels for 13%

profile of v8, /device:TPU:0, one launch (start us, length us, event | category | flops | bytes accessed | tf_op | source)
XLA Modules:
  0.0 21.1 jit_solution(13951848109432976117)
XLA Ops:
  0.6 0.0 copy-start
  0.7 1.1 %multiply_select_fusion.own_ref = f32[3,2,64,128]{3,2,1,0:T(8,128)S(1)} fusion(f32[2,2,64,128]{3,2,1,0:T(8,128)} %param.6, s32[2,64,128]{2,1,0:T(8,128)} %param.5, s32[64,128]{1,0:T(8,128)} %param.7, pred[3]{0:T(512)(128)(4,1)S(1)} %iota_compare_fusion), kind=kLoop, calls=%fused_computation | loop fusion | flops 344064 | bytes 425987 | tf_op jit(solution)/shard_map/jit(_where)/select_n | solution.py:626
  1.8 0.2 shard_map.68.refs_0_.row_ref
  2.0 3.0 %collective-permute-start = (bf16[160,128]{1,0:T(8,128)(2,1)S(1)}, bf16[160,128]{1,0:T(8,128)(2,1)S(1)}, u32[]{:S(2)}, u32[]{:S(2)}) collective-permute-start(bf16[160,128]{1,0:T(8,128)(2,1)S(1)} %shard_map.68.refs_0_.row_ref), channel_id=1, source_target_pairs={{0,4},{4,0},{1,5},{5,1},{2,6},{6,2},{3,7},{7,3},{8,12},{12,8},{9,1... | collective-permute-start | bytes 122888 | tf_op jit(solution)/shard_map/ppermute | solution.py:637
  5.0 0.2 shard_map.69
  5.2 0.7 %collective-permute-start.4 = (bf16[256,128]{1,0:T(8,128)(2,1)S(1)}, bf16[256,128]{1,0:T(8,128)(2,1)S(1)}, u32[]{:S(2)}, u32[]{:S(2)}) collective-permute-start(bf16[256,128]{1,0:T(8,128)(2,1)S(1)} %get-tuple-element.9), channel_id=1, source_target_pairs={{0,7},{1,6},{2,5},{3,4},{4,3},{5,2},{6,1},{7,0},{8,15},{9,14},{10,... | collective-permute-start | bytes 196616 | tf_op jit(solution)/shard_map/ppermute | solution.py:646
  5.9 0.6 %collective-permute-start.3 = (bf16[256,128]{1,0:T(8,128)(2,1)S(1)}, bf16[256,128]{1,0:T(8,128)(2,1)S(1)}, u32[]{:S(2)}, u32[]{:S(2)}) collective-permute-start(bf16[256,128]{1,0:T(8,128)(2,1)S(1)} %get-tuple-element.9), channel_id=1, source_target_pairs={{0,3},{1,2},{2,1},{3,0},{4,7},{5,6},{6,5},{7,4},{8,11},{9,10},{10,... | collective-permute-start | bytes 196616 | tf_op jit(solution)/shard_map/ppermute | solution.py:636
  6.5 0.5 %collective-permute-start.1 = (bf16[256,128]{1,0:T(8,128)(2,1)S(1)}, bf16[256,128]{1,0:T(8,128)(2,1)S(1)}, u32[]{:S(2)}, u32[]{:S(2)}) collective-permute-start(bf16[256,128]{1,0:T(8,128)(2,1)S(1)} %get-tuple-element.9), channel_id=1, source_target_pairs={{0,1},{1,0},{2,3},{3,2},{4,5},{5,4},{6,7},{7,6},{8,9},{9,8},{10,11... | collective-permute-start | bytes 196616 | tf_op jit(solution)/shard_map/ppermute | solution.py:636
  6.9 0.0 collective-permute-done.refs_1_.refs_2_
  7.0 0.0 collective-permute-start.2
  7.0 0.1 shard_map.70.refs_5_.refs_0_.msg_own_ref
  7.1 3.2 %collective-permute-start.7 = (bf16[304,128]{1,0:T(8,128)(2,1)S(1)}, bf16[304,128]{1,0:T(8,128)(2,1)S(1)}, u32[]{:S(2)}, u32[]{:S(2)}) collective-permute-start(bf16[304,128]{1,0:T(8,128)(2,1)S(1)} %shard_map.70.refs_5_.refs_0_.msg_own_ref), channel_id=1, source_target_pairs={{0,16},{8,24},{16,0},{24,8},{1,17},{9,25},{17,1},{25,9},{2,18},{10... | collective-permute-start | bytes 233480 | tf_op jit(solution)/shard_map/ppermute | solution.py:676
  10.3 0.0 collective-permute-done.4.refs_4_
  10.3 1.6 %collective-permute-start.6 = (bf16[304,128]{1,0:T(8,128)(2,1)S(1)}, bf16[304,128]{1,0:T(8,128)(2,1)S(1)}, u32[]{:S(2)}, u32[]{:S(2)}) collective-permute-start(bf16[304,128]{1,0:T(8,128)(2,1)S(1)} %shard_map.70.refs_5_.refs_0_.msg_own_ref), channel_id=1, source_target_pairs={{0,8},{8,0},{16,24},{24,16},{1,9},{9,1},{17,25},{25,17},{2,10},{10... | collective-permute-start | bytes 233480 | tf_op jit(solution)/shard_map/ppermute | solution.py:676
  11.9 0.0 collective-permute-done.3.refs_3_
  11.9 0.0 collective-permute-done.1.refs_0_
  11.9 0.0 collective-permute-done.2.refs_1_
  11.9 0.2 %shard_map.71 = (bf16[304,128]{1,0:T(8,128)(2,1)S(1)}, bf16[48,128]{1,0:T(8,128)(2,1)S(1)}, f32[12,72,128]{2,1,0:T(8,128)S(1)}, f32[72,128]{1,0:T(8,128)S(1)}) custom-call(f32[3,2,64,128]{3,2,1,0:T(8,128)S(1)} %multiply_select_fusion.own_ref, bf16[160,128]{1,0:T(8,128)(2,1)S(1)} %shard_map.68.refs_0_.row_ref, ...), custom_call_target="tpu_custom_call" | custom-call | flops 16777216 | bytes 16777216 | tf_op jit(solution)/shard_map/pallas_call | solution.py:658
  12.1 2.5 %collective-permute-start.5 = (bf16[304,128]{1,0:T(8,128)(2,1)S(1)}, bf16[304,128]{1,0:T(8,128)(2,1)S(1)}, u32[]{:S(2)}, u32[]{:S(2)}) collective-permute-start(bf16[304,128]{1,0:T(8,128)(2,1)S(1)} %get-tuple-element.10), channel_id=1, source_target_pairs={{0,24},{8,16},{16,8},{24,0},{1,25},{9,17},{17,9},{25,1},{2,26},{10... | collective-permute-start | bytes 233480 | tf_op jit(solution)/shard_map/ppermute | solution.py:676
  14.7 0.7 %collective-permute-start.8 = (bf16[48,128]{1,0:T(8,128)(2,1)S(1)}, bf16[48,128]{1,0:T(8,128)(2,1)S(1)}, u32[]{:S(2)}, u32[]{:S(2)}) collective-permute-start(bf16[48,128]{1,0:T(8,128)(2,1)S(1)} %get-tuple-element.11), channel_id=1, source_target_pairs={{0,8},{8,0},{16,24},{24,16},{1,9},{9,1},{17,25},{25,17},{2,10},{10... | collective-permute-start | bytes 36872 | tf_op jit(solution)/shard_map/ppermute | solution.py:679
  15.3 0.0 copy-start.1
  15.3 1.7 %shard_map.72.refs_5_ = f32[38,2,64,128]{3,2,1,0:T(8,128)S(1)} custom-call(f32[12,72,128]{2,1,0:T(8,128)S(1)} %get-tuple-element.13.dens_ref), custom_call_target="tpu_custom_call" | custom-call | flops 1024 | bytes 1024 | tf_op jit(solution)/shard_map/pallas_call | solution.py:681
  17.0 0.0 collective-permute-done.7.refs_2_
  17.0 0.0 collective-permute-done.6.refs_1_
  17.1 0.0 copy-done
  17.1 0.5 %shard_map.73.refs_6_ = f32[256,768]{1,0:T(8,128)S(1)} custom-call(bf16[304,128]{1,0:T(8,128)(2,1)S(1)} %shard_map.70.refs_5_.refs_0_.msg_own_ref, bf16[304,128]{1,0:T(8,128)(2,1)S(1)} %collective-permute-done.6.refs_1_, bf16[304,128]{1,0:T(8,128)(2,1)S(1)} %collective-permute-done.7.refs_2_, bf16[512,1024]{1,0:T(8,128)(2,1)S(1)} %copy-done), custom_call_target="tpu_custom_call" | custom-call | tf_op jit(solution)/shard_map/pallas_call | solution.py:691
  17.5 1.1 %collective-permute-done.8.refs_3_ = bf16[48,128]{1,0:T(8,128)(2,1)S(1)} collective-permute-done((bf16[48,128]{1,0:T(8,128)(2,1)S(1)}, bf16[48,128]{1,0:T(8,128)(2,1)S(1)}, u32[]{:S(2)}, u32[]{:S(2)}) %collective-permute-start.8) | collective-permute-done | bytes 12320 | tf_op jit(solution)/shard_map/ppermute | solution.py:679
  18.7 0.0 collective-permute-done.5.refs_0_
  18.7 0.0 copy-done.1
  18.7 2.4 %shard_map.74 = (f32[38,2,64,128]{3,2,1,0:T(8,128)}, f32[2,256]{1,0:T(2,128)}) custom-call(bf16[304,128]{1,0:T(8,128)(2,1)S(1)} %shard_map.70.refs_5_.refs_0_.msg_own_ref, bf16[304,128]{1,0:T(8,128)(2,1)S(1)} %collective-permute-done.5.refs_0_, bf16[304,128]{1,0:T(8,128)(2,1)S(1)} %collective-permute-done.6.refs_1_, ...), custom_call_target="tpu_custom_call" | custom-call | tf_op jit(solution)/shard_map/pallas_call | solution.py:695
  (1 shorter events, 0.0 us)
Async XLA Ops:
  0.6 16.4 %copy-start = (bf16[512,1024]{1,0:T(8,128)(2,1)S(1)}, bf16[512,1024]{1,0:T(8,128)(2,1)}, u32[]{:S(2)}) copy-start(bf16[512,1024]{1,0:T(8,128)(2,1)} %constant.14.clone.refs_3_.refs_7_) | copy-start | bytes 3145732
  2.0 5.0 %collective-permute-start = (bf16[160,128]{1,0:T(8,128)(2,1)S(1)}, bf16[160,128]{1,0:T(8,128)(2,1)S(1)}, u32[]{:S(2)}, u32[]{:S(2)}) collective-permute-start(bf16[160,128]{1,0:T(8,128)(2,1)S(1)} %shard_map.68.refs_0_.row_ref), channel_id=1, source_target_pairs={{0,4},{4,0},{1,5},{5,1},{2,6},{6,2},{3,7},{7,3},{8,12},{12,8},{9,1... | collective-permute-start | bytes 122888 | tf_op jit(solution)/shard_map/ppermute | solution.py:637
  5.2 5.1 %collective-permute-start.4 = (bf16[256,128]{1,0:T(8,128)(2,1)S(1)}, bf16[256,128]{1,0:T(8,128)(2,1)S(1)}, u32[]{:S(2)}, u32[]{:S(2)}) collective-permute-start(bf16[256,128]{1,0:T(8,128)(2,1)S(1)} %get-tuple-element.9), channel_id=1, source_target_pairs={{0,7},{1,6},{2,5},{3,4},{4,3},{5,2},{6,1},{7,0},{8,15},{9,14},{10,... | collective-permute-start | bytes 196616 | tf_op jit(solution)/shard_map/ppermute | solution.py:646
  5.9 6.0 %collective-permute-start.3 = (bf16[256,128]{1,0:T(8,128)(2,1)S(1)}, bf16[256,128]{1,0:T(8,128)(2,1)S(1)}, u32[]{:S(2)}, u32[]{:S(2)}) collective-permute-start(bf16[256,128]{1,0:T(8,128)(2,1)S(1)} %get-tuple-element.9), channel_id=1, source_target_pairs={{0,3},{1,2},{2,1},{3,0},{4,7},{5,6},{6,5},{7,4},{8,11},{9,10},{10,... | collective-permute-start | bytes 196616 | tf_op jit(solution)/shard_map/ppermute | solution.py:636
  6.5 5.4 %collective-permute-start.1 = (bf16[256,128]{1,0:T(8,128)(2,1)S(1)}, bf16[256,128]{1,0:T(8,128)(2,1)S(1)}, u32[]{:S(2)}, u32[]{:S(2)}) collective-permute-start(bf16[256,128]{1,0:T(8,128)(2,1)S(1)} %get-tuple-element.9), channel_id=1, source_target_pairs={{0,1},{1,0},{2,3},{3,2},{4,5},{5,4},{6,7},{7,6},{8,9},{9,8},{10,11... | collective-permute-start | bytes 196616 | tf_op jit(solution)/shard_map/ppermute | solution.py:636
  7.0 4.9 %collective-permute-start.2 = (bf16[160,128]{1,0:T(8,128)(2,1)S(1)}, bf16[160,128]{1,0:T(8,128)(2,1)S(1)}, u32[]{:S(2)}, u32[]{:S(2)}) collective-permute-start(bf16[160,128]{1,0:T(8,128)(2,1)S(1)} %collective-permute-done.refs_1_.refs_2_), channel_id=1, source_target_pairs={{0,1},{1,0},{2,3},{3,2},{4,5},{5,4},{6,7},{7,6},{8,9},{9,8},{10,11... | collective-permute-start | bytes 122888 | tf_op jit(solution)/shard_map/ppermute | solution.py:643
  7.1 9.9 %collective-permute-start.7 = (bf16[304,128]{1,0:T(8,128)(2,1)S(1)}, bf16[304,128]{1,0:T(8,128)(2,1)S(1)}, u32[]{:S(2)}, u32[]{:S(2)}) collective-permute-start(bf16[304,128]{1,0:T(8,128)(2,1)S(1)} %shard_map.70.refs_5_.refs_0_.msg_own_ref), channel_id=1, source_target_pairs={{0,16},{8,24},{16,0},{24,8},{1,17},{9,25},{17,1},{25,9},{2,18},{10... | collective-permute-start | bytes 233480 | tf_op jit(solution)/shard_map/ppermute | solution.py:676
  10.3 6.8 %collective-permute-start.6 = (bf16[304,128]{1,0:T(8,128)(2,1)S(1)}, bf16[304,128]{1,0:T(8,128)(2,1)S(1)}, u32[]{:S(2)}, u32[]{:S(2)}) collective-permute-start(bf16[304,128]{1,0:T(8,128)(2,1)S(1)} %shard_map.70.refs_5_.refs_0_.msg_own_ref), channel_id=1, source_target_pairs={{0,8},{8,0},{16,24},{24,16},{1,9},{9,1},{17,25},{25,17},{2,10},{10... | collective-permute-start | bytes 233480 | tf_op jit(solution)/shard_map/ppermute | solution.py:676
  12.1 6.6 %collective-permute-start.5 = (bf16[304,128]{1,0:T(8,128)(2,1)S(1)}, bf16[304,128]{1,0:T(8,128)(2,1)S(1)}, u32[]{:S(2)}, u32[]{:S(2)}) collective-permute-start(bf16[304,128]{1,0:T(8,128)(2,1)S(1)} %get-tuple-element.10), channel_id=1, source_target_pairs={{0,24},{8,16},{16,8},{24,0},{1,25},{9,17},{17,9},{25,1},{2,26},{10... | collective-permute-start | bytes 233480 | tf_op jit(solution)/shard_map/ppermute | solution.py:676
  14.7 4.0 %collective-permute-start.8 = (bf16[48,128]{1,0:T(8,128)(2,1)S(1)}, bf16[48,128]{1,0:T(8,128)(2,1)S(1)}, u32[]{:S(2)}, u32[]{:S(2)}) collective-permute-start(bf16[48,128]{1,0:T(8,128)(2,1)S(1)} %get-tuple-element.11), channel_id=1, source_target_pairs={{0,8},{8,0},{16,24},{24,16},{1,9},{9,1},{17,25},{25,17},{2,10},{10... | collective-permute-start | bytes 36872 | tf_op jit(solution)/shard_map/ppermute | solution.py:679
  15.3 3.3 %copy-start.1 = (f32[368,384]{1,0:T(8,128)S(1)}, f32[368,384]{1,0:T(8,128)}, u32[]{:S(2)}) copy-start(f32[368,384]{1,0:T(8,128)} %constant.15.clone.refs_8_) | copy-start | bytes 1695748
